TPU v7x, 128 devices: a whole 4x4x4 slice. The times are simulated.
128 devices in a mesh: seq: 4 (over x_lo, core), blk: 32 (over y, z, x_hi).
Axes of the slice: x: 4 (x_hi: 2, x_lo: 2; x = x_hi * 2 + x_lo), y: 4, z: 4, core: 2. Of those that a mesh axis runs over, the one named last changes fastest.
Arguments:
- tokens: bfloat16 [8, 2048, 768], P('seq', 'blk'), may hold values from -6 to 6
- cotangent: bfloat16 [8, 2048, 768], P('seq', 'blk'), may hold values from -6 to 6
- group_of_seq: int32 [8], P('seq'), may hold values from 0 to 3
- group_weight: float32 [4], replicated, may hold values from 0.25 to 4
- norm_attn: float32 [768], replicated, may hold values from 0.5 to 1.5
- w_query: bfloat16 [768, 768], replicated, may hold values from -0.21875 to 0.21875
- w_qrope: bfloat16 [768, 768], replicated, may hold values from -0.21875 to 0.21875
- w_latent: bfloat16 [768, 512], replicated, may hold values from -0.21875 to 0.21875
- w_krope: bfloat16 [768, 64], replicated, may hold values from -0.21875 to 0.21875
- w_upkey: bfloat16 [2, 256, 384], replicated, may hold values from -0.375 to 0.375
- w_upval: bfloat16 [2, 256, 384], replicated, may hold values from -0.375 to 0.375
- w_out: bfloat16 [768, 768], replicated, may hold values from -0.875 to 0.875
- norm_mlp: float32 [768], replicated, may hold values from 0.5 to 1.5
- w_gate: bfloat16 [768, 2048], replicated, may hold values from -0.21875 to 0.21875
- w_up: bfloat16 [768, 2048], replicated, may hold values from -0.21875 to 0.21875
- w_down: bfloat16 [2048, 768], replicated, may hold values from -0.125 to 0.125
Outputs:
- layer_out: bfloat16 [8, 2048, 768], P('seq', 'blk')
- grad_tokens: float32 [8, 2048, 768], P('seq', 'blk')
- grad_norm_attn: float32 [768], replicated
- grad_w_query: float32 [768, 768], replicated
- grad_w_qrope: float32 [768, 768], replicated
- grad_w_latent: float32 [768, 512], replicated
- grad_w_krope: float32 [768, 64], replicated
- grad_w_upkey: float32 [2, 256, 384], replicated
- grad_w_upval: float32 [2, 256, 384], replicated
- grad_w_out: float32 [768, 768], replicated
- grad_norm_mlp: float32 [768], replicated
- grad_w_gate: float32 [768, 2048], replicated
- grad_w_up: float32 [768, 2048], replicated
- grad_w_down: float32 [2048, 768], replicated
All inputs are finite; a program needn't handle non-finite values.
Results may differ from a plain program's by a relative error of at most 0.023.
Values may be sent and summed in bfloat16 or wider, within the bound.
A program may use at most 192 MiB of HBM per device.

v0:
```python
import jax
import jax.numpy as jnp
from jax import lax
from jax.sharding import PartitionSpec as P

HEADS = 12
HEAD = 64
LAT_HEADS = 2
LATENT = 256
ROPE = 64
KEY_BLK = 512
GROUPS = 4


epsilon = 1e-06
rope_base = 10000.0
masked_score = -1e30


def angles(positions):
    halves = ROPE // 2
    freq_list = rope_base ** (-(jnp.arange(halves, dtype=jnp.float32) * 2.0 / ROPE))
    phases = positions[:, None] * freq_list[None, :]
    return (jnp.cos(phases), jnp.sin(phases))


def rotate(values, cosine, sine):
    halves = values.shape[-1] // 2
    front = values[..., :halves]
    back_half = values[..., halves:]
    return jnp.concatenate(
        [front * cosine - back_half * sine, front * sine + back_half * cosine], axis=-1
    )


def unrotate(grads, cosine, sine):
    halves = grads.shape[-1] // 2
    front = grads[..., :halves]
    back_half = grads[..., halves:]
    return jnp.concatenate(
        [front * cosine + back_half * sine, back_half * cosine - front * sine], axis=-1
    )


def norm_forward(values, gain):
    inverse = lax.rsqrt(jnp.mean(values * values, axis=-1, keepdims=True) + epsilon)
    unit_rows = values * inverse
    return (unit_rows, inverse, unit_rows * gain)


def norm_backward(grads, unit_rows, inverse, gain):
    scaled = grads * gain
    gain_grad = jnp.sum(grads * unit_rows, axis=0)
    input_grad = inverse * (
        scaled - unit_rows * jnp.mean(scaled * unit_rows, axis=-1, keepdims=True)
    )
    return (input_grad, gain_grad)


def product(left, right):
    return jnp.dot(left, right, preferred_element_type=jnp.float32)


def outer_sum(left, right):
    return lax.dot_general(
        left, right, (((0,), (0,)), ((), ())), preferred_element_type=jnp.float32
    )


def times_transpose(left, right):
    return lax.dot_general(
        left, right, (((1,), (1,)), ((), ())), preferred_element_type=jnp.float32
    )


def up_project(latents, w_upkey, w_upval):
    row_count = latents.shape[0]
    grouped = latents.reshape(row_count, LAT_HEADS, LATENT)
    keys = jnp.einsum("ngc,gcf->ngf", grouped, w_upkey, preferred_element_type=jnp.float32)
    values = jnp.einsum("ngc,gcf->ngf", grouped, w_upval, preferred_element_type=jnp.float32)
    return (
        keys.astype(jnp.bfloat16).reshape(row_count, HEADS * HEAD),
        values.astype(jnp.bfloat16).reshape(row_count, HEADS * HEAD),
    )


def block_scores(queries, query_rot, keys, key_rot, query_first, position):
    query_len = queries.shape[0]
    offset = position * KEY_BLK
    key_blk = lax.dynamic_slice_in_dim(keys, offset, KEY_BLK, 0).reshape(KEY_BLK, HEADS, HEAD)
    rot_blk = lax.dynamic_slice_in_dim(key_rot, offset, KEY_BLK, 0)
    raw = jnp.einsum("qhe,khe->hqk", queries, key_blk, preferred_element_type=jnp.float32)
    raw = raw + jnp.einsum("qhr,kr->hqk", query_rot, rot_blk, preferred_element_type=jnp.float32)
    key_pos = offset + jnp.arange(KEY_BLK, dtype=jnp.int32)
    query_pos = query_first + jnp.arange(query_len, dtype=jnp.int32)
    allowed = key_pos[None, :] <= query_pos[:, None]
    scores = jnp.where(allowed[None, :, :], raw * (HEAD + ROPE) ** (-0.5), masked_score)
    return (scores, key_blk, rot_blk)


def value_block(values, position):
    return lax.dynamic_slice_in_dim(values, position * KEY_BLK, KEY_BLK, 0).reshape(
        KEY_BLK, HEADS, HEAD
    )


def attend_forward(queries, query_rot, keys, values, key_rot, query_first, block_count):
    query_len = queries.shape[0]

    def sweep(position, carried):
        highest, summed = carried
        scores = block_scores(queries, query_rot, keys, key_rot, query_first, position)[0]
        new_high = jnp.maximum(highest, jnp.max(scores, axis=-1))
        summed = summed * jnp.exp(highest - new_high) + jnp.sum(
            jnp.exp(scores - new_high[..., None]), axis=-1
        )
        return (new_high, summed)

    start_state = (
        jnp.full((HEADS, query_len), masked_score, jnp.float32),
        jnp.zeros((HEADS, query_len), jnp.float32),
    )
    highest, summed = lax.fori_loop(0, block_count, sweep, start_state)
    log_total = highest + jnp.log(summed)

    def weigh_values(position, acc):
        scores = block_scores(queries, query_rot, keys, key_rot, query_first, position)[0]
        weights = jnp.exp(scores - log_total[..., None]).astype(jnp.bfloat16)
        return acc + jnp.einsum(
            "hqk,khe->qhe",
            weights,
            value_block(values, position),
            preferred_element_type=jnp.float32,
        )

    mixed = lax.fori_loop(
        0, block_count, weigh_values, jnp.zeros((query_len, HEADS, HEAD), jnp.float32)
    )
    return (mixed, log_total)


def attend_backward(
    queries, query_rot, keys, values, key_rot, log_total, grad_mixed, query_first, block_count
):
    query_len = queries.shape[0]
    length = keys.shape[0]
    factor = (HEAD + ROPE) ** (-0.5)

    def row_terms(position, acc):
        scores = block_scores(queries, query_rot, keys, key_rot, query_first, position)[0]
        weights = jnp.exp(scores - log_total[..., None])
        dprob = jnp.einsum(
            "qhe,khe->hqk",
            grad_mixed,
            value_block(values, position),
            preferred_element_type=jnp.float32,
        )
        return acc + jnp.sum(weights * dprob, axis=-1)

    delta = lax.fori_loop(0, block_count, row_terms, jnp.zeros((HEADS, query_len), jnp.float32))

    def accumulate(position, carried):
        grad_q, grad_qr, grad_keys, grad_values, grad_rot = carried
        scores, key_blk, rot_blk = block_scores(
            queries, query_rot, keys, key_rot, query_first, position
        )
        weights = jnp.exp(scores - log_total[..., None])
        dprob = jnp.einsum(
            "qhe,khe->hqk",
            grad_mixed,
            value_block(values, position),
            preferred_element_type=jnp.float32,
        )
        dscore = (weights * (dprob - delta[..., None])).astype(jnp.bfloat16)
        grad_q = grad_q + jnp.einsum(
            "hqk,khe->qhe", dscore, key_blk, preferred_element_type=jnp.float32
        )
        grad_qr = grad_qr + jnp.einsum(
            "hqk,kr->qhr", dscore, rot_blk, preferred_element_type=jnp.float32
        )
        key_part = factor * jnp.einsum(
            "hqk,qhe->khe", dscore, queries, preferred_element_type=jnp.float32
        )
        rot_part = factor * jnp.einsum(
            "hqk,qhr->kr", dscore, query_rot, preferred_element_type=jnp.float32
        )
        value_part = jnp.einsum(
            "hqk,qhe->khe",
            weights.astype(jnp.bfloat16),
            grad_mixed,
            preferred_element_type=jnp.float32,
        )
        offset = position * KEY_BLK
        grad_keys = lax.dynamic_update_slice_in_dim(
            grad_keys, key_part.astype(jnp.bfloat16).reshape(KEY_BLK, HEADS * HEAD), offset, 0
        )
        grad_values = lax.dynamic_update_slice_in_dim(
            grad_values, value_part.astype(jnp.bfloat16).reshape(KEY_BLK, HEADS * HEAD), offset, 0
        )
        grad_rot = lax.dynamic_update_slice_in_dim(grad_rot, rot_part, offset, 0)
        return (grad_q, grad_qr, grad_keys, grad_values, grad_rot)

    start_state = (
        jnp.zeros((query_len, HEADS, HEAD), jnp.float32),
        jnp.zeros((query_len, HEADS, ROPE), jnp.float32),
        jnp.zeros((length, HEADS * HEAD), jnp.bfloat16),
        jnp.zeros((length, HEADS * HEAD), jnp.bfloat16),
        jnp.zeros((length, ROPE), jnp.float32),
    )
    grad_q, grad_qr, grad_keys, grad_values, grad_rot = lax.fori_loop(
        0, block_count, accumulate, start_state
    )
    return (factor * grad_q, factor * grad_qr, grad_keys, grad_values, grad_rot)


def local(
    tokens,
    cotangent,
    group_of_seq,
    group_weight,
    norm_attn,
    w_query,
    w_qrope,
    w_latent,
    w_krope,
    w_upkey,
    w_upval,
    w_out,
    norm_mlp,
    w_gate,
    w_up,
    w_down,
):
    seq_count, blk_width, model_width = tokens.shape
    row_count = seq_count * blk_width
    group_heads = HEADS // LAT_HEADS
    query_first = lax.axis_index("blk") * blk_width
    block_count = (query_first + blk_width + KEY_BLK - 1) // KEY_BLK
    cosine, sine = angles(
        (query_first + jnp.arange(blk_width, dtype=jnp.int32)).astype(jnp.float32)
    )
    cos_heads = cosine[None, :, None, :]
    sin_heads = sine[None, :, None, :]
    inputs = tokens.astype(jnp.float32).reshape(row_count, model_width)
    unit_attn, inv_attn, pre_attn = norm_forward(inputs, norm_attn)
    normed = pre_attn.astype(jnp.bfloat16)
    queries = product(normed, w_query).astype(jnp.bfloat16)
    query_pre = product(normed, w_qrope).reshape(seq_count, blk_width, HEADS, ROPE)
    query_rot = rotate(query_pre, cos_heads, sin_heads).astype(jnp.bfloat16)
    latents = product(normed, w_latent).astype(jnp.bfloat16)
    key_rot = rotate(
        product(normed, w_krope).reshape(seq_count, blk_width, ROPE), cosine[None], sine[None]
    ).astype(jnp.bfloat16)
    own_keys, own_values = up_project(latents, w_upkey, w_upval)
    keys_all, values_all, rot_all = (
        lax.all_gather(
            own_keys.reshape(seq_count, blk_width, HEADS * HEAD), "blk", axis=1, tiled=True
        ),
        lax.all_gather(
            own_values.reshape(seq_count, blk_width, HEADS * HEAD), "blk", axis=1, tiled=True
        ),
        lax.all_gather(key_rot, "blk", axis=1, tiled=True),
    )
    query_heads = queries.reshape(seq_count, blk_width, HEADS, HEAD)
    mixed, log_total = jax.vmap(attend_forward, in_axes=(0, 0, 0, 0, 0, None, None))(
        query_heads, query_rot, keys_all, values_all, rot_all, query_first, block_count
    )
    attn_out = mixed.reshape(row_count, HEADS * HEAD).astype(jnp.bfloat16)
    middle = inputs + product(attn_out, w_out)
    unit_mlp, inv_mlp, pre_mlp = norm_forward(middle, norm_mlp)
    normed_mlp = pre_mlp.astype(jnp.bfloat16)
    gate_pre = product(normed_mlp, w_gate)
    up_pre = product(normed_mlp, w_up)
    sigmoid_gate = jax.nn.sigmoid(gate_pre)
    silu_gate = gate_pre * sigmoid_gate
    hidden = (silu_gate * up_pre).astype(jnp.bfloat16)
    layer_out = (
        (middle + product(hidden, w_down))
        .astype(jnp.bfloat16)
        .reshape(seq_count, blk_width, model_width)
    )
    matches = group_of_seq[:, None] == jnp.arange(GROUPS, dtype=jnp.int32)[None, :]
    seq_weight = jnp.sum(jnp.where(matches, group_weight[None, :], 0.0), axis=1)
    grad_out = (cotangent.astype(jnp.float32) * seq_weight[:, None, None]).reshape(
        row_count, model_width
    )
    grad_branch = grad_out.astype(jnp.bfloat16)
    grad_w_down = outer_sum(hidden, grad_branch)
    grad_hidden = times_transpose(grad_branch, w_down)
    grad_gate = (
        grad_hidden * up_pre * sigmoid_gate * (1.0 + gate_pre * (1.0 - sigmoid_gate))
    ).astype(jnp.bfloat16)
    grad_upper = (grad_hidden * silu_gate).astype(jnp.bfloat16)
    grad_w_gate = outer_sum(normed_mlp, grad_gate)
    grad_w_up = outer_sum(normed_mlp, grad_upper)
    grad_nm = times_transpose(grad_gate, w_gate) + times_transpose(grad_upper, w_up)
    grad_mid_norm, grad_norm_mlp = norm_backward(grad_nm, unit_mlp, inv_mlp, norm_mlp)
    grad_middle = grad_out + grad_mid_norm
    grad_attn = grad_middle.astype(jnp.bfloat16)
    grad_w_out = outer_sum(attn_out, grad_attn)
    grad_mixed = (
        times_transpose(grad_attn, w_out)
        .astype(jnp.bfloat16)
        .reshape(seq_count, blk_width, HEADS, HEAD)
    )
    grad_q, grad_qr, grad_keys, grad_values, grad_rot = jax.vmap(
        attend_backward, in_axes=(0, 0, 0, 0, 0, 0, 0, None, None)
    )(
        query_heads,
        query_rot,
        keys_all,
        values_all,
        rot_all,
        log_total,
        grad_mixed,
        query_first,
        block_count,
    )
    key_total, value_total, grad_krot = (
        lax.psum_scatter(
            grad_keys.astype(jnp.float32).astype(jnp.bfloat16),
            "blk",
            scatter_dimension=1,
            tiled=True,
        ).astype(jnp.float32),
        lax.psum_scatter(
            grad_values.astype(jnp.float32).astype(jnp.bfloat16),
            "blk",
            scatter_dimension=1,
            tiled=True,
        ).astype(jnp.float32),
        lax.psum_scatter(
            grad_rot.astype(jnp.bfloat16), "blk", scatter_dimension=1, tiled=True
        ).astype(jnp.float32),
    )
    keys_grouped = key_total.reshape(row_count, LAT_HEADS, group_heads * HEAD)
    values_grouped = value_total.reshape(row_count, LAT_HEADS, group_heads * HEAD)
    upkey_wide = w_upkey.astype(jnp.float32)
    upval_wide = w_upval.astype(jnp.float32)
    grad_lat = jnp.einsum(
        "ngf,gcf->ngc",
        keys_grouped,
        upkey_wide,
        precision=lax.Precision.HIGHEST,
        preferred_element_type=jnp.float32,
    )
    grad_lat = grad_lat + jnp.einsum(
        "ngf,gcf->ngc",
        values_grouped,
        upval_wide,
        precision=lax.Precision.HIGHEST,
        preferred_element_type=jnp.float32,
    )
    lat_wide = latents.astype(jnp.float32).reshape(row_count, LAT_HEADS, LATENT)
    grad_w_upkey = jnp.einsum(
        "ngc,ngf->gcf",
        lat_wide,
        keys_grouped,
        precision=lax.Precision.HIGHEST,
        preferred_element_type=jnp.float32,
    )
    grad_w_upval = jnp.einsum(
        "ngc,ngf->gcf",
        lat_wide,
        values_grouped,
        precision=lax.Precision.HIGHEST,
        preferred_element_type=jnp.float32,
    )
    grad_latents = grad_lat.reshape(row_count, LAT_HEADS * LATENT).astype(jnp.bfloat16)
    grad_kpre = (
        unrotate(grad_krot, cosine[None], sine[None]).reshape(row_count, ROPE).astype(jnp.bfloat16)
    )
    grad_queries = grad_q.reshape(row_count, HEADS * HEAD).astype(jnp.bfloat16)
    grad_qpre = (
        unrotate(grad_qr, cos_heads, sin_heads)
        .reshape(row_count, HEADS * ROPE)
        .astype(jnp.bfloat16)
    )
    grad_w_query = outer_sum(normed, grad_queries)
    grad_w_qrope = outer_sum(normed, grad_qpre)
    grad_w_latent = outer_sum(normed, grad_latents)
    grad_w_krope = outer_sum(normed, grad_kpre)
    grad_normed = times_transpose(grad_queries, w_query) + times_transpose(grad_qpre, w_qrope)
    grad_normed = (
        grad_normed + times_transpose(grad_latents, w_latent) + times_transpose(grad_kpre, w_krope)
    )
    grad_in_norm, grad_norm_attn = norm_backward(grad_normed, unit_attn, inv_attn, norm_attn)
    grad_tokens = (grad_middle + grad_in_norm).reshape(seq_count, blk_width, model_width)
    totals = lax.psum(
        (
            grad_norm_attn,
            grad_w_query,
            grad_w_qrope,
            grad_w_latent,
            grad_w_krope,
            grad_w_upkey,
            grad_w_upval,
            grad_w_out,
            grad_norm_mlp,
            grad_w_gate,
            grad_w_up,
            grad_w_down,
        ),
        ("seq", "blk"),
    )
    return (
        layer_out,
        grad_tokens,
        totals[0],
        totals[1],
        totals[2],
        totals[3],
        totals[4],
        totals[5],
        totals[6],
        totals[7],
        totals[8],
        totals[9],
        totals[10],
        totals[11],
    )


def solution(mesh):
    in_specs = (
        P("seq", "blk", None),
        P("seq", "blk", None),
        P("seq"),
        P(),
        P(),
        P(),
        P(),
        P(),
        P(),
        P(),
        P(),
        P(),
        P(),
        P(),
        P(),
        P(),
    )
    out_specs = (
        P("seq", "blk", None),
        P("seq", "blk", None),
        P(),
        P(),
        P(),
        P(),
        P(),
        P(),
        P(),
        P(),
        P(),
        P(),
        P(),
        P(),
    )
    return jax.shard_map(local, mesh=mesh, in_specs=in_specs, out_specs=out_specs, check_vma=False)
```

profile of v0, /device:TPU:1, one launch (start us, length us, event | category | flops | bytes accessed | tf_op | source)
XLA Modules:
  0.0 1635.5 jit_solution(4221910754054912597)
XLA Ops:
  20.7 2.3 convolution_convert_fusion.2
  33.3 103.9 %all_gather.11 = bf16[2,2048,64]{2,0,1:T(2,128)(2,1)} all-gather(bf16[2,64,64]{2,0,1:T(2,128)(2,1)} %copy.142), channel_id=1, replica_groups=mesh['seq'=4,'blk'=32] {'blk'}, dimensions={1}, use_global_device_ids=true | all-gather | bytes 540672 | tf_op jit(solution)/shard_map/all_gather | solution.py:262
  137.3 3.5 copy.151
  140.8 2.4 copy.143
  152.0 8.6 copy.149
  161.2 6.8 while.64
  161.3 2.3 constant_dynamic-slice_fusion.16
  169.3 44.2 %all-gather.3.cloned.1.call-done = bf16[2,2048,768]{2,1,0:T(8,128)(2,1)} async-done(((bf16[2,64,768]{2,1,0:T(8,128)(2,1)}), bf16[2,2048,768]{2,1,0:T(8,128)(2,1)}) %all-gather.3.cloned.1.call-update) | async-done | bytes 6291472 | tf_op jit(solution)/shard_map/all_gather | solution.py:259
  213.5 8.6 copy.148
  223.1 14.0 while.65
  223.2 5.0 constant_dynamic-slice_fusion.17
  231.1 5.7 fusion.216
  244.2 2.5 fusion.74
  262.9 8.6 while.66
  263.0 3.9 constant_dynamic-slice_fusion.18
  268.5 2.4 fusion.225
  273.4 4.2 broadcast.327.clone
  277.6 4.2 broadcast.327.clone2
  282.7 69.0 %while.67 = (s32[]{:T(128)}, f32[2,64,12,64]{1,3,2,0:T(8,128)}, f32[2,64,12,64]{1,3,2,0:T(8,128)}, bf16[2,2048,768]{2,0,1:T(2,128)(2,1)}, bf16[2,2048,768]{2,0,1...) while((s32[]{:T(128)}, f32[2,64,12,64]{1,3,2,0:T(8,128)}, ...), condition=%wide.region_15.16_spmd, body=%wide.region_13.15_spmd.sunk | while | flops 815891008 | bytes 124311056 | solution.py:210
  282.7 3.9 constant_dynamic-slice_fusion.19
  294.2 5.7 constant_dynamic-slice_fusion.20
  299.9 4.9 copy.210
  309.8 4.9 copy.211
  314.7 4.3 constant_dynamic-update-slice_fusion.4
  319.0 4.9 copy.212
  323.9 2.7 convolution_convert_fusion.7
  328.6 4.9 copy.213
  333.5 4.4 constant_dynamic-update-slice_fusion.5
  337.9 2.6 fusion.248
  340.5 2.5 scatter.22
  351.7 3.6 copy.189
  355.2 3.1 reshape.751
  360.3 2.5 multiply_convert_fusion.4
  370.3 2.9 fusion.79
  373.2 2.9 fusion.80
  378.0 3.7 fusion.82
  381.7 3.7 fusion.83
  385.4 3.7 fusion.84
  389.1 373.6 %reduce-scatter.4.cloned.1.call-done = bf16[64,128]{1,0:T(8,128)(2,1)} async-done(((bf16[2048,128]{1,0:T(8,128)(2,1)}), bf16[64,128]{1,0:T(8,128)(2,1)}) %reduce-scatter.4.cloned.1.call-update) | async-done | bytes 16400
  766.0 575.4 %all-reduce.10.cloned.1.call-done = (bf16[2,2048,768]{2,0,1:T(2,128)(2,1)}, bf16[2,2048,768]{2,0,1:T(2,128)(2,1)}) async-done(((bf16[2,2048,768]{2,0,1:T(2,128)(2,1)}, bf16[2,2048,768]{2,0,1:T(2,128)(2,1)}), (bf16[2,2048,768]{2,0,1:T(2,128)(2,1)}, bf16[2,2048,768]{2,0,1:T(2,128)(2,1)})) %all-reduce.10.cloned.1.call-update) | async-done | bytes 12582928
  1359.9 2.7 fusion.77
  1362.6 2.3 fusion.47
  1370.2 63.4 %all-reduce.2 = (f32[768]{0:T(1024)}, f32[768]{0:T(1024)}) all-reduce(f32[768]{0:T(1024)S(1)} %get-tuple-element.613, f32[768]{0:T(1024)S(1)} %copy-done.69), channel_id=1, replica_groups=mesh['seq'=4,'blk'=32] {'seq','blk'}, use_global_device_ids=true, to_apply=%region_21.22 | all-reduce | flops 1536 | bytes 12288 | tf_op jit(solution)/shard_map/psum | solution.py:389
  1435.7 172.0 %all-reduce.8.cloned.1.call-done = (f32[768,768]{1,0:T(8,128)}, f32[768,768]{1,0:T(8,128)}, f32[768,512]{1,0:T(8,128)}, f32[768,64]{0,1:T(8,128)}, f32[2,256,384...) async-done(((f32[768,768]{1,0:T(8,128)}, f32[768,768]{1,0:T(8,128)}, ...) | async-done | bytes 29294608 | tf_op jit(solution)/shard_map/psum | solution.py:389
  1607.7 3.4 copy.268
  1617.6 3.2 copy.275
  1622.2 3.0 copy.276
  1626.0 2.7 copy.277
  (310 shorter events, 133.6 us)
Async XLA Ops:
  7.2 240.2 %copy-start = (bf16[2048,768]{1,0:T(8,128)(2,1)S(1)}, bf16[2048,768]{1,0:T(8,128)(2,1)}, u32[]{:S(2)}) copy-start(bf16[2048,768]{1,0:T(8,128)(2,1)} %param.45) | copy-start | bytes 9437188
  7.2 144.8 %all-gather.5.cloned.1.call-start = ((), (), s32[]{:S(2)}) async-start(), calls=%async_computation.2 | async-start | bytes 6488064 | tf_op jit(solution)/shard_map/all_gather | solution.py:256
  12.7 11.4 copy-start.32
  16.7 196.9 %all-gather.3.cloned.1.call-start = ((), (), s32[]{:S(2)}) async-start(), calls=%async_computation.1 | async-start | bytes 6488064 | tf_op jit(solution)/shard_map/all_gather | solution.py:259
  20.6 742.1 %reduce-scatter.4.cloned.1.call-start = ((), (), s32[]{:S(2)}) async-start(), calls=%async_computation.3 | async-start | bytes 540672
  28.3 116.7 %copy-start.56 = (f32[64,32]{0,1:T(8,128)}, f32[64,32]{0,1:T(8,128)S(1)}, u32[]{:S(2)}) copy-start(f32[64,32]{0,1:T(8,128)S(1)} %get-tuple-element.742) | copy-start | bytes 24580
  169.3 53.8 %copy-start.40 = (f32[2,12,64]{2,1,0:T(8,128)S(1)}, f32[2,12,64]{2,1,0:T(8,128)}, u32[]{:S(2)}) copy-start(f32[2,12,64]{2,1,0:T(8,128)} %log_add_fusion) | copy-start | bytes 18436
  223.2 5.0 copy-start.70
  241.4 5.4 copy-start.18
  243.3 9.5 copy-start.19
  263.0 3.9 copy-start.16
  277.6 5.1 copy-start.6
  282.7 3.9 copy-start.7
  291.2 8.7 copy-start.12
  294.2 5.7 copy-start.53
  333.5 4.4 copy-start.2
  333.5 4.4 copy-start.55
  358.3 983.1 %all-reduce.10.cloned.1.call-start = ((), (), s32[]{:S(2)}) async-start(), calls=%async_computation.5 | async-start | bytes 25165824
  358.9 7.0 copy-start.57
  358.9 7.0 copy-start.59
  358.9 1248.7 %all-reduce.8.cloned.1.call-start = ((), (), s32[]{:S(2)}) async-start(), calls=%async_computation.4 | async-start | bytes 58589184 | tf_op jit(solution)/shard_map/psum | solution.py:389
  360.3 10.1 copy-start.22
  368.4 7.7 copy-start.44
  370.3 5.8 copy-start.27
  373.2 4.8 copy-start.24
  373.2 4.8 copy-start.39
  378.0 3.7 copy-start.37
  381.7 3.7 copy-start.29
  381.7 3.7 copy-start.52
  385.4 379.6 %copy-start.60 = (f32[64,32]{0,1:T(8,128)S(1)}, f32[64,32]{0,1:T(8,128)}, u32[]{:S(2)}) copy-start(f32[64,32]{0,1:T(8,128)} %copy-done.58) | copy-start | bytes 24580
  389.1 958.7 %copy-start.33 = (bf16[128,512]{0,1:T(8,128)(2,1)S(1)}, bf16[128,512]{0,1:T(8,128)(2,1)}, u32[]{:S(2)}) copy-start(bf16[128,512]{0,1:T(8,128)(2,1)} %copy-done.32) | copy-start | bytes 393220
  765.0 592.2 %copy-start.63 = (bf16[2,64,32]{1,2,0:T(8,128)(2,1)}, bf16[2,64,32]{1,2,0:T(8,128)(2,1)S(1)}, u32[]{:S(2)}) copy-start(bf16[2,64,32]{1,2,0:T(8,128)(2,1)S(1)} %get-tuple-element.738) | copy-start | bytes 24580
  765.1 592.2 %copy-start.65 = (bf16[2,64,32]{1,2,0:T(8,128)(2,1)}, bf16[2,64,32]{1,2,0:T(8,128)(2,1)S(1)}, u32[]{:S(2)}) copy-start(bf16[2,64,32]{1,2,0:T(8,128)(2,1)S(1)} %get-tuple-element.739) | copy-start | bytes 24580
  1359.9 5.0 copy-start.64
  1359.9 5.0 copy-start.66
  1362.6 6.5 copy-start.67
  1362.6 6.5 copy-start.74
  1364.9 4.2 copy-start.25
  1364.9 4.2 copy-start.61
  1364.9 5.2 copy-start.69
  1607.7 4.8 copy-start.45
  1611.1 6.4 slice-start.4
  1612.5 3.6 copy-start.34
  1613.6 3.9 slice-start.5
  1616.1 5.2 slice-start.2
  1617.6 4.6 slice-start.3
  1617.6 7.6 slice-start
  1622.2 3.8 slice-start.1
  (40 other events, 73.7 us)
Sparse Core Ops, SparseCore 0:
  16.8 102.9 all-gather.4
  123.4 90.0 all-gather.2
  358.5 404.2 reduce-scatter.3
  765.9 575.4 all-reduce.9
  1360.0 247.6 all-reduce.7
where the time goes:
time: 1650 us; the launch traced here: 1640 us
  waiting for transfers between devices  1170 us (71%)
  local copies, waits for them, and re-layouts  167 us (10%)
  blocking collectives  167 us (10%)
  matrix products  85.9 us (5%)
  other arithmetic  24.9 us (2%)
    unnamed x7, waiting for transfers between devices  950 us
    psum x1, waiting for transfers between devices, local(): lax.psum((grad_norm_attn, grad_w_query, grad_w_qrope, grad_w_latent, grad...  172 us
    all_gather x1, blocking collectives, local(): lax.all_gather(key_rot, 'blk', axis=1, tiled=True)  104 us
    psum x1, blocking collectives, local(): lax.psum((grad_norm_attn, grad_w_query, grad_w_qrope, grad_w_latent, grad...  63.4 us
    all_gather x1, waiting for transfers between devices, local(): lax.all_gather(own_values.reshape(seq_count, blk_width, HEADS * HEAD), 'b...  44.2 us
    unnamed x131, local copies, waits for them, and re-layouts  37.6 us
  transfers between devices with their start and end apart: 5, of which 4 were waited for; matrix products, arithmetic and copies ran while one was open for 6% of the time, Pallas kernels for 0%

commit v1 on v0

--- a/solution.py
+++ b/solution.py
@@ -1,7 +1,182 @@
+import functools
 import jax
 import jax.numpy as jnp
 from jax import lax
 from jax.sharding import PartitionSpec as P
+from jax.experimental import pallas as pl
+from jax.experimental.pallas import tpu as pltpu
+
+MESH = pl.DeviceIdType.MESH
+BF = jnp.bfloat16
+F32 = jnp.float32
+
+
+def coords():
+    s = lax.axis_index("seq")
+    b = lax.axis_index("blk")
+    core = lax.rem(s, 2)
+    x = lax.rem(b, 2) * 2 + lax.div(s, 2)
+    return x, lax.div(b, 8), lax.rem(lax.div(b, 2), 4), core
+
+
+def device(x, y, z, core):
+    return (lax.rem(x, 2) * 2 + core, y * 8 + z * 2 + lax.div(x, 2))
+
+
+def on_ring(place, axis, step):
+    spot = list(place)
+    spot[axis] = lax.rem(place[axis] + step, 4)
+    return device(*spot)
+
+
+def greet(place, peers):
+    barrier = pltpu.get_barrier_semaphore()
+    for peer in peers:
+        pl.semaphore_signal(barrier, inc=1, device_id=peer, device_id_type=MESH)
+    pl.semaphore_wait(barrier, len(peers))
+
+
+ORDERS = ((0, 1, 2), (1, 2, 0), (2, 0, 1))
+
+
+class Reduction:
+    def __init__(self, place, total, done, first, second, third, send, recv):
+        self.place = place
+        self.total, self.done = total, done
+        self.first, self.second, self.third = first, second, third
+        self.send, self.recv = send, recv
+        self.n = total.shape[2]
+
+    def spots(self, o):
+        a, b, c = ORDERS[o]
+        return self.place[a], self.place[b], self.place[c]
+
+    def copies(self, o, stage):
+        i, j, k = self.spots(o)
+        made = []
+        for step in (1, 2, 3):
+            axis = ORDERS[o][(0, 1, 2, 2, 1, 0)[stage]]
+            to = lax.rem(self.place[axis] + step, 4)
+            if stage == 0:
+                src, dst = self.total.at[o, to], self.first.at[o, step - 1]
+            elif stage == 1:
+                src = self.total.at[o, i, :, pl.ds(pl.multiple_of(to * 64, 64), 64)]
+                dst = self.second.at[o, step - 1]
+            elif stage == 2:
+                src = self.total.at[o, i, :, pl.ds(pl.multiple_of(j * 64 + to * 16, 16), 16)]
+                dst = self.third.at[o, step - 1]
+            elif stage == 3:
+                src = dst = self.done.at[o, i, :, pl.ds(pl.multiple_of(j * 64 + k * 16, 16), 16)]
+            elif stage == 4:
+                src = dst = self.done.at[o, i, :, pl.ds(pl.multiple_of(j * 64, 64), 64)]
+            else:
+                src = dst = self.done.at[o, i]
+            made.append(
+                pltpu.make_async_remote_copy(
+                    src_ref=src,
+                    dst_ref=dst,
+                    send_sem=self.send.at[o, stage, step - 1],
+                    recv_sem=self.recv.at[o, stage, step - 1],
+                    device_id=on_ring(self.place, axis, step),
+                    device_id_type=MESH,
+                )
+            )
+        return made
+
+    def start(self, o, stage):
+        for copy in self.copies(o, stage):
+            copy.start()
+
+    def finish(self, o, stage):
+        for copy in self.copies(o, stage):
+            copy.wait()
+        if stage > 2:
+            return
+        i, j, k = self.spots(o)
+        rows = (64, 64, 16)[stage]
+        base = (0, j * 64, j * 64 + k * 16)[stage]
+        arrived = (self.first, self.second, self.third)[stage]
+
+        def add(step, _):
+            m = lax.div(step, 4) if stage == 0 else step
+            r = lax.rem(step, 4) * 64 if stage == 0 else 0
+            here = pl.ds(pl.multiple_of(base + r, 16), rows)
+            there = pl.ds(pl.multiple_of(r, 16) if stage == 0 else 0, rows)
+            acc = self.total[o, i, m, here, :].astype(F32)
+            for slot in range(3):
+                acc = acc + arrived[o, slot, m, there, :].astype(F32)
+            summed = self.done if stage == 2 else self.total
+            summed[o, i, m, here, :] = acc.astype(BF)
+            return _
+
+        lax.fori_loop(0, self.n * (4 if stage == 0 else 1), add, 0)
+
+
+def reduction_scratch(n, width):
+    return [
+        pltpu.VMEM((3, 4, n, 256, width), BF),
+        pltpu.VMEM((3, 4, n, 256, width), BF),
+        pltpu.VMEM((3, 3, n, 256, width), BF),
+        pltpu.VMEM((3, 3, n, 64, width), BF),
+        pltpu.VMEM((3, 3, n, 16, width), BF),
+        pltpu.SemaphoreType.DMA((3, 6, 3)),
+        pltpu.SemaphoreType.DMA((3, 6, 3)),
+    ]
+
+
+def all_peers(place):
+    peers = [on_ring(place, axis, step) for axis in range(3) for step in (1, 2, 3)]
+    x, y, z, core = place
+    return peers + [device(x, y, z, 1 - core)]
+
+
+def ar_kernel(parts_ref, out_ref, total, done, first, second, third, send, recv, local_sem, pair, psem):
+    place = coords()
+    x, y, z, core = place
+    sibling = device(x, y, z, 1 - core)
+    greet(place, all_peers(place))
+    own = pltpu.make_async_copy(parts_ref.at[core], total, local_sem.at[0])
+    own.start()
+    cp = pltpu.make_async_remote_copy(
+        src_ref=parts_ref.at[1 - core], dst_ref=pair, send_sem=psem.at[0], recv_sem=psem.at[1], device_id=sibling, device_id_type=MESH)
+    cp.start()
+    own.wait()
+    cp.wait()
+    n = total.shape[2]
+
+    def add(step, _):
+        o = lax.div(step, 4 * n)
+        i = lax.rem(lax.div(step, n), 4)
+        m = lax.rem(step, n)
+        total[o, i, m] = (total[o, i, m].astype(F32) + pair[o, i, m].astype(F32)).astype(BF)
+        return _
+    lax.fori_loop(0, 12 * n, add, 0)
+    red = Reduction(place, total, done, first, second, third, send, recv)
+    for stage in range(6):
+        for o in range(3):
+            red.start(o, stage)
+        for o in range(3):
+            red.finish(o, stage)
+    mine = pltpu.make_async_copy(done, out_ref.at[core], local_sem.at[0])
+    mine.start()
+    cp = pltpu.make_async_remote_copy(
+        src_ref=done, dst_ref=out_ref.at[core], send_sem=psem.at[2], recv_sem=psem.at[3], device_id=sibling, device_id_type=MESH)
+    cp.start()
+    cp.wait()
+    mine.wait()
+
+
+def all_reduce(parts, cid):
+    _, _, _, n, _, width = parts.shape
+    return pl.pallas_call(
+        ar_kernel,
+        out_shape=jax.ShapeDtypeStruct(parts.shape, BF),
+        in_specs=[pl.BlockSpec(memory_space=pl.ANY)],
+        out_specs=pl.BlockSpec(memory_space=pl.ANY),
+        scratch_shapes=reduction_scratch(n, width) + [pltpu.SemaphoreType.DMA((1,)), pltpu.VMEM((3, 4, n, 256, width), BF), pltpu.SemaphoreType.DMA((4,))],
+        compiler_params=pltpu.CompilerParams(collective_id=cid, has_side_effects=True, vmem_limit_bytes=60 * 2**20),
+    )(parts)
+
 
 HEADS = 12
 HEAD = 64
@@ -211,6 +386,59 @@
         0, block_count, accumulate, start_state
     )
     return (factor * grad_q, factor * grad_qr, grad_keys, grad_values, grad_rot)
+
+
+def halves(grad, blocks, width):
+    grad = grad.reshape(3, 256, 2, blocks, width)
+    return jnp.transpose(grad, (2, 0, 3, 1, 4)).astype(BF)
+
+
+def whole(blocks):
+    _, _, count, _, width = blocks.shape
+    return jnp.transpose(blocks, (1, 3, 0, 2, 4)).reshape(768, 2 * count * width)
+
+
+def up_blocks(grad):
+    return jnp.transpose(grad.reshape(2, 256, 3, 128), (0, 2, 1, 3))[:, :, None].astype(BF)
+
+
+def summed(grads):
+    g_norm, g_query, g_qrope, g_latent, g_krope, g_upkey, g_upval, g_out, g_norm2, g_gate, g_up, g_down = grads
+    down = jnp.transpose(g_down.reshape(2, 4, 256, 3, 256), (0, 3, 1, 2, 4)).astype(BF)
+    wide = jnp.stack([halves(g_gate, 4, 256), halves(g_up, 4, 256), down], axis=3)
+    wide = all_reduce(wide, 1)
+    column = jnp.concatenate([g_krope, g_norm[:, None], g_norm2[:, None], jnp.zeros((768, 62), jnp.float32)], axis=1)
+    column = jnp.broadcast_to(column.reshape(1, 3, 1, 256, 128), (2, 3, 1, 256, 128)).astype(BF)
+    column = column * (lax.broadcasted_iota(jnp.int32, (2, 1, 1, 1, 1), 0) == 0)
+    column = column.astype(BF)
+    narrow = jnp.stack(
+        [
+            jnp.concatenate([halves(g_query, 3, 128), up_blocks(g_upkey)], axis=2),
+            jnp.concatenate([halves(g_qrope, 3, 128), up_blocks(g_upval)], axis=2),
+            jnp.concatenate([halves(g_out, 3, 128), column], axis=2),
+            jnp.concatenate([halves(g_latent, 2, 128)] * 2, axis=2),
+        ],
+        axis=3,
+    )
+    narrow = all_reduce(narrow, 2)
+    wide = wide.astype(jnp.float32)
+    narrow = narrow.astype(jnp.float32)
+    column = narrow[0, :, 3, 2].reshape(768, 128)
+    ups = lambda m: jnp.transpose(narrow[:, :, 3, m], (0, 2, 1, 3)).reshape(2, 256, 384)
+    return (
+        column[:, 64],
+        whole(narrow[:, :, :3, 0]),
+        whole(narrow[:, :, :3, 1]),
+        whole(narrow[:, :, :2, 3]),
+        column[:, :64],
+        ups(0),
+        ups(1),
+        whole(narrow[:, :, :3, 2]),
+        column[:, 65],
+        whole(wide[:, :, :, 0]),
+        whole(wide[:, :, :, 1]),
+        jnp.transpose(wide[:, :, :, 2], (0, 2, 3, 1, 4)).reshape(2048, 768),
+    )
 
 
 def local(
@@ -386,7 +614,7 @@
     )
     grad_in_norm, grad_norm_attn = norm_backward(grad_normed, unit_attn, inv_attn, norm_attn)
     grad_tokens = (grad_middle + grad_in_norm).reshape(seq_count, blk_width, model_width)
-    totals = lax.psum(
+    totals = summed(
         (
             grad_norm_attn,
             grad_w_query,
@@ -401,7 +629,6 @@
             grad_w_up,
             grad_w_down,
         ),
-        ("seq", "blk"),
     )
     return (
         layer_out,

time: 1650 us -> 1460 us (0.88)
  waiting for transfers between devices: 1170 us -> 575 us
  Pallas kernels: 0 us -> 371 us
  local copies, waits for them, and re-layouts: 167 us -> 242 us
  blocking collectives: 167 us -> 104 us
  other arithmetic: 24.9 us -> 54.1 us
    unnamed x7 -> x6, waiting for transfers between devices: 950 us -> 530 us
    pallas_call x0 -> x2, Pallas kernels: none -> 371 us  [all_reduce(): pl.pallas_call(ar_kernel, out_shape=jax.ShapeDtypeStruct(parts.shape, BF)...]
    psum x1 -> x0, waiting for transfers between devices: 172 us -> none  [local(): lax.psum((grad_norm_attn, grad_w_query, grad_w_qrope, grad_w_latent, grad...]
    psum x1 -> x0, blocking collectives: 63.4 us -> none  [local(): lax.psum((grad_norm_attn, grad_w_query, grad_w_qrope, grad_w_latent, grad...]
    transpose x0 -> x12, local copies, waits for them, and re-layouts: none -> 47.4 us  [the longest x8 32.7 us: whole(): jnp.transpose(blocks, (1, 3, 0, 2, 4)).reshape(768, 2 * count * width)]
    reshape x0 -> x6, local copies, waits for them, and re-layouts: none -> 29.3 us  [whole(): jnp.transpose(blocks, (1, 3, 0, 2, 4)).reshape(768, 2 * count * width)]
    convert_element_type x1 -> x4, other arithmetic: 0.1 us -> 18.3 us  [the longest x1 12.8 us: summed(): wide = wide.astype(jnp.float32)]
    unnamed x131 -> x148, local copies, waits for them, and re-layouts: 37.6 us -> 33.2 us
  transfers between devices with their start and end apart: 5 -> 4, of which waited for: 4 -> 2; matrix products, arithmetic and copies ran while one was open for 6% -> 12% of each run, Pallas kernels for 0% -> 22%
where the time goes in v1:
time: 1460 us; the launch traced here: 1450 us
  waiting for transfers between devices  575 us (39%)
  Pallas kernels  371 us (25%)
  local copies, waits for them, and re-layouts  242 us (17%)
  blocking collectives  104 us (7%)
  matrix products  69.5 us (5%)
  other arithmetic  54.1 us (4%)
  loops' own time  16.2 us (1%)
  between operations  15.8 us (1%)
    unnamed x6, waiting for transfers between devices  530 us
    pallas_call x2, Pallas kernels, all_reduce(): pl.pallas_call(ar_kernel, out_shape=jax.ShapeDtypeStruct(parts.shape, BF)...  371 us
    all_gather x1, blocking collectives, local(): lax.all_gather(key_rot, 'blk', axis=1, tiled=True)  104 us
    all_gather x1, waiting for transfers between devices, local(): lax.all_gather(own_values.reshape(seq_count, blk_width, HEADS * HEAD), 'b...  44.1 us
    unnamed x148, local copies, waits for them, and re-layouts  33.2 us
    transpose x8, local copies, waits for them, and re-layouts, whole(): jnp.transpose(blocks, (1, 3, 0, 2, 4)).reshape(768, 2 * count * width)  32.7 us
    reshape x6, local copies, waits for them, and re-layouts, whole(): jnp.transpose(blocks, (1, 3, 0, 2, 4)).reshape(768, 2 * count * width)  29.3 us
  transfers between devices with their start and end apart: 4, of which 2 were waited for; matrix products, arithmetic and copies ran while one was open for 12% of the time, Pallas kernels for 22%

profile of v1, /device:TPU:1, one launch (start us, length us, event | category | flops | bytes accessed | tf_op | source)
XLA Modules:
  0.0 1447.6 jit_solution(8701325309483133209)
XLA Ops:
  33.4 103.9 %all_gather.11 = bf16[2,2048,64]{2,0,1:T(2,128)(2,1)} all-gather(bf16[2,64,64]{2,0,1:T(2,128)(2,1)} %copy.217), channel_id=1, replica_groups=mesh['seq'=4,'blk'=32] {'blk'}, dimensions={1}, use_global_device_ids=true | all-gather | bytes 540672 | tf_op jit(solution)/shard_map/all_gather | solution.py:490
  137.3 3.5 copy.226
  152.2 8.6 copy.224
  161.4 6.8 while.64
  169.5 44.1 %all-gather.3.cloned.1.call-done = bf16[2,2048,768]{2,1,0:T(8,128)(2,1)} async-done(((bf16[2,64,768]{2,1,0:T(8,128)(2,1)}), bf16[2,2048,768]{2,1,0:T(8,128)(2,1)}) %all-gather.3.cloned.1.call-update) | async-done | bytes 6291472 | tf_op jit(solution)/shard_map/all_gather | solution.py:487
  213.6 8.6 copy.223
  223.2 29.2 %while.65 = (s32[]{:T(128)}, f32[2,64,12,64]{1,3,2,0:T(8,128)}, s32[]{:T(128)}, bf16[2,2048,768]{1,2,0:T(8,128)(2,1)}, s32[]{:T(128)}, /*index=5*/bf16[2,2048,76...) while((s32[]{:T(128)}, f32[2,64,12,64]{1,3,2,0:T(8,128)}, ...), condition=%wide.region_6.7_spmd, body=%wide.region_5.6_spmd.sunk | while | flops 306053696 | bytes 17706268 | solution.py:311
  223.3 5.0 constant_dynamic-slice_fusion.17
  231.2 5.7 fusion.214
  273.7 8.5 while.66
  273.8 3.9 constant_dynamic-slice_fusion.18
  284.1 4.3 broadcast.338.clone
  288.4 4.2 broadcast.338.clone2
  293.5 54.7 %while.67 = (s32[]{:T(128)}, f32[2,64,12,64]{1,3,2,0:T(8,128)}, f32[2,64,12,64]{1,3,2,0:T(8,128)}, bf16[2,2048,768]{2,0,1:T(2,128)(2,1)}, bf16[2,2048,768]{2,0,1...) while((s32[]{:T(128)}, f32[2,64,12,64]{1,3,2,0:T(8,128)}, ...), condition=%wide.region_15.16_spmd, body=%wide.region_13.15_spmd.sunk | while | flops 815891008 | bytes 92907824 | solution.py:385
  293.5 3.9 constant_dynamic-slice_fusion.19
  304.5 3.1 fusion.245
  307.6 5.7 constant_dynamic-slice_fusion.20
  313.4 3.6 copy.340
  321.4 3.9 copy.341
  325.3 2.9 constant_dynamic-update-slice_fusion.4
  328.2 3.6 copy.342
  331.8 2.6 convolution_convert_fusion.15
  336.5 3.9 copy.343
  340.4 3.0 constant_dynamic-update-slice_fusion.5
  364.9 4.1 convert_element_type.284
  371.1 3.9 convert_element_type.281
  377.2 6.2 copy_bitcast_fusion
  383.4 7.0 pad_maximum_fusion.parts_ref
  390.4 311.6 %shard_map.264 = bf16[2,3,4,3,256,256]{5,4,3,2,1,0:T(8,128)(2,1)} custom-call(bf16[2,3,4,3,256,256]{5,4,3,2,1,0:T(8,128)(2,1)} %pad_maximum_fusion.parts_ref), custom_call_target="tpu_custom_call" | custom-call | tf_op jit(solution)/shard_map/pallas_call | solution.py:171
  702.0 12.8 convert_element_type.289
  714.8 11.8 slice_bitcast_fusion
  726.6 6.7 copy.280
  733.3 8.6 reshape.519
  741.9 9.5 copy.281
  751.4 8.2 reshape.520
  759.6 10.4 copy.309
  770.1 7.9 copy.325
  788.1 530.0 %all-reduce.5.cloned.1.call-done = (bf16[2,2048,768]{2,0,1:T(2,128)(2,1)}, bf16[2,2048,768]{2,0,1:T(2,128)(2,1)}) async-done(((bf16[2,2048,768]{2,0,1:T(2,128)(2,1)}, bf16[2,2048,768]{2,0,1:T(2,128)(2,1)}), (bf16[2,2048,768]{2,0,1:T(2,128)(2,1)}, bf16[2,2048,768]{2,0,1:T(2,128)(2,1)})) %all-reduce.5.cloned.1.call-update) | async-done | bytes 12582928
  1333.9 3.2 pad_maximum_fusion.1.parts_ref
  1337.2 59.8 %shard_map.263 = bf16[2,3,4,4,256,128]{5,4,3,2,1,0:T(8,128)(2,1)} custom-call(bf16[2,3,4,4,256,128]{5,4,3,2,1,0:T(8,128)(2,1)} %pad_maximum_fusion.1.parts_ref), custom_call_target="tpu_custom_call" | custom-call | tf_op jit(solution)/shard_map/pallas_call | solution.py:171
  1398.0 4.7 convert_element_type.279
  1402.6 2.6 slice_bitcast_fusion.3
  1410.5 2.6 reshape.513
  1413.1 3.3 copy.268
  1416.4 2.8 reshape.514
  1419.2 2.7 copy.269
  1429.1 5.1 copy.273
  1434.2 4.6 reshape.518
  (353 shorter events, 157.4 us)
Async XLA Ops:
  7.2 254.7 %copy-start = (bf16[768,2048]{1,0:T(8,128)(2,1)S(1)}, bf16[768,2048]{1,0:T(8,128)(2,1)}, u32[]{:S(2)}) copy-start(bf16[768,2048]{1,0:T(8,128)(2,1)} %param.44) | copy-start | bytes 9437188
  7.2 145.0 %all-gather.5.cloned.1.call-start = ((), (), s32[]{:S(2)}) async-start(), calls=%async_computation.2 | async-start | bytes 6488064 | tf_op jit(solution)/shard_map/all_gather | solution.py:484
  9.6 13.4 copy-start.29
  12.8 12.0 copy-start.25
  16.8 196.9 %all-gather.3.cloned.1.call-start = ((), (), s32[]{:S(2)}) async-start(), calls=%async_computation.1 | async-start | bytes 6488064 | tf_op jit(solution)/shard_map/all_gather | solution.py:487
  20.7 764.6 %reduce-scatter.4.cloned.1.call-start = ((), (), s32[]{:S(2)}) async-start(), calls=%async_computation.3 | async-start | bytes 540672
  30.0 115.3 %copy-start.60 = (f32[64,32]{0,1:T(8,128)}, f32[64,32]{0,1:T(8,128)S(1)}, u32[]{:S(2)}) copy-start(f32[64,32]{0,1:T(8,128)S(1)} %get-tuple-element.783) | copy-start | bytes 24580
  169.5 53.7 %copy-start.35 = (f32[2,12,64]{2,1,0:T(8,128)S(1)}, f32[2,12,64]{2,1,0:T(8,128)}, u32[]{:S(2)}) copy-start(f32[2,12,64]{2,1,0:T(8,128)} %log_add_fusion) | copy-start | bytes 18436
  223.3 5.0 copy-start.70
  258.5 11.0 copy-start.16
  259.3 4.2 copy-start.31
  265.8 3.6 copy-start.33
  265.8 3.6 copy-start.34
  270.3 3.4 copy-start.22
  273.8 3.9 copy-start.10
  288.4 5.1 copy-start.3
  303.0 4.6 copy-start.71
  307.6 5.7 copy-start.55
  351.9 966.1 %all-reduce.5.cloned.1.call-start = ((), (), s32[]{:S(2)}) async-start(), calls=%async_computation.4 | async-start | bytes 25165824
  352.0 4.3 copy-start.9
  352.4 6.5 copy-start.61
  352.5 6.5 copy-start.63
  356.2 4.2 copy-start.73
  356.2 4.8 copy-start.50
  357.6 4.3 copy-start.59
  357.7 5.2 copy-start.32
  371.1 3.9 copy-start.54
  770.1 8.0 copy-start.40
  770.1 9.5 copy-start.41
  770.1 13.7 copy-start.85
  778.0 3.0 copy-start.39
  778.0 3.0 copy-start.51
  778.0 4.5 copy-start.21
  778.0 5.8 copy-start.17
  778.1 5.8 copy-start.47
  778.1 5.8 copy-start.82
  783.8 3.2 copy-start.13
  783.9 3.2 copy-start.66
  783.9 3.2 copy-start.78
  783.9 535.5 %copy-start.45 = (bf16[2,256,384]{2,1,0:T(8,128)(2,1)S(1)}, bf16[2,256,384]{2,1,0:T(8,128)(2,1)}, u32[]{:S(2)}) copy-start(bf16[2,256,384]{2,1,0:T(8,128)(2,1)} %param.39) | copy-start | bytes 1179652
  785.3 534.3 %copy-start.26 = (bf16[128,512]{0,1:T(8,128)(2,1)S(1)}, bf16[128,512]{0,1:T(8,128)(2,1)}, u32[]{:S(2)}) copy-start(bf16[128,512]{0,1:T(8,128)(2,1)} %copy-done.25) | copy-start | bytes 393220
  787.3 535.9 %copy-start.27 = (bf16[768,512]{1,0:T(8,128)(2,1)S(1)}, bf16[768,512]{1,0:T(8,128)(2,1)}, u32[]{:S(2)}) copy-start(bf16[768,512]{1,0:T(8,128)(2,1)} %param.37) | copy-start | bytes 2359300
  1325.8 3.6 copy-start.44
  1325.8 4.9 copy-start.80
  1398.0 9.8 copy-start.14
  1419.2 5.1 copy-start.15
  1421.9 5.8 copy-start.28
  1429.1 11.7 copy-start.1
  (42 other events, 77.2 us)
Sparse Core Ops, SparseCore 0:
  16.9 102.9 all-gather.4
  123.5 90.0 all-gather.2
  352.0 388.3 reduce-scatter.3
  743.0 574.9 all-reduce.4

commit v2 on v0

v2 whole, which is shorter than its diff:
```python
import jax
import jax.numpy as jnp
from jax import lax
from jax.sharding import PartitionSpec as P
from jax.experimental import pallas as pl
from jax.experimental.pallas import tpu as pltpu

MESH = pl.DeviceIdType.MESH
BF = jnp.bfloat16
F32 = jnp.float32
EPSILON = 1e-06
ROPE = 64
GROUPS = 4
FACTOR = 128.0**-0.5
LOG2E = 1.4426950408889634
HIDDEN_SCORE = -1e30
ORDERS = ((0, 1, 2), (1, 2, 0), (2, 0, 1))


def coords():
    s = lax.axis_index("seq")
    b = lax.axis_index("blk")
    x = lax.rem(b, 2) * 2 + lax.div(s, 2)
    return x, lax.div(b, 8), lax.rem(lax.div(b, 2), 4), lax.rem(s, 2)


def device(x, y, z, core):
    return (lax.rem(x, 2) * 2 + core, y * 8 + z * 2 + lax.div(x, 2))


def on_ring(place, axis, step):
    spot = list(place)
    spot[axis] = lax.rem(place[axis] + step, 4)
    return device(*spot)


def remote(src, dst, send, recv, peer):
    return pltpu.make_async_remote_copy(
        src_ref=src, dst_ref=dst, send_sem=send, recv_sem=recv, device_id=peer, device_id_type=MESH
    )


def rows_at(start, size, multiple=16):
    return pl.ds(pl.multiple_of(start, multiple), size)


def dot(left, right):
    return jnp.dot(left, right, preferred_element_type=F32)


def dot_nt(left, right):
    return lax.dot_general(left, right, (((1,), (1,)), ((), ())), preferred_element_type=F32)


def dot_tn(left, right):
    return lax.dot_general(left, right, (((0,), (0,)), ((), ())), preferred_element_type=F32)


class Reduction:
    def __init__(self, place, total, first, second, third, chunk, send, recv, keep, outs, tall):
        self.place = place
        self.total, self.first, self.second, self.third, self.chunk = total, first, second, third, chunk
        self.send, self.recv, self.keep, self.outs, self.tall = send, recv, keep, outs, tall
        self.n, self.width = total.shape[2], total.shape[4]

    def spots(self, o):
        a, b, c = ORDERS[o]
        return self.place[a], self.place[b], self.place[c]

    def region(self, o, m, i, row, rows, count=1):
        core, width = self.place[3], self.width
        if self.tall[m]:
            if count == 4:
                return self.outs[m].at[rows_at(core * 4 * 256, 1024), pl.ds(o * width, width)]
            return self.outs[m].at[rows_at((core * 4 + i) * 256 + row, rows), pl.ds(o * width, width)]
        return self.outs[m].at[rows_at(o * 256 + row, rows), rows_at((core * 4 + i) * width, count * width, 128)]

    def copies(self, o, stage):
        i, j, k = self.spots(o)
        made = []
        if stage == 6:
            x, y, z, core = self.place
            for m in range(self.n):
                here = self.region(o, m, 0, 0, 256, 4)
                made.append(
                    remote(here, here, self.send.at[o, 6, 0, m], self.recv.at[o, 6, 0, m], device(x, y, z, 1 - core))
                )
            return made
        axis = ORDERS[o][(0, 1, 2, 2, 1, 0)[stage]]
        for step in (1, 2, 3):
            to = lax.rem(self.place[axis] + step, 4)
            peer = on_ring(self.place, axis, step)
            if stage < 3:
                if stage == 0:
                    src, dst = self.total.at[o, to], self.first.at[o, step - 1]
                elif stage == 1:
                    src, dst = self.total.at[o, i, :, rows_at(to * 64, 64)], self.second.at[o, step - 1]
                else:
                    src, dst = self.total.at[o, i, :, rows_at(j * 64 + to * 16, 16)], self.third.at[o, step - 1]
                made.append(
                    remote(src, dst, self.send.at[o, stage, step - 1, 0], self.recv.at[o, stage, step - 1, 0], peer)
                )
                continue
            row, rows = ((j * 64 + k * 16, 16), (j * 64, 64), (0, 256))[stage - 3]
            for m in range(self.n):
                here = self.region(o, m, i, row, rows)
                src = self.chunk.at[o, m] if stage == 3 else here
                made.append(
                    remote(src, here, self.send.at[o, stage, step - 1, m], self.recv.at[o, stage, step - 1, m], peer)
                )
        return made

    def kept(self, o):
        i, j, k = self.spots(o)
        return [
            pltpu.make_async_copy(
                self.chunk.at[o, m], self.region(o, m, i, j * 64 + k * 16, 16), self.keep.at[o, m]
            )
            for m in range(self.n)
        ]

    def start(self, stage, orders=(0, 1, 2)):
        for o in orders:
            for copy in self.copies(o, stage):
                copy.start()
            if stage == 3:
                for copy in self.kept(o):
                    copy.start()

    def finish(self, stage, orders=(0, 1, 2)):
        for o in orders:
            for copy in self.copies(o, stage):
                copy.wait()
            if stage == 3:
                for copy in self.kept(o):
                    copy.wait()
            if stage < 3:
                self.add(o, stage)

    def step(self, stage):
        for o in range(3):
            self.finish(stage, (o,))
            self.start(stage + 1, (o,))

    def add(self, o, stage):
        i, j, k = self.spots(o)
        rows = (64, 64, 16)[stage]
        base = (0, j * 64, j * 64 + k * 16)[stage]
        arrived = (self.first, self.second, self.third)[stage]
        parts = 4 if stage == 0 else 1

        def body(step, carried):
            m = lax.div(step, parts)
            shift = lax.rem(step, parts) * 64
            here, there = rows_at(base + shift, rows), rows_at(shift, rows)
            acc = self.total[o, i, m, here, :].astype(F32)
            for slot in range(3):
                acc = acc + arrived[o, slot, m, there, :].astype(F32)
            if stage == 2:
                self.chunk[o, m] = acc.astype(BF)
            else:
                self.total[o, i, m, here, :] = acc.astype(BF)
            return carried

        lax.fori_loop(0, self.n * parts, body, 0)


def reduction_scratch(name, n, width):
    return {
        name + "_total": pltpu.VMEM((3, 4, n, 256, width), BF),
        name + "_first": pltpu.VMEM((3, 3, n, 256, width), BF),
        name + "_second": pltpu.VMEM((3, 3, n, 64, width), BF),
        name + "_third": pltpu.VMEM((3, 3, n, 16, width), BF),
        name + "_chunk": pltpu.VMEM((3, n, 16, width), BF),
        name + "_send": pltpu.SemaphoreType.DMA((3, 7, 3, n)),
        name + "_recv": pltpu.SemaphoreType.DMA((3, 7, 3, n)),
        name + "_keep": pltpu.SemaphoreType.DMA((3, n)),
    }


WEIGHTS = {
    "w_latent": (768, 512),
    "w_krope": (768, 64),
    "w_query": (768, 768),
    "w_qrope": (768, 768),
    "w_upkey": (2, 256, 384),
    "w_upval": (2, 256, 384),
    "w_out": (768, 768),
    "w_gate": (768, 2048),
    "w_up": (768, 2048),
    "w_down": (2048, 768),
}
SMALL = ("tokens", "cotangent", "seq_weight", "cosine", "sine", "norm_attn", "norm_mlp")
OUTS = {
    "layer_out": ((2, 64, 768), BF),
    "grad_tokens": ((2, 64, 768), F32),
    "g_gate": ((768, 2048), BF),
    "g_up": ((768, 2048), BF),
    "g_down": ((2048, 768), BF),
    "g_query": ((768, 1024), BF),
    "g_qrope": ((768, 1024), BF),
    "g_out": ((768, 1024), BF),
    "g_late": ((768, 1024), BF),
}


def scratch():
    vmem, dma = pltpu.VMEM, pltpu.SemaphoreType.DMA
    made = {"v" + name[1:]: vmem(shape, BF) for name, shape in WEIGHTS.items()}
    made.update(
        load_sem=dma((len(WEIGHTS),)),
        swap_sem=dma((4, 2)),
        pair_sem=dma((12, 2)),
        ag_sem=dma((2, 2, 2, 3, 2)),
        rs_sem=dma((2, 2, 2, 3, 2)),
        xbuf=vmem((128, 768), BF),
        cbuf=vmem((128, 768), BF),
        norm2=vmem((256, 768), BF),
        normt=vmem((768, 256), BF),
        krd=vmem((128, 128), F32),
        q=vmem((128, 768), BF),
        qr=vmem((128, 768), BF),
        lat=vmem((4, 4, 4, 64, 256), BF),
        kr=vmem((4, 4, 64, 128), BF),
        latt=vmem((4, 4, 4, 64, 256), BF),
        krt=vmem((2, 4, 128, 256), BF),
        rel=vmem((2, 256, 384), jnp.int32),
        qs=vmem((4, 384, 256), BF),
        ga=vmem((4, 384, 256), BF),
        qrx=vmem((2, 4, 384, 128), BF),
        acc=vmem((4, 256, 384), F32),
        ctx=vmem((4, 256, 384), BF),
        logs=vmem((4, 8, 384), F32),
        delta=vmem((4, 8, 384), F32),
        aof=vmem((128, 768), F32),
        ao2=vmem((256, 768), BF),
        middle=vmem((128, 768), F32),
        nm2=vmem((256, 768), BF),
        nmt=vmem((768, 256), BF),
        gb2=vmem((256, 768), BF),
        acts=vmem((3, 256, 1024), BF),
        other=vmem((3, 128, 1024), BF),
        hidt=vmem((1024, 256), BF),
        outacc=vmem((128, 768), F32),
        gnm=vmem((128, 768), F32),
        outbf=vmem((128, 768), BF),
        gattn=vmem((2, 256, 384), BF),
        gmix=vmem((128, 768), BF),
        dqr=vmem((4, 128, 384), F32),
        dlat=vmem((4, 4, 256, 256), F32),
        dkr=vmem((4, 256, 128), F32),
        skr=vmem((4, 4, 64, 128), BF),
        ro1=vmem((3, 2, 4, 64, 256), BF),
        rk1=vmem((3, 4, 64, 128), BF),
        rt1=vmem((3, 2, 4, 64, 256), BF),
        so1=vmem((2, 4, 64, 256), BF),
        ks1=vmem((4, 64, 128), BF),
        st1=vmem((2, 4, 64, 256), BF),
        ro2=vmem((3, 2, 64, 256), BF),
        rk2=vmem((3, 64, 128), BF),
        rt2=vmem((3, 2, 64, 256), BF),
        gq2=vmem((2, 256, 384), BF),
        gqp2=vmem((2, 256, 384), BF),
        gl2=vmem((2, 256, 256), BF),
        dup=vmem((2, 2, 3, 256, 128), BF),
        sup=vmem((2, 3, 256, 128), BF),
        gmid=vmem((128, 768), F32),
        gains=vmem((16, 128), F32),
    )
    made.update(reduction_scratch("wide", 3, 256))
    made.update(reduction_scratch("early", 3, 128))
    made.update(reduction_scratch("late", 1, 128))
    return made


class Refs:
    pass


def swap_halves(values):
    lanes = values.shape[-1]
    low = lax.rem(lax.broadcasted_iota(jnp.int32, values.shape, 1), 64) < 32
    return jnp.where(low, pltpu.roll(values, lanes - 32, 1), pltpu.roll(values, 32, 1))


def layer_kernel(*args):
    r = Refs()
    shapes = scratch()
    names = list(SMALL) + list(WEIGHTS) + list(OUTS) + list(shapes)
    for name, ref in zip(names, args, strict=True):
        setattr(r, name, ref)
    place = coords()
    x, y, z, core = place
    x_hi = lax.div(x, 2)
    blk = y * 8 + z * 2 + x_hi
    slot = y * 4 + z
    sibling = device(x, y, z, 1 - core)
    partner = device(lax.rem(x + 2, 4), 3 - y, 3 - z, core)
    peers = [on_ring(place, axis, step) for axis in range(3) for step in (1, 2, 3)] + [sibling, partner]
    low64 = lambda rows: lax.broadcasted_iota(jnp.int32, (rows, 128), 1) < 64
    diagonal = (lax.broadcasted_iota(jnp.int32, (128, 128), 0) < 64) == low64(128)

    def both(value):
        return jnp.where(diagonal, jnp.concatenate([value, value], axis=0), jnp.zeros((), value.dtype))

    def pick(value):
        return jnp.where(low64(64), value[0:64], value[64:128])

    loads = {}
    for at, name in enumerate(WEIGHTS):
        loads[name] = pltpu.make_async_copy(getattr(r, name), getattr(r, "v" + name[1:]), r.load_sem.at[at])
        loads[name].start()
    barrier = pltpu.get_barrier_semaphore()
    for peer in peers:
        pl.semaphore_signal(barrier, inc=1, device_id=peer, device_id_type=MESH)
    pl.semaphore_wait(barrier, len(peers))

    def swap(at, src, dst):
        return remote(src, dst, r.swap_sem.at[at, 0], r.swap_sem.at[at, 1], partner)

    def paired(at, src, dst):
        return remote(src, dst, r.pair_sem.at[at, 0], r.pair_sem.at[at, 1], sibling)

    swap_x = swap(0, r.tokens.at[1 - x_hi], r.xbuf.at[pl.ds(64, 64)])
    swap_c = swap(1, r.cotangent.at[1 - x_hi], r.cbuf.at[pl.ds(64, 64)])
    swap_x.start()
    swap_c.start()
    r.xbuf[0:64] = r.tokens[x_hi]
    r.cbuf[0:64] = r.cotangent[x_hi]
    key_row = lax.broadcasted_iota(jnp.int32, (256, 384), 0)
    query_lane = lax.rem(lax.broadcasted_iota(jnp.int32, (256, 384), 1), 64)
    within = lax.rem(key_row, 64) - query_lane
    r.rel[0] = 128 * lax.div(key_row, 64) + within
    r.rel[1] = within - 128 * lax.div(key_row, 64)
    swap_x.wait()

    def unit_of(values):
        inverse = lax.rsqrt(jnp.mean(values * values, axis=-1, keepdims=True) + EPSILON)
        return values * inverse, inverse

    unit = unit_of(r.xbuf[...].astype(F32))[0]
    normed = (unit * r.norm_attn[...]).astype(BF)
    r.norm2[0:128] = normed
    send_norm = paired(0, r.norm2.at[pl.ds(0, 128)], r.norm2.at[pl.ds(128, 128)])
    send_norm.start()
    loads["w_latent"].wait()
    loads["w_krope"].wait()
    key_pre = dot(normed, r.v_krope[...])
    r.krd[:, 0:64] = key_pre
    r.krd[:, 64:128] = key_pre
    key_pre = r.krd[...]
    key_rot = (key_pre * r.cosine[...] + swap_halves(key_pre) * r.sine[...]).astype(BF)
    r.kr[y, z] = pick(key_rot)
    latents = dot(normed, r.v_latent[...]).astype(BF)
    for half in range(2):
        for g in range(2):
            r.lat[half * 2 + g, y, z] = latents[half * 64 : half * 64 + 64, g * 256 : g * 256 + 256]

    def gather(part, phase):
        made = []
        axis = (2, 1)[(part + phase) % 2]
        for step in (1, 2, 3):
            peer = on_ring(place, axis, step)
            two = pl.ds(part * 2, 2)
            if phase == 0:
                pieces = [r.lat.at[two, y, z], r.kr.at[y, z]]
            elif part == 0:
                pieces = [r.lat.at[two, y], r.kr.at[y]]
            else:
                pieces = [r.lat.at[two, :, z], None]
            for at, piece in enumerate(pieces if part == 0 else pieces[:1]):
                sem = r.ag_sem.at[part, phase, at, step - 1]
                made.append(remote(piece, piece, sem.at[0], sem.at[1], peer))
        return made

    for part in range(2):
        for copy in gather(part, 0):
            copy.start()

    loads["w_query"].wait()
    r.q[...] = dot(normed, r.v_query[...]).astype(BF)
    loads["w_qrope"].wait()
    query_pre = dot(normed, r.v_qrope[...])
    for p in range(6):
        lanes = slice(p * 128, p * 128 + 128)
        piece = query_pre[:, lanes]
        r.qr[:, lanes] = (piece * r.cosine[...] + swap_halves(piece) * r.sine[...]).astype(BF)
    loads["w_upkey"].wait()

    def to_latent(source, weights, target):
        for half in range(2):
            for g in range(2):
                for j in range(3):
                    p = g * 3 + j
                    block = both(source[half * 64 : half * 64 + 64, p * 128 : p * 128 + 128])
                    rows = dot_nt(block, weights[g, :, j * 128 : j * 128 + 128])
                    target[half * 2 + g, j * 128 : j * 128 + 128] = rows.astype(BF)

    to_latent(r.q, r.v_upkey, r.qs)
    for half in range(2):
        for p in range(6):
            pair = r.qr[half * 64 : half * 64 + 64, p * 128 : p * 128 + 128].astype(F32)
            turned = pltpu.roll(pair, 64, 1)
            for odd in range(2):
                front, back = (turned, pair) if odd else (pair, turned)
                at = (p % 3) * 128 + odd * 64
                here = (half * 2 + p // 3, slice(at, at + 64))
                r.qrx[(0,) + here] = jnp.where(low64(64), front, 0.0).astype(BF)
                r.qrx[(1,) + here] = jnp.where(low64(64), 0.0, back).astype(BF)

    for part in range(2):
        for copy in gather(part, 0):
            copy.wait()
        for copy in gather(part, 1):
            copy.start()
    for part in range(2):
        for copy in gather(part, 1):
            copy.wait()

    def transpose_latents(step, carried):
        j, c = lax.div(step, 4), lax.rem(step, 4)
        r.latt[j, c] = r.lat[j, c].reshape(256, 256).T.reshape(4, 64, 256)
        return carried

    lax.fori_loop(0, 16, transpose_latents, 0)
    top = lax.broadcasted_iota(jnp.int32, (128, 256), 0) < 64
    for c in range(4):
        turned = r.kr[c].reshape(256, 128).astype(F32).T
        r.krt[0, c] = jnp.where(top, turned, 0.0).astype(BF)
        r.krt[1, c] = jnp.where(top, 0.0, turned).astype(BF)

    own_count = (y + 1, lax.div(16 - x_hi - slot + 3, 4))
    far_count = (lax.div(slot + x_hi + 3, 4), 4 - y)
    query_blk = (blk, 31 - blk)

    def chosen(half, pair):
        return jnp.where(half == 0, pair[0], pair[1])

    def key_chunk(half, step):
        near = chosen(half, own_count)
        far = (step >= near).astype(jnp.int32)
        chunk = jnp.where(step < near, step, 4 - chosen(half, far_count) + step - near)
        first = chosen(half, query_blk) * 64
        edge = jnp.where(far == 0, first - 512 * chunk - 64 * x_hi, first - 1984 + 512 * chunk + 64 * x_hi)
        return far, chunk, r.rel[far] <= edge

    def raw_scores(at, far, chunk, g):
        keys = r.lat[far * 2 + g, chunk].reshape(256, 256)
        rot = r.kr[chunk].reshape(256, 128)
        return dot_nt(keys, r.qs[at]) + dot_nt(rot, r.qrx[far, at]), keys

    r.acc[...] = jnp.zeros_like(r.acc)

    def forward_half(half, carried):
        def chunk_step(step, state):
            far, chunk, allowed = key_chunk(half, step)
            result = []
            for g in range(2):
                at = half * 2 + g
                high, total = state[g]
                raw = raw_scores(at, far, chunk, g)[0]
                raw = jnp.where(allowed, raw, HIDDEN_SCORE)
                new_high = jnp.maximum(high, jnp.max(raw, axis=0, keepdims=True))
                shrink = jnp.exp2((high - new_high) * (FACTOR * LOG2E))
                weights = jnp.exp2((raw - new_high) * (FACTOR * LOG2E))
                total = total * shrink + jnp.sum(weights, axis=0, keepdims=True)
                r.acc[at] = r.acc[at] * shrink + dot(r.latt[far * 2 + g, chunk].reshape(256, 256), weights.astype(BF))
                result.append((new_high, total))
            return tuple(result)

        empty = (jnp.full((1, 384), HIDDEN_SCORE, F32), jnp.zeros((1, 384), F32))
        count = chosen(half, own_count) + chosen(half, far_count)
        state = lax.fori_loop(0, count, chunk_step, (empty, empty))
        for g in range(2):
            high, total = state[g]
            at = half * 2 + g
            r.ctx[at] = (r.acc[at] * (1.0 / total)).astype(BF)
            r.logs[at] = jnp.broadcast_to(high * (FACTOR * LOG2E) + jnp.log2(total), (8, 384))
        return carried

    lax.fori_loop(0, 2, forward_half, 0)
    loads["w_upval"].wait()

    def from_latent(source, weights, half, p):
        g, j = p // 3, p % 3
        lanes = slice(j * 128, j * 128 + 128)
        return pick(dot_tn(source[half * 2 + g, :, lanes].astype(BF), weights[g, :, lanes]))

    for half in range(2):
        for p in range(6):
            r.aof[half * 64 : half * 64 + 64, p * 128 : p * 128 + 128] = from_latent(r.ctx, r.v_upval, half, p)
    r.ao2[0:128] = r.aof[...].astype(BF)
    send_ao = paired(1, r.ao2.at[pl.ds(0, 128)], r.ao2.at[pl.ds(128, 128)])
    send_ao.start()

    loads["w_out"].wait()
    middle = r.xbuf[...].astype(F32) + dot(r.ao2[0:128], r.v_out[...])
    r.middle[...] = middle
    unit_mlp = unit_of(middle)[0]
    r.nm2[0:128] = (unit_mlp * r.norm_mlp[...]).astype(BF)
    send_nm = paired(2, r.nm2.at[pl.ds(0, 128)], r.nm2.at[pl.ds(128, 128)])
    send_nm.start()
    swap_c.wait()
    weight = jnp.where(x_hi == 0, r.seq_weight[0:1, 0:1], r.seq_weight[1:2, 0:1])
    r.gb2[0:128] = (r.cbuf[...].astype(F32) * weight).astype(BF)
    send_gb = paired(3, r.gb2.at[pl.ds(0, 128)], r.gb2.at[pl.ds(128, 128)])
    send_gb.start()
    r.outacc[...] = middle
    r.gnm[...] = jnp.zeros_like(r.gnm)
    for name in ("w_gate", "w_up", "w_down"):
        loads[name].wait()

    def feed(half, target):
        def tile(step, carried):
            at = rows_at(half * 1024 + step * 256, 256, 256)
            cols = rows_at(step * 256, 256, 256)
            act = r.nm2[0:128]
            gate = dot(act, r.v_gate[:, at])
            up = dot(act, r.v_up[:, at])
            sig = jax.nn.sigmoid(gate)
            silu = gate * sig
            hidden = (silu * up).astype(BF)
            grad_hidden = dot_nt(r.gb2[0:128], r.v_down[at, :])
            grad_gate = (grad_hidden * up * sig * (1.0 + gate * (1.0 - sig))).astype(BF)
            grad_up = (grad_hidden * silu).astype(BF)
            target[0, 0:128, cols] = hidden
            target[1, 0:128, cols] = grad_gate
            target[2, 0:128, cols] = grad_up
            r.outacc[...] += dot(hidden, r.v_down[at, :])
            r.gnm[...] += dot_nt(grad_gate, r.v_gate[:, at]) + dot_nt(grad_up, r.v_up[:, at])
            return carried

        lax.fori_loop(0, 4, tile, 0)

    feed(1 - core, r.other)
    send_acts = paired(4, r.other, r.acts.at[:, pl.ds(128, 128)])
    send_acts.start()
    feed(core, r.acts)
    r.outbf[...] = r.outacc[...].astype(BF)
    r.layer_out[x_hi] = r.outbf[0:64]
    swap_out = swap(2, r.outbf.at[pl.ds(64, 64)], r.layer_out.at[x_hi])
    swap_out.start()

    def norm_back(grads, values, gain):
        unit_rows, inverse = unit_of(values)
        scaled = grads * gain
        gain_grad = jnp.sum(grads * unit_rows, axis=0, keepdims=True)
        mean = jnp.mean(scaled * unit_rows, axis=-1, keepdims=True)
        return inverse * (scaled - unit_rows * mean), gain_grad

    back, gain_mlp = norm_back(r.gnm[...], r.middle[...], r.norm_mlp[...])
    r.gmid[...] = r.cbuf[...].astype(F32) * weight + back
    gain_row = lax.broadcasted_iota(jnp.int32, (16, 128), 0)
    gains = jnp.zeros((16, 128), F32)
    for p in range(6):
        gains = gains + jnp.where(gain_row == 6 + p, gain_mlp[:, p * 128 : p * 128 + 128], 0.0)
    r.gains[...] = gains
    grad_attn = r.gmid[...].astype(BF)
    for half in range(2):
        r.gattn[half, 0:128] = grad_attn[:, half * 384 : half * 384 + 384]
    send_ga = paired(5, r.gattn.at[1 - core, pl.ds(0, 128)], r.gattn.at[1 - core, pl.ds(128, 128)])
    send_ga.start()
    mixed = dot_nt(grad_attn, r.v_out[...])
    r.gmix[...] = mixed.astype(BF)
    to_latent(r.gmix, r.v_upval, r.ga)
    ones = jnp.ones((8, 128), F32)
    for half in range(2):
        for p in range(6):
            here = (slice(half * 64, half * 64 + 64), slice(p * 128, p * 128 + 128))
            block = both(r.gmix[here].astype(F32) * r.aof[here])
            sums = lax.dot_general(
                ones, block, (((1,), (1,)), ((), ())), precision=lax.Precision.HIGHEST, preferred_element_type=F32
            )
            r.delta[half * 2 + p // 3, :, (p % 3) * 128 : (p % 3) * 128 + 128] = sums

    wide = Reduction(
        place, r.wide_total, r.wide_first, r.wide_second, r.wide_third, r.wide_chunk, r.wide_send, r.wide_recv,
        r.wide_keep, (r.g_gate, r.g_up, r.g_down), (False, False, True),
    )
    early = Reduction(
        place, r.early_total, r.early_first, r.early_second, r.early_third, r.early_chunk, r.early_send,
        r.early_recv, r.early_keep, (r.g_query, r.g_qrope, r.g_out), (False, False, False),
    )
    late = Reduction(
        place, r.late_total, r.late_first, r.late_second, r.late_third, r.late_chunk, r.late_send, r.late_recv,
        r.late_keep, (r.g_late,), (False,),
    )
    for copy in (send_nm, send_gb, send_acts):
        copy.wait()
    r.nmt[...] = r.nm2[...].T
    r.hidt[...] = r.acts[0].T
    for o in range(3):

        def wide_tile(i, carried):
            cols = rows_at(i * 256, 256, 256)
            left = r.nmt[o * 256 : o * 256 + 256]
            r.wide_total[o, i, 0] = dot(left, r.acts[1, :, cols]).astype(BF)
            r.wide_total[o, i, 1] = dot(left, r.acts[2, :, cols]).astype(BF)
            r.wide_total[o, i, 2] = dot(r.hidt[cols, :], r.gb2[:, o * 256 : o * 256 + 256]).astype(BF)
            return carried

        lax.fori_loop(0, 4, wide_tile, 0)
        wide.start(0, (o,))

    r.acc[...] = jnp.zeros_like(r.acc)
    r.dqr[...] = jnp.zeros_like(r.dqr)
    r.dlat[...] = jnp.zeros_like(r.dlat)
    r.dkr[...] = jnp.zeros_like(r.dkr)

    def backward_half(half, carried):
        def chunk_step(step, inner):
            far, chunk, allowed = key_chunk(half, step)
            for g in range(2):
                at = half * 2 + g
                raw, keys = raw_scores(at, far, chunk, g)
                weights = jnp.exp2(raw * (FACTOR * LOG2E) - r.logs[at, 0:1])
                weights = jnp.where(allowed, weights, 0.0)
                dprob = dot_nt(keys, r.ga[at])
                dscore = (weights * (dprob - r.delta[at, 0:1])).astype(BF)
                weights = weights.astype(BF)
                r.acc[at] += dot(r.latt[far * 2 + g, chunk].reshape(256, 256), dscore)
                r.dqr[at] += dot(r.krt[far, chunk], dscore)
                r.dlat[far * 2 + g, chunk] += FACTOR * dot(dscore, r.qs[at]) + dot(weights, r.ga[at])
                r.dkr[chunk] += FACTOR * dot(dscore, r.qrx[far, at])
            return inner

        count = chosen(half, own_count) + chosen(half, far_count)
        lax.fori_loop(0, count, chunk_step, 0)
        return carried

    lax.fori_loop(0, 2, backward_half, 0)

    def narrow(step, carried):
        j, c = lax.div(step, 4), lax.rem(step, 4)
        r.latt[j, c] = r.dlat[j, c].astype(BF).reshape(4, 64, 256)
        return carried

    lax.fori_loop(0, 16, narrow, 0)
    for c in range(4):
        r.skr[c] = r.dkr[c].astype(BF).reshape(4, 64, 128)

    def scatter(part, phase):
        made = []
        axis = (1, 2)[(part + phase) % 2]
        for step in (1, 2, 3):
            peer = on_ring(place, axis, step)
            to = lax.rem(place[axis] + step, 4)
            at = step - 1
            if part == 0 and phase == 0:
                pieces = [(r.latt.at[pl.ds(0, 2), to], r.ro1.at[at]), (r.skr.at[to], r.rk1.at[at])]
            elif part == 0:
                pieces = [(r.so1.at[:, to], r.ro2.at[at]), (r.ks1.at[to], r.rk2.at[at])]
            elif phase == 0:
                pieces = [(r.latt.at[pl.ds(2, 2), :, to], r.rt1.at[at])]
            else:
                pieces = [(r.st1.at[:, to], r.rt2.at[at])]
            for k, (src, dst) in enumerate(pieces):
                sem = r.rs_sem.at[part, phase, k, at]
                made.append(remote(src, dst, sem.at[0], sem.at[1], peer))
        return made

    for part in range(2):
        for copy in scatter(part, 0):
            copy.start()

    for half in range(2):
        for p in range(6):
            rows, lanes = slice(half * 64, half * 64 + 64), slice((p % 3) * 128, (p % 3) * 128 + 128)
            at = half * 2 + p // 3
            piece = (FACTOR * from_latent(r.acc, r.v_upkey, half, p)).astype(BF)
            r.gq2[p // 3, rows, lanes] = piece
            turned = FACTOR * r.dqr[at, :, lanes].T
            turned = pick(turned + pltpu.roll(turned, 64, 1))
            turned = turned * r.cosine[rows, :] - swap_halves(turned) * r.sine[rows, :]
            r.gqp2[p // 3, rows, lanes] = turned.astype(BF)
    send_gq = paired(6, r.gq2.at[1 - core, pl.ds(0, 128)], r.gq2.at[1 - core, pl.ds(128, 128)])
    send_gqp = paired(7, r.gqp2.at[1 - core, pl.ds(0, 128)], r.gqp2.at[1 - core, pl.ds(128, 128)])
    send_gq.start()
    send_gqp.start()
    for g in range(2):
        for j in range(3):
            lanes = slice(j * 128, j * 128 + 128)
            wide_lanes = slice((g * 3 + j) * 128, (g * 3 + j) * 128 + 128)
            key_sum, value_sum = jnp.zeros((256, 128), F32), jnp.zeros((256, 128), F32)
            for half in range(2):
                rows = slice(half * 64, half * 64 + 64)
                key_sum += FACTOR * dot(r.acc[half * 2 + g, :, lanes].astype(BF), both(r.q[rows, wide_lanes]))
                value_sum += dot(r.ctx[half * 2 + g, :, lanes], both(r.gmix[rows, wide_lanes]))
            r.dup[g, 0, j] = key_sum.astype(BF)
            r.dup[g, 1, j] = value_sum.astype(BF)
    send_up = paired(8, r.dup.at[1 - core], r.sup)
    send_up.start()
    wide.step(0)
    grad_normed = dot_nt(r.gq2[0, 0:128], r.v_query[:, 0:384]) + dot_nt(r.gq2[1, 0:128], r.v_query[:, 384:768])
    grad_normed += dot_nt(r.gqp2[0, 0:128], r.v_qrope[:, 0:384]) + dot_nt(r.gqp2[1, 0:128], r.v_qrope[:, 384:768])
    r.gnm[...] = grad_normed
    send_norm.wait()
    r.normt[...] = r.norm2[...].T
    send_ao.wait()
    send_ga.wait()
    send_gq.wait()
    send_gqp.wait()
    send_up.wait()
    r.nmt[...] = r.ao2[...].T
    for o in range(3):
        rows = slice(o * 256, o * 256 + 256)
        for m, (left, right) in enumerate(((r.normt, r.gq2), (r.normt, r.gqp2), (r.nmt, r.gattn))):
            block = dot(left[rows], right[core]).astype(BF)
            for i in range(3):
                r.early_total[o, i, m] = block[:, i * 128 : i * 128 + 128]
        for m in range(2):
            r.early_total[o, 3, m] = (r.dup[core, m, o].astype(F32) + r.sup[m, o].astype(F32)).astype(BF)
        r.early_total[o, 3, 2] = jnp.zeros((256, 128), BF)
        early.start(0, (o,))

    wide.step(1)
    for copy in scatter(0, 0) + scatter(1, 0):
        copy.wait()

    def fold(at, carried):
        for g in range(2):
            near = r.dlat[g, y, rows_at(at * 64, 64), :]
            far = r.dlat[2 + g, at, rows_at(z * 64, 64), :]
            for k in range(3):
                near = near + r.ro1[k, g, at].astype(F32)
                far = far + r.rt1[k, g, at].astype(F32)
            r.so1[g, at] = near.astype(BF)
            r.st1[g, at] = far.astype(BF)
        rot = r.dkr[y, rows_at(at * 64, 64), :]
        for k in range(3):
            rot = rot + r.rk1[k, at].astype(F32)
        r.ks1[at] = rot.astype(BF)
        return carried

    lax.fori_loop(0, 4, fold, 0)
    for part in range(2):
        for copy in scatter(part, 1):
            copy.start()
    wide.step(2)
    for copy in scatter(0, 1) + scatter(1, 1):
        copy.wait()
    grad_latents = []
    for g in range(2):
        near = r.so1[g, z].astype(F32)
        far = r.st1[g, y].astype(F32)
        for k in range(3):
            near = near + r.ro2[k, g].astype(F32)
            far = far + r.rt2[k, g].astype(F32)
        piece = jnp.concatenate([near, far], axis=0).astype(BF)
        grad_latents.append(piece)
        r.gl2[g, 0:128] = piece
    send_gl = paired(9, r.gl2.at[1 - core, pl.ds(0, 128)], r.gl2.at[1 - core, pl.ds(128, 128)])
    send_gl.start()
    rot = r.ks1[z].astype(F32)
    for k in range(3):
        rot = rot + r.rk2[k].astype(F32)
    turned = pltpu.roll(rot, 64, 1)
    rot = jnp.concatenate([jnp.where(low64(64), rot, turned), jnp.where(low64(64), turned, rot)], axis=0)
    grad_kpre = (rot * r.cosine[...] - swap_halves(rot) * r.sine[...]).astype(BF)
    grad_normed = r.gnm[...] + dot_nt(grad_kpre[:, 0:64], r.v_krope[...])
    for g in range(2):
        grad_normed = grad_normed + dot_nt(grad_latents[g], r.v_latent[:, g * 256 : g * 256 + 256])
    back, gain_attn = norm_back(grad_normed, r.xbuf[...].astype(F32), r.norm_attn[...])
    r.outacc[...] = r.gmid[...] + back
    r.grad_tokens[x_hi] = r.outacc[0:64]
    swap_grad = swap(3, r.outacc.at[pl.ds(64, 64)], r.grad_tokens.at[x_hi])
    swap_grad.start()
    gains = r.gains[...]
    for p in range(6):
        gains = gains + jnp.where(gain_row == p, gain_attn[:, p * 128 : p * 128 + 128], 0.0)
    for o in range(3):
        r.late_total[o, 3, 0] = jnp.zeros((256, 128), BF)
    r.late_total[0, 3, 0, 0:16] = gains.astype(BF)
    send_gl.wait()
    for o in range(3):
        rows = slice(o * 256, o * 256 + 256)
        block = dot(r.normt[rows], r.gl2[core]).astype(BF)
        for i in range(2):
            r.late_total[o, i, 0] = block[:, i * 128 : i * 128 + 128]
        r.late_total[o, 2, 0] = dot(r.normt[rows, 0:128], grad_kpre).astype(BF)
        late.start(0, (o,))
    wide.step(3)
    early.step(0)
    late.step(0)
    wide.step(4)
    early.step(1)
    late.step(1)
    early.step(2)
    late.step(2)
    early.step(3)
    late.step(3)
    early.step(4)
    late.step(4)
    wide.step(5)
    early.step(5)
    late.step(5)
    swap_out.wait()
    swap_grad.wait()
    for reduction in (wide, early, late):
        reduction.finish(6)


def layer(small, weights):
    vmem = pl.BlockSpec(memory_space=pltpu.VMEM)
    hbm = pl.BlockSpec(memory_space=pl.ANY)
    return pl.pallas_call(
        layer_kernel,
        out_shape=[jax.ShapeDtypeStruct(shape, kind) for shape, kind in OUTS.values()],
        in_specs=[vmem] * len(small) + [hbm] * len(weights),
        out_specs=[vmem, vmem] + [hbm] * (len(OUTS) - 2),
        scratch_shapes=list(scratch().values()),
        compiler_params=pltpu.CompilerParams(
            collective_id=1, has_side_effects=True, vmem_limit_bytes=63 * 2**20
        ),
    )(*small, *weights)


def local(
    tokens, cotangent, group_of_seq, group_weight, norm_attn, w_query, w_qrope, w_latent, w_krope, w_upkey, w_upval,
    w_out, norm_mlp, w_gate, w_up, w_down,
):
    blk = lax.axis_index("blk")
    within = jnp.arange(64, dtype=jnp.int32)
    positions = jnp.concatenate([blk * 64 + within, (31 - blk) * 64 + within]).astype(F32)
    halves = ROPE // 2
    freq_list = 10000.0 ** (-(jnp.arange(halves, dtype=F32) * 2.0 / ROPE))
    phases = positions[:, None] * freq_list[None, :]
    cosine, sine = jnp.cos(phases), jnp.sin(phases)
    cosine = jnp.concatenate([cosine] * 4, axis=1)
    sine = jnp.concatenate([-sine, sine, -sine, sine], axis=1)
    matches = group_of_seq[:, None] == jnp.arange(GROUPS, dtype=jnp.int32)[None, :]
    seq_weight = jnp.sum(jnp.where(matches, group_weight[None, :], 0.0), axis=1)
    seq_weight = jnp.broadcast_to(seq_weight[:, None], (2, 128))
    small = (tokens, cotangent, seq_weight, cosine, sine, norm_attn[None, :], norm_mlp[None, :])
    weights = (w_latent, w_krope, w_query, w_qrope, w_upkey, w_upval, w_out, w_gate, w_up, w_down)
    layer_out, grad_tokens, g_gate, g_up, g_down, g_query, g_qrope, g_out, g_late = layer(small, weights)

    def joined(grad, width):
        return jnp.concatenate([grad[:, 0:width], grad[:, 512 : 512 + width]], axis=1).astype(F32)

    def up_part(grad):
        both = jnp.stack([grad[:, 384:512], grad[:, 896:1024]]).reshape(2, 3, 256, 128)
        return jnp.transpose(both, (0, 2, 1, 3)).reshape(2, 256, 384).astype(F32)

    extra = g_late[:, 256:512].astype(F32) + g_late[:, 768:1024].astype(F32)
    gains = extra[0:12, 128:256].reshape(2, 768)
    return (
        layer_out,
        grad_tokens,
        gains[0],
        joined(g_query, 384),
        joined(g_qrope, 384),
        joined(g_late, 256),
        extra[:, 0:64],
        up_part(g_query),
        up_part(g_qrope),
        joined(g_out, 384),
        gains[1],
        g_gate.astype(F32),
        g_up.astype(F32),
        g_down.astype(F32),
    )


def solution(mesh):
    split = P("seq", "blk", None)
    in_specs = (split, split, P("seq")) + (P(),) * 13
    out_specs = (split, split) + (P(),) * 12
    return jax.shard_map(local, mesh=mesh, in_specs=in_specs, out_specs=out_specs, check_vma=False)
```

time: 1650 us -> 231 us (0.14)
  waiting for transfers between devices: 1170 us -> 0 us
  Pallas kernels: 0 us -> 192 us
  blocking collectives: 167 us -> 0 us
  local copies, waits for them, and re-layouts: 167 us -> 17.7 us
  matrix products: 85.9 us -> 0 us
    unnamed x7 -> x0, waiting for transfers between devices: 950 us -> none
    pallas_call x0 -> x1, Pallas kernels: none -> 192 us  [layer(): pl.pallas_call(layer_kernel, out_shape=[jax.ShapeDtypeStruct(shape, kind)...]
    psum x1 -> x0, waiting for transfers between devices: 172 us -> none  [local(): lax.psum((grad_norm_attn, grad_w_query, grad_w_qrope, grad_w_latent, grad...]
    all_gather x1 -> x0, blocking collectives: 104 us -> none  [local(): lax.all_gather(key_rot, 'blk', axis=1, tiled=True)]
    dot_general x45 -> x0, matrix products: 85.9 us -> none  [the longest x8 21.2 us: outer_sum(): lax.dot_general(left, right, (((0,), (0,)), ((), ())), preferred_element_...]
    psum x1 -> x0, blocking collectives: 63.4 us -> none  [local(): lax.psum((grad_norm_attn, grad_w_query, grad_w_qrope, grad_w_latent, grad...]
    while x65 -> x0, local copies, waits for them, and re-layouts: 49.9 us -> none  [the longest x5 24 us: attend_forward(): lax.fori_loop(0, block_count, weigh_values, jnp.zeros((query_len, HEADS,...]
    all_gather x2 -> x0, waiting for transfers between devices: 44.2 us -> none  [the longest x1 44.2 us: local(): lax.all_gather(own_values.reshape(seq_count, blk_width, HEADS * HEAD), 'b...]
  transfers between devices with their start and end apart: 5 -> 0, of which waited for: 4 -> 0; matrix products, arithmetic and copies ran while one was open for 6% -> 0% of each run, Pallas kernels for 0% -> 0%
where the time goes in v2:
time: 231 us
  Pallas kernels  192 us (83%)
  other arithmetic  20.5 us (9%)
  local copies, waits for them, and re-layouts  17.7 us (8%)
    pallas_call x1, Pallas kernels, layer(): pl.pallas_call(layer_kernel, out_shape=[jax.ShapeDtypeStruct(shape, kind)...  192 us
    unnamed x20, local copies, waits for them, and re-layouts  8.34 us
    convert_element_type x4, other arithmetic, joined(): jnp.concatenate([grad[:, 0:width], grad[:, 512:512 + width]], axis=1)  6.06 us

profile of v2, /device:TPU:1, one launch (start us, length us, event | category | flops | bytes accessed | tf_op | source)
XLA Modules:
  0.0 230.9 jit_solution(9461133741022504751)
XLA Ops:
  0.7 0.1 add_convert_fusion
  0.7 0.9 fusion.1
  1.6 0.6 broadcast_in_dim.31.args_2_
  2.2 1.3 broadcast_in_dim.32.args_5_
  3.5 1.3 broadcast_in_dim.33.args_6_
  4.8 0.3 fusion
  5.1 0.8 pad_maximum_fusion.1.args_4_
  5.8 0.8 pad_maximum_fusion.args_3_
  6.6 1.7 copy.51.args_8_
  8.3 191.8 %shard_map.263 = (bf16[2,64,768]{2,1,0:T(8,128)(2,1)}, f32[2,64,768]{2,1,0:T(8,128)}, bf16[768,2048]{1,0:T(8,128)(2,1)}, bf16[768,2048]{1,0:T(8,128)(2,1)}, bf16...) custom-call(bf16[2,64,768]{2,1,0:T(8,128)(2,1)} %args_0_.4, ...), custom_call_target="tpu_custom_call" | custom-call | tf_op jit(solution)/shard_map/pallas_call | solution.py:806
  200.1 1.1 fusion.4
  201.2 1.4 fusion.7
  202.6 0.1 copy.52
  202.7 0.1 copy.53
  202.9 0.1 maximum_convert_fusion.4
  202.9 1.1 copy.57
  204.1 1.1 fusion.3
  205.1 1.4 fusion.6
  206.5 0.1 copy.54
  206.7 0.1 copy.55
  206.8 0.1 maximum_convert_fusion.5
  206.9 1.1 copy.58
  208.0 0.0 copy-start.3
  208.0 1.3 convert_add_fusion
  209.3 0.3 copy-done.3
  209.7 0.1 fusion.5
  209.7 0.6 slice_bitcast_fusion
  210.4 0.8 copy.56
  211.2 1.4 maximum_convert_fusion.3
  212.5 1.6 maximum_convert_fusion.1
  214.1 0.0 copy-start.4
  214.1 1.6 maximum_convert_fusion
  215.7 0.6 copy-done.4
  216.3 0.1 fusion.2
  216.4 0.0 copy-start.2
  216.4 1.6 maximum_convert_fusion.2
  218.0 1.2 copy-done.2
  219.1 0.0 copy-start.1
  219.1 3.6 %convert_element_type.65 = f32[768,2048]{1,0:T(8,128)} convert(bf16[768,2048]{1,0:T(8,128)(2,1)S(1)} %copy-done.2) | non-fusion elementwise | flops 1572864 | bytes 9437184 | tf_op jit(solution)/shard_map/convert_element_type | solution.py:859
  222.7 0.0 copy-done.1
  222.7 0.0 copy-start
  222.7 3.6 %convert_element_type.66 = f32[768,2048]{1,0:T(8,128)} convert(bf16[768,2048]{1,0:T(8,128)(2,1)S(1)} %copy-done.1) | non-fusion elementwise | flops 1572864 | bytes 9437184 | tf_op jit(solution)/shard_map/convert_element_type | solution.py:860
  226.2 0.0 copy-done
  226.2 3.2 %convert_element_type.67 = f32[2048,768]{1,0:T(8,128)} convert(bf16[2048,768]{1,0:T(8,128)(2,1)S(1)} %copy-done) | non-fusion elementwise | flops 1572864 | bytes 9437184 | tf_op jit(solution)/shard_map/convert_element_type | solution.py:861
  229.4 0.0 copy-done.6
  229.4 0.7 copy.61
  230.1 0.0 copy-done.5
  230.1 0.7 copy.62
  (5 shorter events, 0.0 us)
Async XLA Ops:
  208.0 1.7 copy-start.3
  214.1 2.1 copy-start.4
  216.4 2.7 %copy-start.2 = (bf16[768,2048]{1,0:T(8,128)(2,1)S(1)}, bf16[768,2048]{1,0:T(8,128)(2,1)}, u32[]{:S(2)}) copy-start(bf16[768,2048]{1,0:T(8,128)(2,1)} %get-tuple-element.29) | copy-start | bytes 9437188
  219.1 3.6 %copy-start.1 = (bf16[768,2048]{1,0:T(8,128)(2,1)S(1)}, bf16[768,2048]{1,0:T(8,128)(2,1)}, u32[]{:S(2)}) copy-start(bf16[768,2048]{1,0:T(8,128)(2,1)} %get-tuple-element.30) | copy-start | bytes 9437188
  222.7 3.6 %copy-start = (bf16[2048,768]{1,0:T(8,128)(2,1)S(1)}, bf16[2048,768]{1,0:T(8,128)(2,1)}, u32[]{:S(2)}) copy-start(bf16[2048,768]{1,0:T(8,128)(2,1)} %get-tuple-element.31) | copy-start | bytes 9437188
  226.2 3.2 %copy-start.6 = (bf16[2,64,768]{2,1,0:T(8,128)(2,1)S(1)}, bf16[2,64,768]{2,1,0:T(8,128)(2,1)}, u32[]{:S(2)}) copy-start(bf16[2,64,768]{2,1,0:T(8,128)(2,1)} %get-tuple-element.121) | copy-start | bytes 589828
  226.2 3.9 %copy-start.5 = (f32[2,64,768]{2,1,0:T(8,128)S(1)}, f32[2,64,768]{2,1,0:T(8,128)}, u32[]{:S(2)}) copy-start(f32[2,64,768]{2,1,0:T(8,128)} %get-tuple-element.122) | copy-start | bytes 1179652

commit v3 on v2

--- a/solution.py
+++ b/solution.py
@@ -1,5 +1,6 @@
 import jax
 import jax.numpy as jnp
+import numpy as np
 from jax import lax
 from jax.sharding import PartitionSpec as P
 from jax.experimental import pallas as pl
@@ -57,15 +58,23 @@
 
 
 class Reduction:
-    def __init__(self, place, total, first, second, third, chunk, send, recv, keep, outs, tall):
-        self.place = place
-        self.total, self.first, self.second, self.third, self.chunk = total, first, second, third, chunk
-        self.send, self.recv, self.keep, self.outs, self.tall = send, recv, keep, outs, tall
-        self.n, self.width = total.shape[2], total.shape[4]
+    def __init__(self, r, name, place, outs, tall=None, halving=True):
+        self.place, self.outs, self.halving = place, outs, halving
+        for part in ("total", "first", "second", "third", "chunk", "send", "recv", "keep"):
+            setattr(self, part, getattr(r, name + "_" + part))
+        self.n, self.width = self.total.shape[2], self.total.shape[4]
+        self.tall = tall or (False,) * self.n
 
     def spots(self, o):
         a, b, c = ORDERS[o]
         return self.place[a], self.place[b], self.place[c]
+
+    def sides(self, o, s):
+        me = self.place[ORDERS[o][0]]
+        odd = lax.rem(me, 2)
+        near, far = 1 + 2 * odd, 3 - 2 * odd
+        steps = (near, far) if s == 0 else (far, near)
+        return steps, lax.rem(me + steps[0], 4), lax.rem(me + steps[1], 4), lax.rem(me + 2, 4)
 
     def region(self, o, m, i, row, rows, count=1):
         core, width = self.place[3], self.width
@@ -75,40 +84,54 @@
             return self.outs[m].at[rows_at((core * 4 + i) * 256 + row, rows), pl.ds(o * width, width)]
         return self.outs[m].at[rows_at(o * 256 + row, rows), rows_at((core * 4 + i) * width, count * width, 128)]
 
-    def copies(self, o, stage):
+    def moves(self, o, stage):
         i, j, k = self.spots(o)
+        every = range(self.n)
+        if stage == 8:
+            x, y, z, core = self.place
+            here = [self.region(o, m, 0, 0, 256, 4) for m in every]
+            return [(spot, spot, device(x, y, z, 1 - core)) for spot in here]
         made = []
-        if stage == 6:
-            x, y, z, core = self.place
-            for m in range(self.n):
-                here = self.region(o, m, 0, 0, 256, 4)
-                made.append(
-                    remote(here, here, self.send.at[o, 6, 0, m], self.recv.at[o, 6, 0, m], device(x, y, z, 1 - core))
-                )
+        axis = ORDERS[o][(0, 0, 1, 2, 2, 1, 0, 0)[stage]]
+        if stage in (0, 1, 6, 7) and self.halving:
+            for s in range(2):
+                steps, front, last, across = self.sides(o, s)
+                half = pl.ds(s * 128, 128)
+                peer = on_ring(self.place, axis, steps[0 if stage in (0, 7) else 1])
+                if stage == 0:
+                    made.append((self.total.at[o, front, :, half], self.first.at[o, s, 0], peer))
+                    made.append((self.total.at[o, across, :, half], self.first.at[o, s, 1], peer))
+                elif stage == 1:
+                    made.append((self.total.at[o, last, :, half], self.first.at[o, s, 2], peer))
+                else:
+                    for spot in (i, last) if stage == 7 else (i,):
+                        here = [self.region(o, m, spot, s * 128, 128) for m in every]
+                        made += [(where, where, peer) for where in here]
             return made
-        axis = ORDERS[o][(0, 1, 2, 2, 1, 0)[stage]]
+        if stage in (1, 6):
+            return made
         for step in (1, 2, 3):
             to = lax.rem(self.place[axis] + step, 4)
             peer = on_ring(self.place, axis, step)
-            if stage < 3:
-                if stage == 0:
-                    src, dst = self.total.at[o, to], self.first.at[o, step - 1]
-                elif stage == 1:
-                    src, dst = self.total.at[o, i, :, rows_at(to * 64, 64)], self.second.at[o, step - 1]
-                else:
-                    src, dst = self.total.at[o, i, :, rows_at(j * 64 + to * 16, 16)], self.third.at[o, step - 1]
-                made.append(
-                    remote(src, dst, self.send.at[o, stage, step - 1, 0], self.recv.at[o, stage, step - 1, 0], peer)
-                )
-                continue
-            row, rows = ((j * 64 + k * 16, 16), (j * 64, 64), (0, 256))[stage - 3]
-            for m in range(self.n):
-                here = self.region(o, m, i, row, rows)
-                src = self.chunk.at[o, m] if stage == 3 else here
-                made.append(
-                    remote(src, here, self.send.at[o, stage, step - 1, m], self.recv.at[o, stage, step - 1, m], peer)
-                )
+            at = step - 1
+            if stage == 0:
+                made.append((self.total.at[o, to], self.first.at[o, at], peer))
+            elif stage == 2:
+                made.append((self.total.at[o, i, :, rows_at(to * 64, 64)], self.second.at[o, at], peer))
+            elif stage == 3:
+                made.append((self.total.at[o, i, :, rows_at(j * 64 + to * 16, 16)], self.third.at[o, at], peer))
+            else:
+                row, rows = {4: (j * 64 + k * 16, 16), 5: (j * 64, 64), 7: (0, 256)}[stage]
+                for m in every:
+                    here = self.region(o, m, i, row, rows)
+                    made.append((self.chunk.at[o, m] if stage == 4 else here, here, peer))
         return made
+
+    def copies(self, o, stage):
+        return [
+            remote(src, dst, self.send.at[o, stage, at], self.recv.at[o, stage, at], peer)
+            for at, (src, dst, peer) in enumerate(self.moves(o, stage))
+        ]
 
     def kept(self, o):
         i, j, k = self.spots(o)
@@ -123,7 +146,7 @@
         for o in orders:
             for copy in self.copies(o, stage):
                 copy.start()
-            if stage == 3:
+            if stage == 4:
                 for copy in self.kept(o):
                     copy.start()
 
@@ -131,66 +154,79 @@
         for o in orders:
             for copy in self.copies(o, stage):
                 copy.wait()
-            if stage == 3:
+            if stage == 4:
                 for copy in self.kept(o):
                     copy.wait()
-            if stage < 3:
+            if stage < 4:
                 self.add(o, stage)
 
-    def step(self, stage):
-        for o in range(3):
-            self.finish(stage, (o,))
-            self.start(stage + 1, (o,))
+    def step(self, *stages):
+        for stage in stages:
+            for o in range(3):
+                self.finish(stage, (o,))
+                self.start(stage + 1, (o,))
 
     def add(self, o, stage):
         i, j, k = self.spots(o)
-        rows = (64, 64, 16)[stage]
-        base = (0, j * 64, j * 64 + k * 16)[stage]
-        arrived = (self.first, self.second, self.third)[stage]
-        parts = 4 if stage == 0 else 1
-
-        def body(step, carried):
-            m = lax.div(step, parts)
-            shift = lax.rem(step, parts) * 64
-            here, there = rows_at(base + shift, rows), rows_at(shift, rows)
-            acc = self.total[o, i, m, here, :].astype(F32)
-            for slot in range(3):
-                acc = acc + arrived[o, slot, m, there, :].astype(F32)
-            if stage == 2:
+
+        def body(m, carried):
+            if stage < 2 and self.halving:
+                for s in range(2):
+                    _, _, last, _ = self.sides(o, s)
+                    half = slice(s * 128, s * 128 + 128)
+                    for spot, slot in ((i, 0), (last, 1)) if stage == 0 else ((i, 2),):
+                        acc = self.total[o, spot, m, half, :].astype(F32) + self.first[o, s, slot, m].astype(F32)
+                        self.total[o, spot, m, half, :] = acc.astype(BF)
+            elif stage == 0:
+                for part in range(4):
+                    rows = slice(part * 64, part * 64 + 64)
+                    acc = self.total[o, i, m, rows, :].astype(F32)
+                    for slot in range(3):
+                        acc = acc + self.first[o, slot, m, rows, :].astype(F32)
+                    self.total[o, i, m, rows, :] = acc.astype(BF)
+            elif stage == 2:
+                rows = rows_at(j * 64, 64)
+                acc = self.total[o, i, m, rows, :].astype(F32)
+                for slot in range(3):
+                    acc = acc + self.second[o, slot, m].astype(F32)
+                self.total[o, i, m, rows, :] = acc.astype(BF)
+            elif stage == 3:
+                acc = self.total[o, i, m, rows_at(j * 64 + k * 16, 16), :].astype(F32)
+                for slot in range(3):
+                    acc = acc + self.third[o, slot, m].astype(F32)
                 self.chunk[o, m] = acc.astype(BF)
-            else:
-                self.total[o, i, m, here, :] = acc.astype(BF)
             return carried
 
-        lax.fori_loop(0, self.n * parts, body, 0)
-
-
-def reduction_scratch(name, n, width):
+        lax.fori_loop(0, self.n, body, 0)
+
+
+def reduction_scratch(name, n, width, halving=True):
+    copies = max(4 * n, 3 * n, 4)
     return {
         name + "_total": pltpu.VMEM((3, 4, n, 256, width), BF),
-        name + "_first": pltpu.VMEM((3, 3, n, 256, width), BF),
+        name + "_first": pltpu.VMEM((3, 2, 3, n, 128, width) if halving else (3, 3, n, 256, width), BF),
         name + "_second": pltpu.VMEM((3, 3, n, 64, width), BF),
         name + "_third": pltpu.VMEM((3, 3, n, 16, width), BF),
         name + "_chunk": pltpu.VMEM((3, n, 16, width), BF),
-        name + "_send": pltpu.SemaphoreType.DMA((3, 7, 3, n)),
-        name + "_recv": pltpu.SemaphoreType.DMA((3, 7, 3, n)),
+        name + "_send": pltpu.SemaphoreType.DMA((3, 9, copies)),
+        name + "_recv": pltpu.SemaphoreType.DMA((3, 9, copies)),
         name + "_keep": pltpu.SemaphoreType.DMA((3, n)),
     }
 
 
 WEIGHTS = {
     "w_latent": (768, 512),
-    "w_krope": (768, 64),
+    "w_krope": (64, 768),
     "w_query": (768, 768),
     "w_qrope": (768, 768),
     "w_upkey": (2, 256, 384),
     "w_upval": (2, 256, 384),
     "w_out": (768, 768),
-    "w_gate": (768, 2048),
-    "w_up": (768, 2048),
-    "w_down": (2048, 768),
+    "w_gate": (768, 1024),
+    "w_up": (768, 1024),
+    "w_down": (1024, 768),
 }
-SMALL = ("tokens", "cotangent", "seq_weight", "cosine", "sine", "norm_attn", "norm_mlp")
+SMALL = ("tokens", "cotangent", "norm_attn", "norm_mlp", "group_of_seq", "group_weight")
 OUTS = {
     "layer_out": ((2, 64, 768), BF),
     "grad_tokens": ((2, 64, 768), F32),
@@ -209,6 +245,10 @@
     made = {"v" + name[1:]: vmem(shape, BF) for name, shape in WEIGHTS.items()}
     made.update(
         load_sem=dma((len(WEIGHTS),)),
+        table_sem=dma((2,)),
+        turns=vmem((128, 128), F32),
+        cosine=vmem((128, 128), F32),
+        sine=vmem((128, 128), F32),
         swap_sem=dma((4, 2)),
         pair_sem=dma((12, 2)),
         ag_sem=dma((2, 2, 2, 3, 2)),
@@ -239,10 +279,11 @@
         nmt=vmem((768, 256), BF),
         gb2=vmem((256, 768), BF),
         acts=vmem((3, 256, 1024), BF),
-        other=vmem((3, 128, 1024), BF),
         hidt=vmem((1024, 256), BF),
-        outacc=vmem((128, 768), F32),
-        gnm=vmem((128, 768), F32),
+        outacc=vmem((256, 768), F32),
+        gnm=vmem((256, 768), F32),
+        outx=vmem((128, 768), F32),
+        gnmx=vmem((128, 768), F32),
         outbf=vmem((128, 768), BF),
         gattn=vmem((2, 256, 384), BF),
         gmix=vmem((128, 768), BF),
@@ -268,8 +309,9 @@
         gains=vmem((16, 128), F32),
     )
     made.update(reduction_scratch("wide", 3, 256))
-    made.update(reduction_scratch("early", 3, 128))
-    made.update(reduction_scratch("late", 1, 128))
+    made.update(reduction_scratch("out", 1, 128))
+    made.update(reduction_scratch("early", 2, 128))
+    made.update(reduction_scratch("late", 1, 128, False))
     return made
 
 
@@ -286,7 +328,7 @@
 def layer_kernel(*args):
     r = Refs()
     shapes = scratch()
-    names = list(SMALL) + list(WEIGHTS) + list(OUTS) + list(shapes)
+    names = list(SMALL) + ["table"] + list(WEIGHTS) + list(OUTS) + list(shapes)
     for name, ref in zip(names, args, strict=True):
         setattr(r, name, ref)
     place = coords()
@@ -300,6 +342,9 @@
     low64 = lambda rows: lax.broadcasted_iota(jnp.int32, (rows, 128), 1) < 64
     diagonal = (lax.broadcasted_iota(jnp.int32, (128, 128), 0) < 64) == low64(128)
 
+    def gain_of(ref):
+        return ref[...].reshape(1, 768)
+
     def both(value):
         return jnp.where(diagonal, jnp.concatenate([value, value], axis=0), jnp.zeros((), value.dtype))
 
@@ -308,8 +353,22 @@
 
     loads = {}
     for at, name in enumerate(WEIGHTS):
-        loads[name] = pltpu.make_async_copy(getattr(r, name), getattr(r, "v" + name[1:]), r.load_sem.at[at])
-        loads[name].start()
+        source = getattr(r, name)
+        if name in ("w_gate", "w_up"):
+            source = source.at[:, rows_at(core * 1024, 1024, 128)]
+        elif name == "w_down":
+            source = source.at[rows_at(core * 1024, 1024), :]
+        loads[name] = pltpu.make_async_copy(source, getattr(r, "v" + name[1:]), r.load_sem.at[at])
+    tables = [
+        pltpu.make_async_copy(
+            r.table.at[rows_at(where * 64, 64)], r.turns.at[pl.ds(half * 64, 64)], r.table_sem.at[half]
+        )
+        for half, where in enumerate((blk, 31 - blk))
+    ]
+    loads["w_latent"].start()
+    loads["w_krope"].start()
+    for table in tables:
+        table.start()
     barrier = pltpu.get_barrier_semaphore()
     for peer in peers:
         pl.semaphore_signal(barrier, inc=1, device_id=peer, device_id_type=MESH)
@@ -325,6 +384,8 @@
     swap_c = swap(1, r.cotangent.at[1 - x_hi], r.cbuf.at[pl.ds(64, 64)])
     swap_x.start()
     swap_c.start()
+    for name in ("w_query", "w_qrope", "w_upkey"):
+        loads[name].start()
     r.xbuf[0:64] = r.tokens[x_hi]
     r.cbuf[0:64] = r.cotangent[x_hi]
     key_row = lax.broadcasted_iota(jnp.int32, (256, 384), 0)
@@ -332,6 +393,12 @@
     within = lax.rem(key_row, 64) - query_lane
     r.rel[0] = 128 * lax.div(key_row, 64) + within
     r.rel[1] = within - 128 * lax.div(key_row, 64)
+    for table in tables:
+        table.wait()
+    turns = r.turns[...]
+    other = pltpu.roll(turns, 64, 1)
+    r.cosine[...] = jnp.where(low64(128), turns, other)
+    r.sine[...] = jnp.where(low64(128), other, turns)
     swap_x.wait()
 
     def unit_of(values):
@@ -339,13 +406,13 @@
         return values * inverse, inverse
 
     unit = unit_of(r.xbuf[...].astype(F32))[0]
-    normed = (unit * r.norm_attn[...]).astype(BF)
+    normed = (unit * gain_of(r.norm_attn)).astype(BF)
     r.norm2[0:128] = normed
     send_norm = paired(0, r.norm2.at[pl.ds(0, 128)], r.norm2.at[pl.ds(128, 128)])
     send_norm.start()
     loads["w_latent"].wait()
     loads["w_krope"].wait()
-    key_pre = dot(normed, r.v_krope[...])
+    key_pre = dot_nt(normed, r.v_krope[...])
     r.krd[:, 0:64] = key_pre
     r.krd[:, 64:128] = key_pre
     key_pre = r.krd[...]
@@ -376,6 +443,8 @@
     for part in range(2):
         for copy in gather(part, 0):
             copy.start()
+    for name in ("w_upval", "w_out", "w_gate", "w_up", "w_down"):
+        loads[name].start()
 
     loads["w_query"].wait()
     r.q[...] = dot(normed, r.v_query[...]).astype(BF)
@@ -497,49 +566,66 @@
     middle = r.xbuf[...].astype(F32) + dot(r.ao2[0:128], r.v_out[...])
     r.middle[...] = middle
     unit_mlp = unit_of(middle)[0]
-    r.nm2[0:128] = (unit_mlp * r.norm_mlp[...]).astype(BF)
+    r.nm2[0:128] = (unit_mlp * gain_of(r.norm_mlp)).astype(BF)
     send_nm = paired(2, r.nm2.at[pl.ds(0, 128)], r.nm2.at[pl.ds(128, 128)])
     send_nm.start()
     swap_c.wait()
-    weight = jnp.where(x_hi == 0, r.seq_weight[0:1, 0:1], r.seq_weight[1:2, 0:1])
+    group = jnp.where(x_hi == 0, r.group_of_seq[0], r.group_of_seq[1])
+    weight = r.group_weight[0]
+    for g in range(1, GROUPS):
+        weight = jnp.where(group == g, r.group_weight[g], weight)
     r.gb2[0:128] = (r.cbuf[...].astype(F32) * weight).astype(BF)
     send_gb = paired(3, r.gb2.at[pl.ds(0, 128)], r.gb2.at[pl.ds(128, 128)])
     send_gb.start()
-    r.outacc[...] = middle
+    r.outacc[...] = jnp.zeros_like(r.outacc)
     r.gnm[...] = jnp.zeros_like(r.gnm)
     for name in ("w_gate", "w_up", "w_down"):
         loads[name].wait()
-
-    def feed(half, target):
-        def tile(step, carried):
-            at = rows_at(half * 1024 + step * 256, 256, 256)
-            cols = rows_at(step * 256, 256, 256)
-            act = r.nm2[0:128]
-            gate = dot(act, r.v_gate[:, at])
-            up = dot(act, r.v_up[:, at])
-            sig = jax.nn.sigmoid(gate)
-            silu = gate * sig
-            hidden = (silu * up).astype(BF)
-            grad_hidden = dot_nt(r.gb2[0:128], r.v_down[at, :])
-            grad_gate = (grad_hidden * up * sig * (1.0 + gate * (1.0 - sig))).astype(BF)
-            grad_up = (grad_hidden * silu).astype(BF)
-            target[0, 0:128, cols] = hidden
-            target[1, 0:128, cols] = grad_gate
-            target[2, 0:128, cols] = grad_up
-            r.outacc[...] += dot(hidden, r.v_down[at, :])
-            r.gnm[...] += dot_nt(grad_gate, r.v_gate[:, at]) + dot_nt(grad_up, r.v_up[:, at])
+    send_nm.wait()
+    send_gb.wait()
+
+    def tile(step, carried):
+        at = rows_at(step * 256, 256, 256)
+        act = r.nm2[...]
+        gate = dot(act, r.v_gate[:, at])
+        up = dot(act, r.v_up[:, at])
+        sig = jax.nn.sigmoid(gate)
+        silu = gate * sig
+        hidden = (silu * up).astype(BF)
+        grad_hidden = dot_nt(r.gb2[...], r.v_down[at, :])
+        grad_gate = (grad_hidden * up * sig * (1.0 + gate * (1.0 - sig))).astype(BF)
+        grad_up = (grad_hidden * silu).astype(BF)
+        r.acts[0, :, at] = hidden
+        r.acts[1, :, at] = grad_gate
+        r.acts[2, :, at] = grad_up
+        r.outacc[...] += dot(hidden, r.v_down[at, :])
+        r.gnm[...] += dot_nt(grad_gate, r.v_gate[:, at]) + dot_nt(grad_up, r.v_up[:, at])
+        return carried
+
+    lax.fori_loop(0, 4, tile, 0)
+    send_gnm = paired(4, r.gnm.at[pl.ds(128, 128)], r.gnmx)
+    send_out = paired(10, r.outacc.at[pl.ds(128, 128)], r.outx)
+    send_gnm.start()
+    send_out.start()
+
+    wide = Reduction(r, "wide", place, (r.g_gate, r.g_up, r.g_down), (False, False, True))
+    outer = Reduction(r, "out", place, (r.g_out,))
+    early = Reduction(r, "early", place, (r.g_query, r.g_qrope))
+    late = Reduction(r, "late", place, (r.g_late,), halving=False)
+    r.nmt[...] = r.nm2[...].T
+    r.hidt[...] = r.acts[0].T
+    for o in range(3):
+
+        def wide_tile(i, carried):
+            cols = rows_at(i * 256, 256, 256)
+            left = r.nmt[o * 256 : o * 256 + 256]
+            r.wide_total[o, i, 0] = dot(left, r.acts[1, :, cols]).astype(BF)
+            r.wide_total[o, i, 1] = dot(left, r.acts[2, :, cols]).astype(BF)
+            r.wide_total[o, i, 2] = dot(r.hidt[cols, :], r.gb2[:, o * 256 : o * 256 + 256]).astype(BF)
             return carried
 
-        lax.fori_loop(0, 4, tile, 0)
-
-    feed(1 - core, r.other)
-    send_acts = paired(4, r.other, r.acts.at[:, pl.ds(128, 128)])
-    send_acts.start()
-    feed(core, r.acts)
-    r.outbf[...] = r.outacc[...].astype(BF)
-    r.layer_out[x_hi] = r.outbf[0:64]
-    swap_out = swap(2, r.outbf.at[pl.ds(64, 64)], r.layer_out.at[x_hi])
-    swap_out.start()
+        lax.fori_loop(0, 4, wide_tile, 0)
+        wide.start(0, (o,))
 
     def norm_back(grads, values, gain):
         unit_rows, inverse = unit_of(values)
@@ -548,7 +634,8 @@
         mean = jnp.mean(scaled * unit_rows, axis=-1, keepdims=True)
         return inverse * (scaled - unit_rows * mean), gain_grad
 
-    back, gain_mlp = norm_back(r.gnm[...], r.middle[...], r.norm_mlp[...])
+    send_gnm.wait()
+    back, gain_mlp = norm_back(r.gnm[0:128] + r.gnmx[...], r.middle[...], gain_of(r.norm_mlp))
     r.gmid[...] = r.cbuf[...].astype(F32) * weight + back
     gain_row = lax.broadcasted_iota(jnp.int32, (16, 128), 0)
     gains = jnp.zeros((16, 128), F32)
@@ -563,6 +650,11 @@
     mixed = dot_nt(grad_attn, r.v_out[...])
     r.gmix[...] = mixed.astype(BF)
     to_latent(r.gmix, r.v_upval, r.ga)
+    send_out.wait()
+    r.outbf[...] = (r.middle[...] + r.outacc[0:128] + r.outx[...]).astype(BF)
+    r.layer_out[x_hi] = r.outbf[0:64]
+    swap_out = swap(2, r.outbf.at[pl.ds(64, 64)], r.layer_out.at[x_hi])
+    swap_out.start()
     ones = jnp.ones((8, 128), F32)
     for half in range(2):
         for p in range(6):
@@ -573,41 +665,22 @@
             )
             r.delta[half * 2 + p // 3, :, (p % 3) * 128 : (p % 3) * 128 + 128] = sums
 
-    wide = Reduction(
-        place, r.wide_total, r.wide_first, r.wide_second, r.wide_third, r.wide_chunk, r.wide_send, r.wide_recv,
-        r.wide_keep, (r.g_gate, r.g_up, r.g_down), (False, False, True),
-    )
-    early = Reduction(
-        place, r.early_total, r.early_first, r.early_second, r.early_third, r.early_chunk, r.early_send,
-        r.early_recv, r.early_keep, (r.g_query, r.g_qrope, r.g_out), (False, False, False),
-    )
-    late = Reduction(
-        place, r.late_total, r.late_first, r.late_second, r.late_third, r.late_chunk, r.late_send, r.late_recv,
-        r.late_keep, (r.g_late,), (False,),
-    )
-    for copy in (send_nm, send_gb, send_acts):
-        copy.wait()
-    r.nmt[...] = r.nm2[...].T
-    r.hidt[...] = r.acts[0].T
+    send_ao.wait()
+    send_ga.wait()
+    r.nmt[...] = r.ao2[...].T
     for o in range(3):
-
-        def wide_tile(i, carried):
-            cols = rows_at(i * 256, 256, 256)
-            left = r.nmt[o * 256 : o * 256 + 256]
-            r.wide_total[o, i, 0] = dot(left, r.acts[1, :, cols]).astype(BF)
-            r.wide_total[o, i, 1] = dot(left, r.acts[2, :, cols]).astype(BF)
-            r.wide_total[o, i, 2] = dot(r.hidt[cols, :], r.gb2[:, o * 256 : o * 256 + 256]).astype(BF)
-            return carried
-
-        lax.fori_loop(0, 4, wide_tile, 0)
-        wide.start(0, (o,))
+        block = dot(r.nmt[o * 256 : o * 256 + 256], r.gattn[core]).astype(BF)
+        for i in range(3):
+            r.out_total[o, i, 0] = block[:, i * 128 : i * 128 + 128]
+        r.out_total[o, 3, 0] = jnp.zeros((256, 128), BF)
+    outer.start(0)
 
     r.acc[...] = jnp.zeros_like(r.acc)
     r.dqr[...] = jnp.zeros_like(r.dqr)
     r.dlat[...] = jnp.zeros_like(r.dlat)
     r.dkr[...] = jnp.zeros_like(r.dkr)
 
-    def backward_half(half, carried):
+    def backward_half(half):
         def chunk_step(step, inner):
             far, chunk, allowed = key_chunk(half, step)
             for g in range(2):
@@ -626,9 +699,10 @@
 
         count = chosen(half, own_count) + chosen(half, far_count)
         lax.fori_loop(0, count, chunk_step, 0)
-        return carried
-
-    lax.fori_loop(0, 2, backward_half, 0)
+
+    backward_half(0)
+    wide.step(0)
+    backward_half(1)
 
     def narrow(step, carried):
         j, c = lax.div(step, 4), lax.rem(step, 4)
@@ -662,6 +736,9 @@
     for part in range(2):
         for copy in scatter(part, 0):
             copy.start()
+
+    wide.step(1)
+    outer.step(0)
 
     for half in range(2):
         for p in range(6):
@@ -690,30 +767,26 @@
             r.dup[g, 1, j] = value_sum.astype(BF)
     send_up = paired(8, r.dup.at[1 - core], r.sup)
     send_up.start()
-    wide.step(0)
+    wide.step(2)
     grad_normed = dot_nt(r.gq2[0, 0:128], r.v_query[:, 0:384]) + dot_nt(r.gq2[1, 0:128], r.v_query[:, 384:768])
     grad_normed += dot_nt(r.gqp2[0, 0:128], r.v_qrope[:, 0:384]) + dot_nt(r.gqp2[1, 0:128], r.v_qrope[:, 384:768])
-    r.gnm[...] = grad_normed
+    r.gnm[0:128] = grad_normed
     send_norm.wait()
     r.normt[...] = r.norm2[...].T
-    send_ao.wait()
-    send_ga.wait()
     send_gq.wait()
     send_gqp.wait()
     send_up.wait()
-    r.nmt[...] = r.ao2[...].T
     for o in range(3):
         rows = slice(o * 256, o * 256 + 256)
-        for m, (left, right) in enumerate(((r.normt, r.gq2), (r.normt, r.gqp2), (r.nmt, r.gattn))):
-            block = dot(left[rows], right[core]).astype(BF)
+        for m, right in enumerate((r.gq2, r.gqp2)):
+            block = dot(r.normt[rows], right[core]).astype(BF)
             for i in range(3):
                 r.early_total[o, i, m] = block[:, i * 128 : i * 128 + 128]
-        for m in range(2):
             r.early_total[o, 3, m] = (r.dup[core, m, o].astype(F32) + r.sup[m, o].astype(F32)).astype(BF)
-        r.early_total[o, 3, 2] = jnp.zeros((256, 128), BF)
         early.start(0, (o,))
 
-    wide.step(1)
+    outer.step(1)
+    wide.step(3)
     for copy in scatter(0, 0) + scatter(1, 0):
         copy.wait()
 
@@ -736,7 +809,9 @@
     for part in range(2):
         for copy in scatter(part, 1):
             copy.start()
-    wide.step(2)
+    outer.step(2)
+    wide.step(4)
+    early.step(0)
     for copy in scatter(0, 1) + scatter(1, 1):
         copy.wait()
     grad_latents = []
@@ -757,11 +832,11 @@
     turned = pltpu.roll(rot, 64, 1)
     rot = jnp.concatenate([jnp.where(low64(64), rot, turned), jnp.where(low64(64), turned, rot)], axis=0)
     grad_kpre = (rot * r.cosine[...] - swap_halves(rot) * r.sine[...]).astype(BF)
-    grad_normed = r.gnm[...] + dot_nt(grad_kpre[:, 0:64], r.v_krope[...])
+    grad_normed = r.gnm[0:128] + dot(grad_kpre[:, 0:64], r.v_krope[...])
     for g in range(2):
         grad_normed = grad_normed + dot_nt(grad_latents[g], r.v_latent[:, g * 256 : g * 256 + 256])
-    back, gain_attn = norm_back(grad_normed, r.xbuf[...].astype(F32), r.norm_attn[...])
-    r.outacc[...] = r.gmid[...] + back
+    back, gain_attn = norm_back(grad_normed, r.xbuf[...].astype(F32), gain_of(r.norm_attn))
+    r.outacc[0:128] = r.gmid[...] + back
     r.grad_tokens[x_hi] = r.outacc[0:64]
     swap_grad = swap(3, r.outacc.at[pl.ds(64, 64)], r.grad_tokens.at[x_hi])
     swap_grad.start()
@@ -779,86 +854,123 @@
             r.late_total[o, i, 0] = block[:, i * 128 : i * 128 + 128]
         r.late_total[o, 2, 0] = dot(r.normt[rows, 0:128], grad_kpre).astype(BF)
         late.start(0, (o,))
-    wide.step(3)
-    early.step(0)
-    late.step(0)
-    wide.step(4)
+    wide.step(5)
+    outer.step(3)
     early.step(1)
-    late.step(1)
+    late.step(0, 1)
+    wide.step(6)
+    outer.step(4)
     early.step(2)
     late.step(2)
+    outer.step(5)
     early.step(3)
     late.step(3)
+    outer.step(6)
     early.step(4)
     late.step(4)
-    wide.step(5)
+    wide.step(7)
+    outer.step(7)
     early.step(5)
-    late.step(5)
+    late.step(5, 6)
+    early.step(6)
+    late.step(7)
+    early.step(7)
     swap_out.wait()
     swap_grad.wait()
-    for reduction in (wide, early, late):
-        reduction.finish(6)
+    for reduction in (wide, outer, early, late):
+        reduction.finish(8)
 
 
 def layer(small, weights):
     vmem = pl.BlockSpec(memory_space=pltpu.VMEM)
     hbm = pl.BlockSpec(memory_space=pl.ANY)
+    smem = pl.BlockSpec(memory_space=pltpu.SMEM)
     return pl.pallas_call(
         layer_kernel,
         out_shape=[jax.ShapeDtypeStruct(shape, kind) for shape, kind in OUTS.values()],
-        in_specs=[vmem] * len(small) + [hbm] * len(weights),
+        in_specs=[vmem] * 4 + [smem] * 2 + [hbm] * (1 + len(weights)),
         out_specs=[vmem, vmem] + [hbm] * (len(OUTS) - 2),
         scratch_shapes=list(scratch().values()),
         compiler_params=pltpu.CompilerParams(
             collective_id=1, has_side_effects=True, vmem_limit_bytes=63 * 2**20
         ),
-    )(*small, *weights)
+    )(*small, jnp.asarray(rotary_table()), *weights)
+
+
+def rotary_table():
+    halves = ROPE // 2
+    powers = -(np.arange(halves, dtype=np.float32) * np.float32(2.0) / np.float32(ROPE))
+    freq_list = np.power(np.float32(10000.0), powers, dtype=np.float32)
+    phases = (np.arange(2048, dtype=np.float32)[:, None] * freq_list[None, :]).astype(np.float32)
+    cosine, sine = np.cos(phases), np.sin(phases)
+    return np.concatenate([cosine, cosine, -sine, sine], axis=1).astype(np.float32)
+
+
+CAST_STEPS = 12
+
+
+def cast_kernel(
+    gate, up, down, query, qrope, out, late,
+    o_gate, o_up, o_down, o_query, o_qrope, o_out, o_latent, o_krope, o_upkey, o_upval, o_gains,
+):
+    o_gate[...] = gate[...].astype(F32)
+    o_up[...] = up[...].astype(F32)
+    o_down[...] = down[...].astype(F32)
+    for source, target, width in ((query, o_query, 384), (qrope, o_qrope, 384), (out, o_out, 384), (late, o_latent, 256)):
+        target[:, 0:width] = source[:, 0:width].astype(F32)
+        target[:, width : 2 * width] = source[:, 512 : 512 + width].astype(F32)
+    for source, target in ((query, o_upkey), (qrope, o_upval)):
+        target[0] = source[:, 384:512].astype(F32)
+        target[1] = source[:, 896:1024].astype(F32)
+    o_krope[...] = late[:, 256:320].astype(F32) + late[:, 768:832].astype(F32)
+
+    @pl.when(pl.program_id(0) == 0)
+    def _():
+        o_gains[...] = late[0:16, 384:512].astype(F32) + late[0:16, 896:1024].astype(F32)
+
+
+def cast_sums(sums):
+    rows = lambda width: pl.BlockSpec((64, width), lambda i: (i, 0))
+    tall = pl.BlockSpec((1024, 128), lambda i: (lax.rem(i, 2), lax.div(i, 2)))
+    ups = pl.BlockSpec((2, 64, 128), lambda i: (0, lax.rem(i, 4), lax.div(i, 4)))
+    shapes = (
+        (768, 2048), (768, 2048), (2048, 768), (768, 768), (768, 768), (768, 768), (768, 512), (768, 64),
+        (2, 256, 384), (2, 256, 384), (16, 128),
+    )
+    return pl.pallas_call(
+        cast_kernel,
+        grid=(CAST_STEPS,),
+        out_shape=[jax.ShapeDtypeStruct(shape, F32) for shape in shapes],
+        in_specs=[rows(2048), rows(2048), tall] + [rows(1024)] * 4,
+        out_specs=[rows(2048), rows(2048), tall] + [rows(768)] * 3 + [rows(512), rows(64), ups, ups]
+        + [pl.BlockSpec((16, 128), lambda i: (0, 0))],
+        compiler_params=pltpu.CompilerParams(vmem_limit_bytes=40 * 2**20),
+    )(*sums)
 
 
 def local(
     tokens, cotangent, group_of_seq, group_weight, norm_attn, w_query, w_qrope, w_latent, w_krope, w_upkey, w_upval,
     w_out, norm_mlp, w_gate, w_up, w_down,
 ):
-    blk = lax.axis_index("blk")
-    within = jnp.arange(64, dtype=jnp.int32)
-    positions = jnp.concatenate([blk * 64 + within, (31 - blk) * 64 + within]).astype(F32)
-    halves = ROPE // 2
-    freq_list = 10000.0 ** (-(jnp.arange(halves, dtype=F32) * 2.0 / ROPE))
-    phases = positions[:, None] * freq_list[None, :]
-    cosine, sine = jnp.cos(phases), jnp.sin(phases)
-    cosine = jnp.concatenate([cosine] * 4, axis=1)
-    sine = jnp.concatenate([-sine, sine, -sine, sine], axis=1)
-    matches = group_of_seq[:, None] == jnp.arange(GROUPS, dtype=jnp.int32)[None, :]
-    seq_weight = jnp.sum(jnp.where(matches, group_weight[None, :], 0.0), axis=1)
-    seq_weight = jnp.broadcast_to(seq_weight[:, None], (2, 128))
-    small = (tokens, cotangent, seq_weight, cosine, sine, norm_attn[None, :], norm_mlp[None, :])
-    weights = (w_latent, w_krope, w_query, w_qrope, w_upkey, w_upval, w_out, w_gate, w_up, w_down)
-    layer_out, grad_tokens, g_gate, g_up, g_down, g_query, g_qrope, g_out, g_late = layer(small, weights)
-
-    def joined(grad, width):
-        return jnp.concatenate([grad[:, 0:width], grad[:, 512 : 512 + width]], axis=1).astype(F32)
-
-    def up_part(grad):
-        both = jnp.stack([grad[:, 384:512], grad[:, 896:1024]]).reshape(2, 3, 256, 128)
-        return jnp.transpose(both, (0, 2, 1, 3)).reshape(2, 256, 384).astype(F32)
-
-    extra = g_late[:, 256:512].astype(F32) + g_late[:, 768:1024].astype(F32)
-    gains = extra[0:12, 128:256].reshape(2, 768)
+    small = (tokens, cotangent, norm_attn, norm_mlp, group_of_seq, group_weight)
+    weights = (w_latent, w_krope.T, w_query, w_qrope, w_upkey, w_upval, w_out, w_gate, w_up, w_down)
+    layer_out, grad_tokens, *sums = layer(small, weights)
+    gate, up, down, query, qrope, out, latent, krope, upkey, upval, gains = cast_sums(sums)
     return (
         layer_out,
         grad_tokens,
-        gains[0],
-        joined(g_query, 384),
-        joined(g_qrope, 384),
-        joined(g_late, 256),
-        extra[:, 0:64],
-        up_part(g_query),
-        up_part(g_qrope),
-        joined(g_out, 384),
-        gains[1],
-        g_gate.astype(F32),
-        g_up.astype(F32),
-        g_down.astype(F32),
+        gains[0:6].reshape(768),
+        query,
+        qrope,
+        latent,
+        krope,
+        upkey,
+        upval,
+        out,
+        gains[6:12].reshape(768),
+        gate,
+        up,
+        down,
     )
 
 

time: 231 us -> 215 us (0.931)
  other arithmetic: 20.5 us -> 0 us
  Pallas kernels: 192 us -> 202 us
  local copies, waits for them, and re-layouts: 17.7 us -> 12.3 us
    convert_element_type x10 -> x0, other arithmetic: 16.5 us -> none  [the longest x4 6.06 us: joined(): jnp.concatenate([grad[:, 0:width], grad[:, 512:512 + width]], axis=1)]
    pallas_call x0 -> x1, Pallas kernels: none -> 12.1 us  [cast_sums(): pl.pallas_call(cast_kernel, grid=(CAST_STEPS,), out_shape=[jax.ShapeDtype...]
    slice x7 -> x0, local copies, waits for them, and re-layouts: 5.05 us -> none  [the longest x4 2.91 us: joined(): grad[:, 0:width]]
    unnamed x20 -> x19, local copies, waits for them, and re-layouts: 8.34 us -> 11.7 us
    broadcast_in_dim x3 -> x0, local copies, waits for them, and re-layouts: 3.17 us -> none  [the longest x1 1.27 us: local(): norm_attn[None, :]]
    pallas_call x1, Pallas kernels: 192 us -> 189 us  [layer(): pl.pallas_call(layer_kernel, out_shape=[jax.ShapeDtypeStruct(shape, kind)...]
where the time goes in v3:
time: 215 us; the launch traced here: 214 us
  Pallas kernels  202 us (94%)
  local copies, waits for them, and re-layouts  12.3 us (6%)
    pallas_call x1, Pallas kernels, layer(): pl.pallas_call(layer_kernel, out_shape=[jax.ShapeDtypeStruct(shape, kind)...  189 us
    pallas_call x1, Pallas kernels, cast_sums(): pl.pallas_call(cast_kernel, grid=(CAST_STEPS,), out_shape=[jax.ShapeDtype...  12.1 us
    unnamed x19, local copies, waits for them, and re-layouts  11.7 us

profile of v3, /device:TPU:1, one launch (start us, length us, event | category | flops | bytes accessed | tf_op | source)
XLA Modules:
  0.0 214.5 jit_solution(6577744696618375456)
XLA Ops:
  0.7 189.4 %shard_map.272 = (bf16[2,64,768]{2,1,0:T(8,128)(2,1)}, f32[2,64,768]{2,1,0:T(8,128)}, bf16[768,2048]{1,0:T(8,128)(2,1)}, bf16[768,2048]{1,0:T(8,128)(2,1)}, bf16...) custom-call(bf16[2,64,768]{2,1,0:T(8,128)(2,1)} %args_0_.4, ...), custom_call_target="tpu_custom_call" | custom-call | tf_op jit(solution)/shard_map/pallas_call | solution.py:888
  190.1 0.0 copy-start
  190.1 1.9 copy-done
  192.0 0.0 copy-start.1
  192.0 1.9 copy-done.1
  193.9 0.0 copy-start.2
  193.9 1.4 copy-done.2
  195.3 0.0 copy-start.3
  195.3 1.4 copy-done.3
  196.7 0.0 copy-start.4
  196.7 1.4 copy-done.4
  198.1 0.0 copy-start.5
  198.1 1.4 copy-done.5
  199.5 0.0 copy-start.7
  199.5 0.0 copy-start.6
  199.5 12.1 %shard_map.273 = (f32[768,2048]{1,0:T(8,128)}, f32[768,2048]{1,0:T(8,128)}, f32[2048,768]{1,0:T(8,128)}, f32[768,768]{1,0:T(8,128)}, f32[768,768]{1,0:T(8,128)},...) custom-call(bf16[768,2048]{1,0:T(8,128)(2,1)S(1)} %copy-done, ...), custom_call_target="tpu_custom_call" | custom-call | tf_op jit(solution)/shard_map/pallas_call | solution.py:940
  211.6 0.6 slice_bitcast_fusion
  212.2 0.8 copy.31
  213.1 0.0 copy-done.7
  213.1 0.7 copy.34
  213.7 0.0 copy-done.6
  213.7 0.7 copy.35
Async XLA Ops:
  190.1 1.9 copy-start
  192.0 1.9 copy-start.1
  193.9 1.4 copy-start.2
  195.3 1.4 copy-start.3
  196.7 1.4 copy-start.4
  198.1 1.4 copy-start.5
  199.5 13.6 %copy-start.7 = (bf16[2,64,768]{2,1,0:T(8,128)(2,1)S(1)}, bf16[2,64,768]{2,1,0:T(8,128)(2,1)}, u32[]{:S(2)}) copy-start(bf16[2,64,768]{2,1,0:T(8,128)(2,1)} %get-tuple-element.84) | copy-start | bytes 589828
  199.5 14.3 %copy-start.6 = (f32[2,64,768]{2,1,0:T(8,128)S(1)}, f32[2,64,768]{2,1,0:T(8,128)}, u32[]{:S(2)}) copy-start(f32[2,64,768]{2,1,0:T(8,128)} %get-tuple-element.85) | copy-start | bytes 1179652

commit v4 on v3

--- a/solution.py
+++ b/solution.py
@@ -16,6 +16,7 @@
 LOG2E = 1.4426950408889634
 HIDDEN_SCORE = -1e30
 ORDERS = ((0, 1, 2), (1, 2, 0), (2, 0, 1))
+X_FIRST = ((0, 1, 2), (0, 2, 1), (0, 1, 2))
 
 
 def coords():
@@ -58,41 +59,37 @@
 
 
 class Reduction:
-    def __init__(self, r, name, place, outs, tall=None, halving=True):
-        self.place, self.outs, self.halving = place, outs, halving
+    def __init__(self, r, name, place, out, halving, flat=False, orders=ORDERS):
+        self.place, self.out, self.halving, self.flat, self.orders = place, out, halving, flat, orders
         for part in ("total", "first", "second", "third", "chunk", "send", "recv", "keep"):
             setattr(self, part, getattr(r, name + "_" + part))
         self.n, self.width = self.total.shape[2], self.total.shape[4]
-        self.tall = tall or (False,) * self.n
+        counts = stage_counts(halving, flat)
+        self.base = [sum(counts[:stage]) for stage in range(9)]
 
     def spots(self, o):
-        a, b, c = ORDERS[o]
+        a, b, c = self.orders[o]
         return self.place[a], self.place[b], self.place[c]
 
     def sides(self, o, s):
-        me = self.place[ORDERS[o][0]]
+        me = self.place[self.orders[o][0]]
         odd = lax.rem(me, 2)
         near, far = 1 + 2 * odd, 3 - 2 * odd
         steps = (near, far) if s == 0 else (far, near)
         return steps, lax.rem(me + steps[0], 4), lax.rem(me + steps[1], 4), lax.rem(me + 2, 4)
 
-    def region(self, o, m, i, row, rows, count=1):
+    def region(self, o, i, row, rows, count=1):
         core, width = self.place[3], self.width
-        if self.tall[m]:
-            if count == 4:
-                return self.outs[m].at[rows_at(core * 4 * 256, 1024), pl.ds(o * width, width)]
-            return self.outs[m].at[rows_at((core * 4 + i) * 256 + row, rows), pl.ds(o * width, width)]
-        return self.outs[m].at[rows_at(o * 256 + row, rows), rows_at((core * 4 + i) * width, count * width, 128)]
+        return self.out.at[:, rows_at(o * 256 + row, rows), rows_at((core * 4 + i) * width, count * width, 128)]
 
     def moves(self, o, stage):
         i, j, k = self.spots(o)
-        every = range(self.n)
         if stage == 8:
             x, y, z, core = self.place
-            here = [self.region(o, m, 0, 0, 256, 4) for m in every]
-            return [(spot, spot, device(x, y, z, 1 - core)) for spot in here]
+            here = self.region(o, 0, 0, 256, 4)
+            return [(here, here, device(x, y, z, 1 - core))]
         made = []
-        axis = ORDERS[o][(0, 0, 1, 2, 2, 1, 0, 0)[stage]]
+        axis = self.orders[o][(0, 0, 1, 2, 2, 1, 0, 0)[stage]]
         if stage in (0, 1, 6, 7) and self.halving:
             for s in range(2):
                 steps, front, last, across = self.sides(o, s)
@@ -105,10 +102,10 @@
                     made.append((self.total.at[o, last, :, half], self.first.at[o, s, 2], peer))
                 else:
                     for spot in (i, last) if stage == 7 else (i,):
-                        here = [self.region(o, m, spot, s * 128, 128) for m in every]
-                        made += [(where, where, peer) for where in here]
+                        here = self.region(o, spot, s * 128, 128)
+                        made.append((here, here, peer))
             return made
-        if stage in (1, 6):
+        if stage in (1, 6) or (stage == 4 and self.flat):
             return made
         for step in (1, 2, 3):
             to = lax.rem(self.place[axis] + step, 4)
@@ -118,45 +115,44 @@
                 made.append((self.total.at[o, to], self.first.at[o, at], peer))
             elif stage == 2:
                 made.append((self.total.at[o, i, :, rows_at(to * 64, 64)], self.second.at[o, at], peer))
+            elif stage == 3 and self.flat:
+                made.append((self.total.at[o, i, :, rows_at(j * 64, 64)], self.third.at[o, k], peer))
             elif stage == 3:
                 made.append((self.total.at[o, i, :, rows_at(j * 64 + to * 16, 16)], self.third.at[o, at], peer))
+            elif stage == 4:
+                made.append((self.chunk.at[o], self.region(o, i, j * 64 + k * 16, 16), peer))
+            elif stage == 5:
+                here = self.region(o, i, j * 64, 64)
+                made.append((self.chunk.at[o] if self.flat else here, here, peer))
             else:
-                row, rows = {4: (j * 64 + k * 16, 16), 5: (j * 64, 64), 7: (0, 256)}[stage]
-                for m in every:
-                    here = self.region(o, m, i, row, rows)
-                    made.append((self.chunk.at[o, m] if stage == 4 else here, here, peer))
+                here = self.region(o, i, 0, 256)
+                made.append((here, here, peer))
         return made
 
     def copies(self, o, stage):
         return [
-            remote(src, dst, self.send.at[o, stage, at], self.recv.at[o, stage, at], peer)
+            remote(src, dst, self.send.at[o, at], self.recv.at[o, self.base[stage] + at], peer)
             for at, (src, dst, peer) in enumerate(self.moves(o, stage))
         ]
 
     def kept(self, o):
         i, j, k = self.spots(o)
-        return [
-            pltpu.make_async_copy(
-                self.chunk.at[o, m], self.region(o, m, i, j * 64 + k * 16, 16), self.keep.at[o, m]
-            )
-            for m in range(self.n)
-        ]
+        row, rows = (j * 64, 64) if self.flat else (j * 64 + k * 16, 16)
+        return pltpu.make_async_copy(self.chunk.at[o], self.region(o, i, row, rows), self.keep.at[o])
 
     def start(self, stage, orders=(0, 1, 2)):
         for o in orders:
             for copy in self.copies(o, stage):
                 copy.start()
             if stage == 4:
-                for copy in self.kept(o):
-                    copy.start()
+                self.kept(o).start()
 
     def finish(self, stage, orders=(0, 1, 2)):
         for o in orders:
             for copy in self.copies(o, stage):
                 copy.wait()
             if stage == 4:
-                for copy in self.kept(o):
-                    copy.wait()
+                self.kept(o).wait()
             if stage < 4:
                 self.add(o, stage)
 
@@ -168,6 +164,8 @@
 
     def add(self, o, stage):
         i, j, k = self.spots(o)
+        if stage == 1 and not self.halving:
+            return
 
         def body(m, carried):
             if stage < 2 and self.halving:
@@ -190,7 +188,13 @@
                 for slot in range(3):
                     acc = acc + self.second[o, slot, m].astype(F32)
                 self.total[o, i, m, rows, :] = acc.astype(BF)
-            elif stage == 3:
+            elif self.flat:
+                self.third[o, k, m] = self.total[o, i, m, rows_at(j * 64, 64), :]
+                acc = self.third[o, 0, m].astype(F32)
+                for slot in range(1, 4):
+                    acc = acc + self.third[o, slot, m].astype(F32)
+                self.chunk[o, m] = acc.astype(BF)
+            else:
                 acc = self.total[o, i, m, rows_at(j * 64 + k * 16, 16), :].astype(F32)
                 for slot in range(3):
                     acc = acc + self.third[o, slot, m].astype(F32)
@@ -200,17 +204,20 @@
         lax.fori_loop(0, self.n, body, 0)
 
 
-def reduction_scratch(name, n, width, halving=True):
-    copies = max(4 * n, 3 * n, 4)
+def stage_counts(halving, flat):
+    return (4 if halving else 3, 2 if halving else 0, 3, 3, 0 if flat else 3, 3, 2 if halving else 0, 4 if halving else 3, 1)
+
+
+def reduction_scratch(name, n, width, halving, flat=False):
     return {
         name + "_total": pltpu.VMEM((3, 4, n, 256, width), BF),
         name + "_first": pltpu.VMEM((3, 2, 3, n, 128, width) if halving else (3, 3, n, 256, width), BF),
         name + "_second": pltpu.VMEM((3, 3, n, 64, width), BF),
-        name + "_third": pltpu.VMEM((3, 3, n, 16, width), BF),
-        name + "_chunk": pltpu.VMEM((3, n, 16, width), BF),
-        name + "_send": pltpu.SemaphoreType.DMA((3, 9, copies)),
-        name + "_recv": pltpu.SemaphoreType.DMA((3, 9, copies)),
-        name + "_keep": pltpu.SemaphoreType.DMA((3, n)),
+        name + "_third": pltpu.VMEM((3, 4, n, 64, width) if flat else (3, 3, n, 16, width), BF),
+        name + "_chunk": pltpu.VMEM((3, n, 64 if flat else 16, width), BF),
+        name + "_send": pltpu.SemaphoreType.DMA((3, 4)),
+        name + "_recv": pltpu.SemaphoreType.DMA((3, sum(stage_counts(halving, flat)))),
+        name + "_keep": pltpu.SemaphoreType.DMA((3,)),
     }
 
 
@@ -230,13 +237,10 @@
 OUTS = {
     "layer_out": ((2, 64, 768), BF),
     "grad_tokens": ((2, 64, 768), F32),
-    "g_gate": ((768, 2048), BF),
-    "g_up": ((768, 2048), BF),
-    "g_down": ((2048, 768), BF),
-    "g_query": ((768, 1024), BF),
-    "g_qrope": ((768, 1024), BF),
-    "g_out": ((768, 1024), BF),
-    "g_late": ((768, 1024), BF),
+    "g_wide": ((3, 768, 2048), BF),
+    "g_out": ((1, 768, 1024), BF),
+    "g_early": ((2, 768, 1024), BF),
+    "g_late": ((1, 768, 1024), BF),
 }
 
 
@@ -251,8 +255,8 @@
         sine=vmem((128, 128), F32),
         swap_sem=dma((4, 2)),
         pair_sem=dma((12, 2)),
-        ag_sem=dma((2, 2, 2, 3, 2)),
-        rs_sem=dma((2, 2, 2, 3, 2)),
+        lat_send=dma((2, 2, 3)),
+        lat_recv=dma((2, 2, 2, 2, 3)),
         xbuf=vmem((128, 768), BF),
         cbuf=vmem((128, 768), BF),
         norm2=vmem((256, 768), BF),
@@ -308,10 +312,10 @@
         gmid=vmem((128, 768), F32),
         gains=vmem((16, 128), F32),
     )
-    made.update(reduction_scratch("wide", 3, 256))
-    made.update(reduction_scratch("out", 1, 128))
-    made.update(reduction_scratch("early", 2, 128))
-    made.update(reduction_scratch("late", 1, 128, False))
+    made.update(reduction_scratch("wide", 3, 256, True))
+    made.update(reduction_scratch("out", 1, 128, False))
+    made.update(reduction_scratch("early", 2, 128, False, True))
+    made.update(reduction_scratch("late", 1, 128, False, True))
     return made
 
 
@@ -436,8 +440,8 @@
             else:
                 pieces = [r.lat.at[two, :, z], None]
             for at, piece in enumerate(pieces if part == 0 else pieces[:1]):
-                sem = r.ag_sem.at[part, phase, at, step - 1]
-                made.append(remote(piece, piece, sem.at[0], sem.at[1], peer))
+                send = r.lat_send.at[part, at, step - 1]
+                made.append(remote(piece, piece, send, r.lat_recv.at[0, part, phase, at, step - 1], peer))
         return made
 
     for part in range(2):
@@ -477,77 +481,78 @@
                 r.qrx[(0,) + here] = jnp.where(low64(64), front, 0.0).astype(BF)
                 r.qrx[(1,) + here] = jnp.where(low64(64), 0.0, back).astype(BF)
 
-    for part in range(2):
+    for part in (1, 0):
         for copy in gather(part, 0):
             copy.wait()
         for copy in gather(part, 1):
             copy.start()
-    for part in range(2):
-        for copy in gather(part, 1):
-            copy.wait()
-
-    def transpose_latents(step, carried):
-        j, c = lax.div(step, 4), lax.rem(step, 4)
-        r.latt[j, c] = r.lat[j, c].reshape(256, 256).T.reshape(4, 64, 256)
-        return carried
-
-    lax.fori_loop(0, 16, transpose_latents, 0)
+
+    def transpose_latents():
+        def body(step, carried):
+            j, c = lax.div(step, 4), lax.rem(step, 4)
+            r.latt[j, c] = r.lat[j, c].reshape(256, 256).T.reshape(4, 64, 256)
+            return carried
+
+        lax.fori_loop(0, 16, body, 0)
+
+    query_blk = (blk, 31 - blk)
+
+    counts = (y + 1, 4 - y)
+
+    def masks(half, step):
+        first = query_blk[half] * 64
+        near = r.rel[0] <= first - 512 * step - 64 * x_hi
+        far = r.rel[1] <= first - 1984 + 512 * (3 - step) + 64 * x_hi
+        return (step, near), (3 - step, far)
+
+    def raw_scores(at, far, chunk, g):
+        keys = r.lat[far * 2 + g, chunk].reshape(256, 256)
+        rot = r.kr[chunk].reshape(256, 128)
+        return dot_nt(keys, r.qs[at]) + dot_nt(rot, r.qrx[far, at]), keys
+
+    r.acc[...] = jnp.zeros_like(r.acc)
+    for copy in gather(1, 1) + gather(0, 1):
+        copy.wait()
     top = lax.broadcasted_iota(jnp.int32, (128, 256), 0) < 64
     for c in range(4):
         turned = r.kr[c].reshape(256, 128).astype(F32).T
         r.krt[0, c] = jnp.where(top, turned, 0.0).astype(BF)
         r.krt[1, c] = jnp.where(top, 0.0, turned).astype(BF)
-
-    own_count = (y + 1, lax.div(16 - x_hi - slot + 3, 4))
-    far_count = (lax.div(slot + x_hi + 3, 4), 4 - y)
-    query_blk = (blk, 31 - blk)
-
-    def chosen(half, pair):
-        return jnp.where(half == 0, pair[0], pair[1])
-
-    def key_chunk(half, step):
-        near = chosen(half, own_count)
-        far = (step >= near).astype(jnp.int32)
-        chunk = jnp.where(step < near, step, 4 - chosen(half, far_count) + step - near)
-        first = chosen(half, query_blk) * 64
-        edge = jnp.where(far == 0, first - 512 * chunk - 64 * x_hi, first - 1984 + 512 * chunk + 64 * x_hi)
-        return far, chunk, r.rel[far] <= edge
-
-    def raw_scores(at, far, chunk, g):
-        keys = r.lat[far * 2 + g, chunk].reshape(256, 256)
-        rot = r.kr[chunk].reshape(256, 128)
-        return dot_nt(keys, r.qs[at]) + dot_nt(rot, r.qrx[far, at]), keys
-
-    r.acc[...] = jnp.zeros_like(r.acc)
-
-    def forward_half(half, carried):
+    transpose_latents()
+
+    def forward(half):
         def chunk_step(step, state):
-            far, chunk, allowed = key_chunk(half, step)
+            places = masks(half, step)
             result = []
             for g in range(2):
                 at = half * 2 + g
                 high, total = state[g]
-                raw = raw_scores(at, far, chunk, g)[0]
-                raw = jnp.where(allowed, raw, HIDDEN_SCORE)
-                new_high = jnp.maximum(high, jnp.max(raw, axis=0, keepdims=True))
+                raws = [
+                    jnp.where(allowed, raw_scores(at, far, chunk, g)[0], HIDDEN_SCORE)
+                    for far, (chunk, allowed) in enumerate(places)
+                ]
+                new_high = jnp.maximum(high, jnp.max(jnp.maximum(*raws), axis=0, keepdims=True))
                 shrink = jnp.exp2((high - new_high) * (FACTOR * LOG2E))
-                weights = jnp.exp2((raw - new_high) * (FACTOR * LOG2E))
-                total = total * shrink + jnp.sum(weights, axis=0, keepdims=True)
-                r.acc[at] = r.acc[at] * shrink + dot(r.latt[far * 2 + g, chunk].reshape(256, 256), weights.astype(BF))
+                weights = [jnp.exp2((raw - new_high) * (FACTOR * LOG2E)) for raw in raws]
+                total = total * shrink + jnp.sum(weights[0] + weights[1], axis=0, keepdims=True)
+                mixed = r.acc[at] * shrink
+                for far, (chunk, _) in enumerate(places):
+                    value = r.latt[far * 2 + g, chunk].reshape(256, 256)
+                    mixed = mixed + dot(value, weights[far].astype(BF))
+                r.acc[at] = mixed
                 result.append((new_high, total))
             return tuple(result)
 
         empty = (jnp.full((1, 384), HIDDEN_SCORE, F32), jnp.zeros((1, 384), F32))
-        count = chosen(half, own_count) + chosen(half, far_count)
-        state = lax.fori_loop(0, count, chunk_step, (empty, empty))
+        state = lax.fori_loop(0, counts[half], chunk_step, (empty, empty))
         for g in range(2):
             high, total = state[g]
             at = half * 2 + g
             r.ctx[at] = (r.acc[at] * (1.0 / total)).astype(BF)
-            r.logs[at] = jnp.broadcast_to(high * (FACTOR * LOG2E) + jnp.log2(total), (8, 384))
-        return carried
-
-    lax.fori_loop(0, 2, forward_half, 0)
+            r.logs[at, 0:1] = high * (FACTOR * LOG2E) + jnp.log2(total)
+
+    forward(0)
+    forward(1)
     loads["w_upval"].wait()
 
     def from_latent(source, weights, half, p):
@@ -608,10 +613,10 @@
     send_gnm.start()
     send_out.start()
 
-    wide = Reduction(r, "wide", place, (r.g_gate, r.g_up, r.g_down), (False, False, True))
-    outer = Reduction(r, "out", place, (r.g_out,))
-    early = Reduction(r, "early", place, (r.g_query, r.g_qrope))
-    late = Reduction(r, "late", place, (r.g_late,), halving=False)
+    wide = Reduction(r, "wide", place, r.g_wide, True)
+    outer = Reduction(r, "out", place, r.g_out, False)
+    early = Reduction(r, "early", place, r.g_early, False, True)
+    late = Reduction(r, "late", place, r.g_late, False, True)
     r.nmt[...] = r.nm2[...].T
     r.hidt[...] = r.acts[0].T
     for o in range(3):
@@ -680,38 +685,32 @@
     r.dlat[...] = jnp.zeros_like(r.dlat)
     r.dkr[...] = jnp.zeros_like(r.dkr)
 
-    def backward_half(half):
-        def chunk_step(step, inner):
-            far, chunk, allowed = key_chunk(half, step)
+    def backward(half):
+        def chunk_step(step, carried):
+            places = masks(half, step)
             for g in range(2):
                 at = half * 2 + g
-                raw, keys = raw_scores(at, far, chunk, g)
-                weights = jnp.exp2(raw * (FACTOR * LOG2E) - r.logs[at, 0:1])
-                weights = jnp.where(allowed, weights, 0.0)
-                dprob = dot_nt(keys, r.ga[at])
-                dscore = (weights * (dprob - r.delta[at, 0:1])).astype(BF)
-                weights = weights.astype(BF)
-                r.acc[at] += dot(r.latt[far * 2 + g, chunk].reshape(256, 256), dscore)
-                r.dqr[at] += dot(r.krt[far, chunk], dscore)
-                r.dlat[far * 2 + g, chunk] += FACTOR * dot(dscore, r.qs[at]) + dot(weights, r.ga[at])
-                r.dkr[chunk] += FACTOR * dot(dscore, r.qrx[far, at])
-            return inner
-
-        count = chosen(half, own_count) + chosen(half, far_count)
-        lax.fori_loop(0, count, chunk_step, 0)
-
-    backward_half(0)
-    wide.step(0)
-    backward_half(1)
+                mixed, turned = r.acc[at], r.dqr[at]
+                for far, (chunk, allowed) in enumerate(places):
+                    raw, keys = raw_scores(at, far, chunk, g)
+                    weights = jnp.exp2(raw * (FACTOR * LOG2E) - r.logs[at, 0:1])
+                    weights = jnp.where(allowed, weights, 0.0)
+                    dprob = dot_nt(keys, r.ga[at])
+                    dscore = (weights * (dprob - r.delta[at, 0:1])).astype(BF)
+                    weights = weights.astype(BF)
+                    mixed = mixed + dot(r.latt[far * 2 + g, chunk].reshape(256, 256), dscore)
+                    turned = turned + dot(r.krt[far, chunk], dscore)
+                    r.dlat[far * 2 + g, chunk] += FACTOR * dot(dscore, r.qs[at]) + dot(weights, r.ga[at])
+                    r.dkr[chunk] += FACTOR * dot(dscore, r.qrx[far, at])
+                r.acc[at], r.dqr[at] = mixed, turned
+            return carried
+
+        lax.fori_loop(0, counts[half], chunk_step, 0)
 
     def narrow(step, carried):
         j, c = lax.div(step, 4), lax.rem(step, 4)
         r.latt[j, c] = r.dlat[j, c].astype(BF).reshape(4, 64, 256)
         return carried
-
-    lax.fori_loop(0, 16, narrow, 0)
-    for c in range(4):
-        r.skr[c] = r.dkr[c].astype(BF).reshape(4, 64, 128)
 
     def scatter(part, phase):
         made = []
@@ -729,16 +728,20 @@
             else:
                 pieces = [(r.st1.at[:, to], r.rt2.at[at])]
             for k, (src, dst) in enumerate(pieces):
-                sem = r.rs_sem.at[part, phase, k, at]
-                made.append(remote(src, dst, sem.at[0], sem.at[1], peer))
+                send = r.lat_send.at[part, k, at]
+                made.append(remote(src, dst, send, r.lat_recv.at[1, part, phase, k, at], peer))
         return made
 
-    for part in range(2):
-        for copy in scatter(part, 0):
-            copy.start()
-
+    backward(0)
+    wide.step(0)
+    backward(1)
+    lax.fori_loop(0, 16, narrow, 0)
+    for c in range(4):
+        r.skr[c] = r.dkr[c].astype(BF).reshape(4, 64, 128)
+    for copy in scatter(1, 0) + scatter(0, 0):
+        copy.start()
     wide.step(1)
-    outer.step(0)
+    outer.step(0, 1)
 
     for half in range(2):
         for p in range(6):
@@ -767,7 +770,6 @@
             r.dup[g, 1, j] = value_sum.astype(BF)
     send_up = paired(8, r.dup.at[1 - core], r.sup)
     send_up.start()
-    wide.step(2)
     grad_normed = dot_nt(r.gq2[0, 0:128], r.v_query[:, 0:384]) + dot_nt(r.gq2[1, 0:128], r.v_query[:, 384:768])
     grad_normed += dot_nt(r.gqp2[0, 0:128], r.v_qrope[:, 0:384]) + dot_nt(r.gqp2[1, 0:128], r.v_qrope[:, 384:768])
     r.gnm[0:128] = grad_normed
@@ -785,19 +787,22 @@
             r.early_total[o, 3, m] = (r.dup[core, m, o].astype(F32) + r.sup[m, o].astype(F32)).astype(BF)
         early.start(0, (o,))
 
-    outer.step(1)
-    wide.step(3)
-    for copy in scatter(0, 0) + scatter(1, 0):
-        copy.wait()
-
-    def fold(at, carried):
+    outer.step(2)
+    wide.step(2, 3)
+
+    def fold_near(at, carried):
         for g in range(2):
             near = r.dlat[g, y, rows_at(at * 64, 64), :]
+            for k in range(3):
+                near = near + r.ro1[k, g, at].astype(F32)
+            r.so1[g, at] = near.astype(BF)
+        return carried
+
+    def fold_far(at, carried):
+        for g in range(2):
             far = r.dlat[2 + g, at, rows_at(z * 64, 64), :]
             for k in range(3):
-                near = near + r.ro1[k, g, at].astype(F32)
                 far = far + r.rt1[k, g, at].astype(F32)
-            r.so1[g, at] = near.astype(BF)
             r.st1[g, at] = far.astype(BF)
         rot = r.dkr[y, rows_at(at * 64, 64), :]
         for k in range(3):
@@ -805,13 +810,19 @@
         r.ks1[at] = rot.astype(BF)
         return carried
 
-    lax.fori_loop(0, 4, fold, 0)
-    for part in range(2):
-        for copy in scatter(part, 1):
-            copy.start()
-    outer.step(2)
+    for copy in scatter(0, 0)[0::2]:
+        copy.wait()
+    lax.fori_loop(0, 4, fold_near, 0)
+    for copy in scatter(0, 1)[0::2]:
+        copy.start()
+    outer.step(3)
+    for copy in scatter(1, 0) + scatter(0, 0)[1::2]:
+        copy.wait()
+    lax.fori_loop(0, 4, fold_far, 0)
+    for copy in scatter(1, 1) + scatter(0, 1)[1::2]:
+        copy.start()
     wide.step(4)
-    early.step(0)
+    early.step(0, 1)
     for copy in scatter(0, 1) + scatter(1, 1):
         copy.wait()
     grad_latents = []
@@ -846,35 +857,33 @@
     for o in range(3):
         r.late_total[o, 3, 0] = jnp.zeros((256, 128), BF)
     r.late_total[0, 3, 0, 0:16] = gains.astype(BF)
+    grad_krope = dot_tn(grad_kpre, r.norm2[0:128]).astype(BF)
     send_gl.wait()
     for o in range(3):
         rows = slice(o * 256, o * 256 + 256)
         block = dot(r.normt[rows], r.gl2[core]).astype(BF)
         for i in range(2):
             r.late_total[o, i, 0] = block[:, i * 128 : i * 128 + 128]
-        r.late_total[o, 2, 0] = dot(r.normt[rows, 0:128], grad_kpre).astype(BF)
+        for part in range(2):
+            at = o * 256 + part * 128
+            r.late_total[o, 2, 0, part * 64 : part * 64 + 64] = grad_krope[0:64, at : at + 128]
+        r.late_total[o, 2, 0, 128:256] = jnp.zeros((128, 128), BF)
         late.start(0, (o,))
     wide.step(5)
-    outer.step(3)
-    early.step(1)
+    early.step(2)
     late.step(0, 1)
+    outer.step(4)
     wide.step(6)
-    outer.step(4)
-    early.step(2)
+    early.step(3, 4)
     late.step(2)
-    outer.step(5)
-    early.step(3)
-    late.step(3)
-    outer.step(6)
-    early.step(4)
-    late.step(4)
+    early.step(5, 6)
+    late.step(3, 4)
+    outer.step(5, 6)
     wide.step(7)
+    late.step(5, 6)
     outer.step(7)
-    early.step(5)
-    late.step(5, 6)
-    early.step(6)
+    early.step(7)
     late.step(7)
-    early.step(7)
     swap_out.wait()
     swap_grad.wait()
     for reduction in (wide, outer, early, late):
@@ -910,42 +919,78 @@
 
 
 def cast_kernel(
-    gate, up, down, query, qrope, out, late,
-    o_gate, o_up, o_down, o_query, o_qrope, o_out, o_latent, o_krope, o_upkey, o_upval, o_gains,
+    wide, down, out, early, late, layer_out, grad_tokens,
+    o_gate, o_up, o_down, o_query, o_qrope, o_out, o_latent, o_krope, o_upkey, o_upval, o_attn, o_mlp, o_layer, o_tokens,
 ):
-    o_gate[...] = gate[...].astype(F32)
-    o_up[...] = up[...].astype(F32)
-    o_down[...] = down[...].astype(F32)
-    for source, target, width in ((query, o_query, 384), (qrope, o_qrope, 384), (out, o_out, 384), (late, o_latent, 256)):
-        target[:, 0:width] = source[:, 0:width].astype(F32)
-        target[:, width : 2 * width] = source[:, 512 : 512 + width].astype(F32)
-    for source, target in ((query, o_upkey), (qrope, o_upval)):
-        target[0] = source[:, 384:512].astype(F32)
-        target[1] = source[:, 896:1024].astype(F32)
-    o_krope[...] = late[:, 256:320].astype(F32) + late[:, 768:832].astype(F32)
-
-    @pl.when(pl.program_id(0) == 0)
+    o_gate[...] = wide[0].astype(F32)
+    o_up[...] = wide[1].astype(F32)
+    o_down[0:256] = down[0, :, 0:256].astype(F32)
+    o_down[256:512] = down[0, :, 256:512].astype(F32)
+    for source, m, target, width in (
+        (early, 0, o_query, 384), (early, 1, o_qrope, 384), (out, 0, o_out, 384), (late, 0, o_latent, 256)
+    ):
+        target[:, 0:width] = source[m, :, 0:width].astype(F32)
+        target[:, width : 2 * width] = source[m, :, 512 : 512 + width].astype(F32)
+    for m, target in ((0, o_upkey), (1, o_upval)):
+        target[0] = early[m, :, 384:512].astype(F32)
+        target[1] = early[m, :, 896:1024].astype(F32)
+    step = pl.program_id(0)
+
+    @pl.when(lax.rem(step, 4) < 2)
     def _():
-        o_gains[...] = late[0:16, 384:512].astype(F32) + late[0:16, 896:1024].astype(F32)
-
-
-def cast_sums(sums):
+        lanes = rows_at(lax.div(step, 4) * 256 + lax.rem(step, 4) * 128, 128, 128)
+        o_krope[:, lanes] = late[0, :, 256:384].astype(F32) + late[0, :, 768:896].astype(F32)
+
+    @pl.when(step == 0)
+    def _():
+        gains = late[0, 0:16, 384:512].astype(F32) + late[0, 0:16, 896:1024].astype(F32)
+        for p in range(6):
+            o_attn[p * 128 : p * 128 + 128] = gains[p]
+            o_mlp[p * 128 : p * 128 + 128] = gains[6 + p]
+        o_layer[...] = layer_out[...]
+        o_tokens[...] = grad_tokens[...]
+
+
+def cast_sums(layer_out, grad_tokens, wide, out, early, late):
     rows = lambda width: pl.BlockSpec((64, width), lambda i: (i, 0))
-    tall = pl.BlockSpec((1024, 128), lambda i: (lax.rem(i, 2), lax.div(i, 2)))
+    group = lambda n, width: pl.BlockSpec((n, 64, width), lambda i: (0, i, 0))
     ups = pl.BlockSpec((2, 64, 128), lambda i: (0, lax.rem(i, 4), lax.div(i, 4)))
     shapes = (
-        (768, 2048), (768, 2048), (2048, 768), (768, 768), (768, 768), (768, 768), (768, 512), (768, 64),
-        (2, 256, 384), (2, 256, 384), (16, 128),
+        (768, 2048), (768, 2048), (2048, 768), (768, 768), (768, 768), (768, 768), (768, 512), (64, 768),
+        (2, 256, 384), (2, 256, 384), (768,), (768,),
     )
+    whole = lambda shape: pl.BlockSpec(shape, lambda i: (0,) * len(shape))
+    rows_out = (layer_out, grad_tokens)
     return pl.pallas_call(
         cast_kernel,
         grid=(CAST_STEPS,),
-        out_shape=[jax.ShapeDtypeStruct(shape, F32) for shape in shapes],
-        in_specs=[rows(2048), rows(2048), tall] + [rows(1024)] * 4,
-        out_specs=[rows(2048), rows(2048), tall] + [rows(768)] * 3 + [rows(512), rows(64), ups, ups]
-        + [pl.BlockSpec((16, 128), lambda i: (0, 0))],
-        compiler_params=pltpu.CompilerParams(vmem_limit_bytes=40 * 2**20),
-    )(*sums)
+        out_shape=[jax.ShapeDtypeStruct(shape, F32) for shape in shapes]
+        + [jax.ShapeDtypeStruct(array.shape, array.dtype) for array in rows_out],
+        in_specs=[
+            group(2, 2048),
+            pl.BlockSpec((1, 256, 512), lambda i: (2, lax.div(i, 4), lax.rem(i, 4))),
+            group(1, 1024),
+            group(2, 1024),
+            group(1, 1024),
+        ]
+        + [whole(array.shape) for array in rows_out],
+        out_specs=[
+            rows(2048),
+            rows(2048),
+            pl.BlockSpec((512, 256), lambda i: (lax.rem(i, 4), lax.div(i, 4))),
+            rows(768),
+            rows(768),
+            rows(768),
+            rows(512),
+            whole((64, 768)),
+            ups,
+            ups,
+            whole((768,)),
+            whole((768,)),
+        ]
+        + [whole(array.shape) for array in rows_out],
+        compiler_params=pltpu.CompilerParams(vmem_limit_bytes=63 * 2**20),
+    )(wide, wide, out, early, late, layer_out, grad_tokens)
 
 
 def local(
@@ -954,23 +999,11 @@
 ):
     small = (tokens, cotangent, norm_attn, norm_mlp, group_of_seq, group_weight)
     weights = (w_latent, w_krope.T, w_query, w_qrope, w_upkey, w_upval, w_out, w_gate, w_up, w_down)
-    layer_out, grad_tokens, *sums = layer(small, weights)
-    gate, up, down, query, qrope, out, latent, krope, upkey, upval, gains = cast_sums(sums)
+    gate, up, down, query, qrope, out, latent, krope, upkey, upval, attn, mlp, layer_out, grad_tokens = cast_sums(
+        *layer(small, weights)
+    )
     return (
-        layer_out,
-        grad_tokens,
-        gains[0:6].reshape(768),
-        query,
-        qrope,
-        latent,
-        krope,
-        upkey,
-        upval,
-        out,
-        gains[6:12].reshape(768),
-        gate,
-        up,
-        down,
+        layer_out, grad_tokens, attn, query, qrope, latent, krope.T, upkey, upval, out, mlp, gate, up, down,
     )
 
 

time: 215 us -> 195 us (0.907)
  local copies, waits for them, and re-layouts: 12.3 us -> 0 us
  Pallas kernels: 202 us -> 194 us
    pallas_call x1, Pallas kernels: 189 us -> 176 us  [layer(): pl.pallas_call(layer_kernel, out_shape=[jax.ShapeDtypeStruct(shape, kind)...]
    unnamed x19 -> x0, local copies, waits for them, and re-layouts: 11.7 us -> none
    pallas_call x1, Pallas kernels: 12.1 us -> 17.4 us  [cast_sums(): pl.pallas_call(cast_kernel, grid=(CAST_STEPS,), out_shape=[jax.ShapeDtype...]
where the time goes in v4:
time: 195 us
  Pallas kernels  194 us (99%)
    pallas_call x1, Pallas kernels, layer(): pl.pallas_call(layer_kernel, out_shape=[jax.ShapeDtypeStruct(shape, kind)...  176 us
    pallas_call x1, Pallas kernels, cast_sums(): pl.pallas_call(cast_kernel, grid=(CAST_STEPS,), out_shape=[jax.ShapeDtype...  17.4 us

profile of v4, /device:TPU:1, one launch (start us, length us, event | category | flops | bytes accessed | tf_op | source)
XLA Modules:
  0.0 194.5 jit_solution(17221988264884107477)
XLA Ops:
  0.7 176.3 %shard_map.272 = (bf16[2,64,768]{2,1,0:T(8,128)(2,1)}, f32[2,64,768]{2,1,0:T(8,128)}, bf16[3,768,2048]{2,1,0:T(8,128)(2,1)}, bf16[1,768,1024]{2,1,0:T(8,128)(2,1...) custom-call(bf16[2,64,768]{2,1,0:T(8,128)(2,1)} %args_0_.4, bf16[2,64,768]{2,1,0:T(8,128)(2,1)} %args_1_.4, ...), custom_call_target="tpu_custom_call" | custom-call | tf_op jit(solution)/shard_map/pallas_call | solution.py:897
  177.0 17.4 %shard_map.273 = (f32[768,2048]{1,0:T(8,128)}, f32[768,2048]{1,0:T(8,128)}, f32[2048,768]{1,0:T(8,128)}, f32[768,768]{1,0:T(8,128)}, f32[768,768]{1,0:T(8,128)},...) custom-call(bf16[3,768,2048]{2,1,0:T(8,128)(2,1)} %get-tuple-element, ...), custom_call_target="tpu_custom_call" | custom-call | tf_op jit(solution)/shard_map/pallas_call | solution.py:964

commit v5 on v4

--- a/solution.py
+++ b/solution.py
@@ -274,6 +274,7 @@
         qrx=vmem((2, 4, 384, 128), BF),
         acc=vmem((4, 256, 384), F32),
         ctx=vmem((4, 256, 384), BF),
+        dqa=vmem((4, 256, 384), F32),
         logs=vmem((4, 8, 384), F32),
         delta=vmem((4, 8, 384), F32),
         aof=vmem((128, 768), F32),
@@ -481,6 +482,17 @@
                 r.qrx[(0,) + here] = jnp.where(low64(64), front, 0.0).astype(BF)
                 r.qrx[(1,) + here] = jnp.where(low64(64), 0.0, back).astype(BF)
 
+    swap_c.wait()
+    group = jnp.where(x_hi == 0, r.group_of_seq[0], r.group_of_seq[1])
+    weight = r.group_weight[0]
+    for g in range(1, GROUPS):
+        weight = jnp.where(group == g, r.group_weight[g], weight)
+    r.gb2[0:128] = (r.cbuf[...].astype(F32) * weight).astype(BF)
+    send_gb = paired(3, r.gb2.at[pl.ds(0, 128)], r.gb2.at[pl.ds(128, 128)])
+    send_gb.start()
+    for ref in (r.outacc, r.gnm, r.acc, r.dqa, r.dqr, r.dlat, r.dkr):
+        ref[...] = jnp.zeros_like(ref)
+
     for part in (1, 0):
         for copy in gather(part, 0):
             copy.wait()
@@ -510,7 +522,6 @@
         rot = r.kr[chunk].reshape(256, 128)
         return dot_nt(keys, r.qs[at]) + dot_nt(rot, r.qrx[far, at]), keys
 
-    r.acc[...] = jnp.zeros_like(r.acc)
     for copy in gather(1, 1) + gather(0, 1):
         copy.wait()
     top = lax.broadcasted_iota(jnp.int32, (128, 256), 0) < 64
@@ -574,23 +585,13 @@
     r.nm2[0:128] = (unit_mlp * gain_of(r.norm_mlp)).astype(BF)
     send_nm = paired(2, r.nm2.at[pl.ds(0, 128)], r.nm2.at[pl.ds(128, 128)])
     send_nm.start()
-    swap_c.wait()
-    group = jnp.where(x_hi == 0, r.group_of_seq[0], r.group_of_seq[1])
-    weight = r.group_weight[0]
-    for g in range(1, GROUPS):
-        weight = jnp.where(group == g, r.group_weight[g], weight)
-    r.gb2[0:128] = (r.cbuf[...].astype(F32) * weight).astype(BF)
-    send_gb = paired(3, r.gb2.at[pl.ds(0, 128)], r.gb2.at[pl.ds(128, 128)])
-    send_gb.start()
-    r.outacc[...] = jnp.zeros_like(r.outacc)
-    r.gnm[...] = jnp.zeros_like(r.gnm)
     for name in ("w_gate", "w_up", "w_down"):
         loads[name].wait()
     send_nm.wait()
     send_gb.wait()
 
     def tile(step, carried):
-        at = rows_at(step * 256, 256, 256)
+        at = rows_at(step * 512, 512, 512)
         act = r.nm2[...]
         gate = dot(act, r.v_gate[:, at])
         up = dot(act, r.v_up[:, at])
@@ -607,7 +608,7 @@
         r.gnm[...] += dot_nt(grad_gate, r.v_gate[:, at]) + dot_nt(grad_up, r.v_up[:, at])
         return carried
 
-    lax.fori_loop(0, 4, tile, 0)
+    lax.fori_loop(0, 2, tile, 0)
     send_gnm = paired(4, r.gnm.at[pl.ds(128, 128)], r.gnmx)
     send_out = paired(10, r.outacc.at[pl.ds(128, 128)], r.outx)
     send_gnm.start()
@@ -620,16 +621,12 @@
     r.nmt[...] = r.nm2[...].T
     r.hidt[...] = r.acts[0].T
     for o in range(3):
-
-        def wide_tile(i, carried):
-            cols = rows_at(i * 256, 256, 256)
-            left = r.nmt[o * 256 : o * 256 + 256]
+        left = r.nmt[o * 256 : o * 256 + 256]
+        for i in range(4):
+            cols = slice(i * 256, i * 256 + 256)
             r.wide_total[o, i, 0] = dot(left, r.acts[1, :, cols]).astype(BF)
             r.wide_total[o, i, 1] = dot(left, r.acts[2, :, cols]).astype(BF)
             r.wide_total[o, i, 2] = dot(r.hidt[cols, :], r.gb2[:, o * 256 : o * 256 + 256]).astype(BF)
-            return carried
-
-        lax.fori_loop(0, 4, wide_tile, 0)
         wide.start(0, (o,))
 
     def norm_back(grads, values, gain):
@@ -680,17 +677,12 @@
         r.out_total[o, 3, 0] = jnp.zeros((256, 128), BF)
     outer.start(0)
 
-    r.acc[...] = jnp.zeros_like(r.acc)
-    r.dqr[...] = jnp.zeros_like(r.dqr)
-    r.dlat[...] = jnp.zeros_like(r.dlat)
-    r.dkr[...] = jnp.zeros_like(r.dkr)
-
     def backward(half):
         def chunk_step(step, carried):
             places = masks(half, step)
             for g in range(2):
                 at = half * 2 + g
-                mixed, turned = r.acc[at], r.dqr[at]
+                mixed, turned = r.dqa[at], r.dqr[at]
                 for far, (chunk, allowed) in enumerate(places):
                     raw, keys = raw_scores(at, far, chunk, g)
                     weights = jnp.exp2(raw * (FACTOR * LOG2E) - r.logs[at, 0:1])
@@ -702,7 +694,7 @@
                     turned = turned + dot(r.krt[far, chunk], dscore)
                     r.dlat[far * 2 + g, chunk] += FACTOR * dot(dscore, r.qs[at]) + dot(weights, r.ga[at])
                     r.dkr[chunk] += FACTOR * dot(dscore, r.qrx[far, at])
-                r.acc[at], r.dqr[at] = mixed, turned
+                r.dqa[at], r.dqr[at] = mixed, turned
             return carried
 
         lax.fori_loop(0, counts[half], chunk_step, 0)
@@ -747,7 +739,7 @@
         for p in range(6):
             rows, lanes = slice(half * 64, half * 64 + 64), slice((p % 3) * 128, (p % 3) * 128 + 128)
             at = half * 2 + p // 3
-            piece = (FACTOR * from_latent(r.acc, r.v_upkey, half, p)).astype(BF)
+            piece = (FACTOR * from_latent(r.dqa, r.v_upkey, half, p)).astype(BF)
             r.gq2[p // 3, rows, lanes] = piece
             turned = FACTOR * r.dqr[at, :, lanes].T
             turned = pick(turned + pltpu.roll(turned, 64, 1))
@@ -764,7 +756,7 @@
             key_sum, value_sum = jnp.zeros((256, 128), F32), jnp.zeros((256, 128), F32)
             for half in range(2):
                 rows = slice(half * 64, half * 64 + 64)
-                key_sum += FACTOR * dot(r.acc[half * 2 + g, :, lanes].astype(BF), both(r.q[rows, wide_lanes]))
+                key_sum += FACTOR * dot(r.dqa[half * 2 + g, :, lanes].astype(BF), both(r.q[rows, wide_lanes]))
                 value_sum += dot(r.ctx[half * 2 + g, :, lanes], both(r.gmix[rows, wide_lanes]))
             r.dup[g, 0, j] = key_sum.astype(BF)
             r.dup[g, 1, j] = value_sum.astype(BF)
@@ -915,7 +907,7 @@
     return np.concatenate([cosine, cosine, -sine, sine], axis=1).astype(np.float32)
 
 
-CAST_STEPS = 12
+CAST_STEPS = 3
 
 
 def cast_kernel(
@@ -924,8 +916,8 @@
 ):
     o_gate[...] = wide[0].astype(F32)
     o_up[...] = wide[1].astype(F32)
-    o_down[0:256] = down[0, :, 0:256].astype(F32)
-    o_down[256:512] = down[0, :, 256:512].astype(F32)
+    for k in range(8):
+        o_down[k * 256 : k * 256 + 256] = down[0, :, k * 256 : k * 256 + 256].astype(F32)
     for source, m, target, width in (
         (early, 0, o_query, 384), (early, 1, o_qrope, 384), (out, 0, o_out, 384), (late, 0, o_latent, 256)
     ):
@@ -935,11 +927,10 @@
         target[0] = early[m, :, 384:512].astype(F32)
         target[1] = early[m, :, 896:1024].astype(F32)
     step = pl.program_id(0)
-
-    @pl.when(lax.rem(step, 4) < 2)
-    def _():
-        lanes = rows_at(lax.div(step, 4) * 256 + lax.rem(step, 4) * 128, 128, 128)
-        o_krope[:, lanes] = late[0, :, 256:384].astype(F32) + late[0, :, 768:896].astype(F32)
+    for part in range(2):
+        rows = slice(part * 64, part * 64 + 64)
+        lanes = rows_at(step * 256 + part * 128, 128, 128)
+        o_krope[:, lanes] = late[0, rows, 256:384].astype(F32) + late[0, rows, 768:896].astype(F32)
 
     @pl.when(step == 0)
     def _():
@@ -952,14 +943,14 @@
 
 
 def cast_sums(layer_out, grad_tokens, wide, out, early, late):
-    rows = lambda width: pl.BlockSpec((64, width), lambda i: (i, 0))
-    group = lambda n, width: pl.BlockSpec((n, 64, width), lambda i: (0, i, 0))
-    ups = pl.BlockSpec((2, 64, 128), lambda i: (0, lax.rem(i, 4), lax.div(i, 4)))
+    rows = lambda width: pl.BlockSpec((256, width), lambda i: (i, 0))
+    group = lambda n, width: pl.BlockSpec((n, 256, width), lambda i: (0, i, 0))
+    ups = pl.BlockSpec((2, 256, 128), lambda i: (0, 0, i))
+    whole = lambda shape: pl.BlockSpec(shape, lambda i: (0,) * len(shape))
     shapes = (
         (768, 2048), (768, 2048), (2048, 768), (768, 768), (768, 768), (768, 768), (768, 512), (64, 768),
         (2, 256, 384), (2, 256, 384), (768,), (768,),
     )
-    whole = lambda shape: pl.BlockSpec(shape, lambda i: (0,) * len(shape))
     rows_out = (layer_out, grad_tokens)
     return pl.pallas_call(
         cast_kernel,
@@ -968,26 +959,15 @@
         + [jax.ShapeDtypeStruct(array.shape, array.dtype) for array in rows_out],
         in_specs=[
             group(2, 2048),
-            pl.BlockSpec((1, 256, 512), lambda i: (2, lax.div(i, 4), lax.rem(i, 4))),
+            pl.BlockSpec((1, 256, 2048), lambda i: (2, i, 0)),
             group(1, 1024),
             group(2, 1024),
             group(1, 1024),
         ]
         + [whole(array.shape) for array in rows_out],
-        out_specs=[
-            rows(2048),
-            rows(2048),
-            pl.BlockSpec((512, 256), lambda i: (lax.rem(i, 4), lax.div(i, 4))),
-            rows(768),
-            rows(768),
-            rows(768),
-            rows(512),
-            whole((64, 768)),
-            ups,
-            ups,
-            whole((768,)),
-            whole((768,)),
-        ]
+        out_specs=[rows(2048), rows(2048), pl.BlockSpec((2048, 256), lambda i: (0, i))]
+        + [rows(768)] * 3
+        + [rows(512), whole((64, 768)), ups, ups, whole((768,)), whole((768,))]
         + [whole(array.shape) for array in rows_out],
         compiler_params=pltpu.CompilerParams(vmem_limit_bytes=63 * 2**20),
     )(wide, wide, out, early, late, layer_out, grad_tokens)

time: 195 us -> 189 us (0.969)
  Pallas kernels: 194 us -> 188 us
    pallas_call x1, Pallas kernels: 17.4 us -> 14.5 us  [cast_sums(): pl.pallas_call(cast_kernel, grid=(CAST_STEPS,), out_shape=[jax.ShapeDtype...]
    pallas_call x1, Pallas kernels: 176 us -> 174 us  [layer(): pl.pallas_call(layer_kernel, out_shape=[jax.ShapeDtypeStruct(shape, kind)...]
where the time goes in v5:
time: 189 us
  Pallas kernels  188 us (99%)
    pallas_call x1, Pallas kernels, layer(): pl.pallas_call(layer_kernel, out_shape=[jax.ShapeDtypeStruct(shape, kind)...  174 us
    pallas_call x1, Pallas kernels, cast_sums(): pl.pallas_call(cast_kernel, grid=(CAST_STEPS,), out_shape=[jax.ShapeDtype...  14.5 us

profile of v5, /device:TPU:1, one launch (start us, length us, event | category | flops | bytes accessed | tf_op | source)
XLA Modules:
  0.0 188.9 jit_solution(13635450114189965830)
XLA Ops:
  0.7 173.5 %shard_map.272 = (bf16[2,64,768]{2,1,0:T(8,128)(2,1)}, f32[2,64,768]{2,1,0:T(8,128)}, bf16[3,768,2048]{2,1,0:T(8,128)(2,1)}, bf16[1,768,1024]{2,1,0:T(8,128)(2,1...) custom-call(bf16[2,64,768]{2,1,0:T(8,128)(2,1)} %args_0_.4, bf16[2,64,768]{2,1,0:T(8,128)(2,1)} %args_1_.4, ...), custom_call_target="tpu_custom_call" | custom-call | tf_op jit(solution)/shard_map/pallas_call | solution.py:889
  174.2 14.5 %shard_map.273 = (f32[768,2048]{1,0:T(8,128)}, f32[768,2048]{1,0:T(8,128)}, f32[2048,768]{1,0:T(8,128)}, f32[768,768]{1,0:T(8,128)}, f32[768,768]{1,0:T(8,128)},...) custom-call(bf16[3,768,2048]{2,1,0:T(8,128)(2,1)} %get-tuple-element, ...), custom_call_target="tpu_custom_call" | custom-call | tf_op jit(solution)/shard_map/pallas_call | solution.py:955

commit v6 on v5

--- a/solution.py
+++ b/solution.py
@@ -254,9 +254,11 @@
         cosine=vmem((128, 128), F32),
         sine=vmem((128, 128), F32),
         swap_sem=dma((4, 2)),
-        pair_sem=dma((12, 2)),
+        pair_sem=dma((11, 2)),
         lat_send=dma((2, 2, 3)),
-        lat_recv=dma((2, 2, 2, 2, 3)),
+        ag_recv=dma((2, 2, 3)),
+        lat_recv=dma((2, 2, 2, 3)),
+        fw_sem=dma((2, 7, 2)),
         xbuf=vmem((128, 768), BF),
         cbuf=vmem((128, 768), BF),
         norm2=vmem((256, 768), BF),
@@ -271,7 +273,9 @@
         rel=vmem((2, 256, 384), jnp.int32),
         qs=vmem((4, 384, 256), BF),
         ga=vmem((4, 384, 256), BF),
-        qrx=vmem((2, 4, 384, 128), BF),
+        qrx=vmem((4, 384, 128), BF),
+        krm=vmem((2, 4, 256, 128), BF),
+        gh=vmem((256, 1024), F32),
         acc=vmem((4, 256, 384), F32),
         ctx=vmem((4, 256, 384), BF),
         dqa=vmem((4, 256, 384), F32),
@@ -428,25 +432,18 @@
         for g in range(2):
             r.lat[half * 2 + g, y, z] = latents[half * 64 : half * 64 + 64, g * 256 : g * 256 + 256]
 
-    def gather(part, phase):
+    def gather(part):
         made = []
-        axis = (2, 1)[(part + phase) % 2]
+        axis = (2, 1)[part]
         for step in (1, 2, 3):
-            peer = on_ring(place, axis, step)
-            two = pl.ds(part * 2, 2)
-            if phase == 0:
-                pieces = [r.lat.at[two, y, z], r.kr.at[y, z]]
-            elif part == 0:
-                pieces = [r.lat.at[two, y], r.kr.at[y]]
-            else:
-                pieces = [r.lat.at[two, :, z], None]
-            for at, piece in enumerate(pieces if part == 0 else pieces[:1]):
-                send = r.lat_send.at[part, at, step - 1]
-                made.append(remote(piece, piece, send, r.lat_recv.at[0, part, phase, at, step - 1], peer))
+            pieces = [r.lat.at[pl.ds(part * 2, 2), y, z]] + ([r.kr.at[y, z]] if part == 0 else [])
+            for at, piece in enumerate(pieces):
+                send, recv = r.lat_send.at[part, at, step - 1], r.ag_recv.at[part, at, step - 1]
+                made.append(remote(piece, piece, send, recv, on_ring(place, axis, step)))
         return made
 
     for part in range(2):
-        for copy in gather(part, 0):
+        for copy in gather(part):
             copy.start()
     for name in ("w_upval", "w_out", "w_gate", "w_up", "w_down"):
         loads[name].start()
@@ -478,9 +475,7 @@
             for odd in range(2):
                 front, back = (turned, pair) if odd else (pair, turned)
                 at = (p % 3) * 128 + odd * 64
-                here = (half * 2 + p // 3, slice(at, at + 64))
-                r.qrx[(0,) + here] = jnp.where(low64(64), front, 0.0).astype(BF)
-                r.qrx[(1,) + here] = jnp.where(low64(64), 0.0, back).astype(BF)
+                r.qrx[half * 2 + p // 3, at : at + 64] = jnp.where(low64(64), front, back).astype(BF)
 
     swap_c.wait()
     group = jnp.where(x_hi == 0, r.group_of_seq[0], r.group_of_seq[1])
@@ -490,13 +485,46 @@
     r.gb2[0:128] = (r.cbuf[...].astype(F32) * weight).astype(BF)
     send_gb = paired(3, r.gb2.at[pl.ds(0, 128)], r.gb2.at[pl.ds(128, 128)])
     send_gb.start()
+    def spread(part, stage):
+        axis = (1, 2)[part]
+        me = place[axis]
+        right, left = on_ring(place, axis, 1), on_ring(place, axis, 3)
+        before, after = lax.rem(me + 3, 4), lax.rem(me + 1, 4)
+
+        def plane(which, where):
+            return r.lat.at[which, where] if part == 0 else r.lat.at[which, :, where]
+
+        if stage == 0:
+            mine = plane(pl.ds(part * 2, 2), me)
+            pieces = [(mine, right), (mine, left)]
+            if part == 0:
+                pieces += [(r.kr.at[me], right), (r.kr.at[me], left)]
+        else:
+            pieces = [(plane(part * 2, before), right), (plane(part * 2 + 1, after), left)]
+            if part == 0:
+                pieces += [(r.kr.at[after], left)]
+        return [
+            remote(piece, piece, r.fw_sem.at[part, stage * 4 + at, 0], r.fw_sem.at[part, stage * 4 + at, 1], peer)
+            for at, (piece, peer) in enumerate(pieces)
+        ]
+
+    for part in (1, 0):
+        for copy in gather(part):
+            copy.wait()
+        for copy in spread(part, 0):
+            copy.start()
+    loads["w_down"].wait()
+    send_gb.wait()
+    for part in range(4):
+        cols = slice(part * 256, part * 256 + 256)
+        r.gh[:, cols] = dot_nt(r.gb2[...], r.v_down[cols, :])
     for ref in (r.outacc, r.gnm, r.acc, r.dqa, r.dqr, r.dlat, r.dkr):
         ref[...] = jnp.zeros_like(ref)
 
     for part in (1, 0):
-        for copy in gather(part, 0):
+        for copy in spread(part, 0):
             copy.wait()
-        for copy in gather(part, 1):
+        for copy in spread(part, 1):
             copy.start()
 
     def transpose_latents():
@@ -515,41 +543,47 @@
         first = query_blk[half] * 64
         near = r.rel[0] <= first - 512 * step - 64 * x_hi
         far = r.rel[1] <= first - 1984 + 512 * (3 - step) + 64 * x_hi
-        return (step, near), (3 - step, far)
-
-    def raw_scores(at, far, chunk, g):
-        keys = r.lat[far * 2 + g, chunk].reshape(256, 256)
-        rot = r.kr[chunk].reshape(256, 128)
-        return dot_nt(keys, r.qs[at]) + dot_nt(rot, r.qrx[far, at]), keys
-
-    for copy in gather(1, 1) + gather(0, 1):
+        return near, far
+
+    def pair_keys(g, step):
+        keys = [r.lat[far * 2 + g, chunk].reshape(256, 256) for far, chunk in ((0, step), (1, 3 - step))]
+        return jnp.concatenate(keys, axis=0)
+
+    def pair_scores(at, keys, step):
+        rot = jnp.concatenate([r.krm[0, step], r.krm[1, 3 - step]], axis=0)
+        return dot_nt(keys, r.qs[at]) + dot_nt(rot, r.qrx[at])
+
+    def pair_turned(g, step):
+        turned = [r.latt[far * 2 + g, chunk].reshape(256, 256) for far, chunk in ((0, step), (1, 3 - step))]
+        return jnp.concatenate(turned, axis=1)
+
+    for copy in spread(1, 1) + spread(0, 1):
         copy.wait()
     top = lax.broadcasted_iota(jnp.int32, (128, 256), 0) < 64
     for c in range(4):
-        turned = r.kr[c].reshape(256, 128).astype(F32).T
+        rot = r.kr[c].reshape(256, 128).astype(F32)
+        r.krm[0, c] = jnp.where(low64(256), rot, 0.0).astype(BF)
+        r.krm[1, c] = jnp.where(low64(256), 0.0, rot).astype(BF)
+        turned = rot.T
         r.krt[0, c] = jnp.where(top, turned, 0.0).astype(BF)
         r.krt[1, c] = jnp.where(top, 0.0, turned).astype(BF)
     transpose_latents()
 
     def forward(half):
         def chunk_step(step, state):
-            places = masks(half, step)
+            near, far = masks(half, step)
             result = []
             for g in range(2):
                 at = half * 2 + g
                 high, total = state[g]
-                raws = [
-                    jnp.where(allowed, raw_scores(at, far, chunk, g)[0], HIDDEN_SCORE)
-                    for far, (chunk, allowed) in enumerate(places)
-                ]
+                raw = pair_scores(at, pair_keys(g, step), step)
+                raws = [jnp.where(near, raw[0:256], HIDDEN_SCORE), jnp.where(far, raw[256:512], HIDDEN_SCORE)]
                 new_high = jnp.maximum(high, jnp.max(jnp.maximum(*raws), axis=0, keepdims=True))
                 shrink = jnp.exp2((high - new_high) * (FACTOR * LOG2E))
                 weights = [jnp.exp2((raw - new_high) * (FACTOR * LOG2E)) for raw in raws]
                 total = total * shrink + jnp.sum(weights[0] + weights[1], axis=0, keepdims=True)
-                mixed = r.acc[at] * shrink
-                for far, (chunk, _) in enumerate(places):
-                    value = r.latt[far * 2 + g, chunk].reshape(256, 256)
-                    mixed = mixed + dot(value, weights[far].astype(BF))
+                weights = jnp.concatenate([weight.astype(BF) for weight in weights], axis=0)
+                mixed = r.acc[at] * shrink + dot(pair_turned(g, step), weights)
                 r.acc[at] = mixed
                 result.append((new_high, total))
             return tuple(result)
@@ -585,10 +619,9 @@
     r.nm2[0:128] = (unit_mlp * gain_of(r.norm_mlp)).astype(BF)
     send_nm = paired(2, r.nm2.at[pl.ds(0, 128)], r.nm2.at[pl.ds(128, 128)])
     send_nm.start()
-    for name in ("w_gate", "w_up", "w_down"):
-        loads[name].wait()
+    loads["w_gate"].wait()
+    loads["w_up"].wait()
     send_nm.wait()
-    send_gb.wait()
 
     def tile(step, carried):
         at = rows_at(step * 512, 512, 512)
@@ -598,7 +631,7 @@
         sig = jax.nn.sigmoid(gate)
         silu = gate * sig
         hidden = (silu * up).astype(BF)
-        grad_hidden = dot_nt(r.gb2[...], r.v_down[at, :])
+        grad_hidden = r.gh[:, at]
         grad_gate = (grad_hidden * up * sig * (1.0 + gate * (1.0 - sig))).astype(BF)
         grad_up = (grad_hidden * silu).astype(BF)
         r.acts[0, :, at] = hidden
@@ -679,22 +712,28 @@
 
     def backward(half):
         def chunk_step(step, carried):
-            places = masks(half, step)
+            near, far = masks(half, step)
+            rot_turned = jnp.concatenate([r.krt[0, step], r.krt[1, 3 - step]], axis=1)
+            rot_sum = None
             for g in range(2):
                 at = half * 2 + g
-                mixed, turned = r.dqa[at], r.dqr[at]
-                for far, (chunk, allowed) in enumerate(places):
-                    raw, keys = raw_scores(at, far, chunk, g)
-                    weights = jnp.exp2(raw * (FACTOR * LOG2E) - r.logs[at, 0:1])
-                    weights = jnp.where(allowed, weights, 0.0)
-                    dprob = dot_nt(keys, r.ga[at])
-                    dscore = (weights * (dprob - r.delta[at, 0:1])).astype(BF)
-                    weights = weights.astype(BF)
-                    mixed = mixed + dot(r.latt[far * 2 + g, chunk].reshape(256, 256), dscore)
-                    turned = turned + dot(r.krt[far, chunk], dscore)
-                    r.dlat[far * 2 + g, chunk] += FACTOR * dot(dscore, r.qs[at]) + dot(weights, r.ga[at])
-                    r.dkr[chunk] += FACTOR * dot(dscore, r.qrx[far, at])
-                r.dqa[at], r.dqr[at] = mixed, turned
+                keys = pair_keys(g, step)
+                raw = pair_scores(at, keys, step)
+                weights = jnp.exp2(raw * (FACTOR * LOG2E) - r.logs[at, 0:1])
+                weights = [jnp.where(near, weights[0:256], 0.0), jnp.where(far, weights[256:512], 0.0)]
+                dprob = dot_nt(keys, r.ga[at]) - r.delta[at, 0:1]
+                dscore = [weights[0] * dprob[0:256], weights[1] * dprob[256:512]]
+                dscore = jnp.concatenate([part.astype(BF) for part in dscore], axis=0)
+                weights = jnp.concatenate([part.astype(BF) for part in weights], axis=0)
+                r.dqa[at] += dot(pair_turned(g, step), dscore)
+                r.dqr[at] += dot(rot_turned, dscore)
+                grads = FACTOR * dot(dscore, r.qs[at]) + dot(weights, r.ga[at])
+                r.dlat[g, step] += grads[0:256]
+                r.dlat[2 + g, 3 - step] += grads[256:512]
+                rots = dot(dscore, r.qrx[at])
+                rot_sum = rots if rot_sum is None else rot_sum + rots
+            r.dkr[step] += jnp.where(low64(256), FACTOR * rot_sum[0:256], 0.0)
+            r.dkr[3 - step] += jnp.where(low64(256), 0.0, FACTOR * rot_sum[256:512])
             return carried
 
         lax.fori_loop(0, counts[half], chunk_step, 0)
@@ -721,7 +760,7 @@
                 pieces = [(r.st1.at[:, to], r.rt2.at[at])]
             for k, (src, dst) in enumerate(pieces):
                 send = r.lat_send.at[part, k, at]
-                made.append(remote(src, dst, send, r.lat_recv.at[1, part, phase, k, at], peer))
+                made.append(remote(src, dst, send, r.lat_recv.at[part, phase, k, at], peer))
         return made
 
     backward(0)

time: 189 us -> 182 us (0.963)
  Pallas kernels: 188 us -> 182 us
    pallas_call x1, Pallas kernels: 174 us -> 167 us  [layer(): pl.pallas_call(layer_kernel, out_shape=[jax.ShapeDtypeStruct(shape, kind)...]
where the time goes in v6:
time: 182 us
  Pallas kernels  182 us (100%)
    pallas_call x1, Pallas kernels, layer(): pl.pallas_call(layer_kernel, out_shape=[jax.ShapeDtypeStruct(shape, kind)...  167 us
    pallas_call x1, Pallas kernels, cast_sums(): pl.pallas_call(cast_kernel, grid=(CAST_STEPS,), out_shape=[jax.ShapeDtype...  14.5 us

profile of v6, /device:TPU:1, one launch (start us, length us, event | category | flops | bytes accessed | tf_op | source)
XLA Modules:
  0.0 182.3 jit_solution(3616353800925406177)
XLA Ops:
  0.7 167.0 %shard_map.272 = (bf16[2,64,768]{2,1,0:T(8,128)(2,1)}, f32[2,64,768]{2,1,0:T(8,128)}, bf16[3,768,2048]{2,1,0:T(8,128)(2,1)}, bf16[1,768,1024]{2,1,0:T(8,128)(2,1...) custom-call(bf16[2,64,768]{2,1,0:T(8,128)(2,1)} %args_0_.4, bf16[2,64,768]{2,1,0:T(8,128)(2,1)} %args_1_.4, ...), custom_call_target="tpu_custom_call" | custom-call | tf_op jit(solution)/shard_map/pallas_call | solution.py:928
  167.7 14.5 %shard_map.273 = (f32[768,2048]{1,0:T(8,128)}, f32[768,2048]{1,0:T(8,128)}, f32[2048,768]{1,0:T(8,128)}, f32[768,768]{1,0:T(8,128)}, f32[768,768]{1,0:T(8,128)},...) custom-call(bf16[3,768,2048]{2,1,0:T(8,128)(2,1)} %get-tuple-element, ...), custom_call_target="tpu_custom_call" | custom-call | tf_op jit(solution)/shard_map/pallas_call | solution.py:994

commit v7 on v6

--- a/solution.py
+++ b/solution.py
@@ -408,29 +408,18 @@
     other = pltpu.roll(turns, 64, 1)
     r.cosine[...] = jnp.where(low64(128), turns, other)
     r.sine[...] = jnp.where(low64(128), other, turns)
-    swap_x.wait()
-
     def unit_of(values):
         inverse = lax.rsqrt(jnp.mean(values * values, axis=-1, keepdims=True) + EPSILON)
         return values * inverse, inverse
 
-    unit = unit_of(r.xbuf[...].astype(F32))[0]
-    normed = (unit * gain_of(r.norm_attn)).astype(BF)
-    r.norm2[0:128] = normed
-    send_norm = paired(0, r.norm2.at[pl.ds(0, 128)], r.norm2.at[pl.ds(128, 128)])
-    send_norm.start()
-    loads["w_latent"].wait()
-    loads["w_krope"].wait()
-    key_pre = dot_nt(normed, r.v_krope[...])
-    r.krd[:, 0:64] = key_pre
-    r.krd[:, 64:128] = key_pre
-    key_pre = r.krd[...]
-    key_rot = (key_pre * r.cosine[...] + swap_halves(key_pre) * r.sine[...]).astype(BF)
-    r.kr[y, z] = pick(key_rot)
-    latents = dot(normed, r.v_latent[...]).astype(BF)
-    for half in range(2):
+    def start_half(half):
+        rows = slice(half * 64, half * 64 + 64)
+        unit = unit_of(r.xbuf[rows].astype(F32))[0]
+        normed = (unit * gain_of(r.norm_attn)).astype(BF)
+        r.norm2[rows] = normed
+        latents = dot(normed, r.v_latent[...]).astype(BF)
         for g in range(2):
-            r.lat[half * 2 + g, y, z] = latents[half * 64 : half * 64 + 64, g * 256 : g * 256 + 256]
+            r.lat[half * 2 + g, y, z] = latents[:, g * 256 : g * 256 + 256]
 
     def gather(part):
         made = []
@@ -442,9 +431,26 @@
                 made.append(remote(piece, piece, send, recv, on_ring(place, axis, step)))
         return made
 
-    for part in range(2):
-        for copy in gather(part):
-            copy.start()
+    loads["w_latent"].wait()
+    start_half(0)
+    for copy in gather(0)[0::2]:
+        copy.start()
+    swap_x.wait()
+    start_half(1)
+    for copy in gather(1):
+        copy.start()
+    loads["w_krope"].wait()
+    key_pre = dot_nt(r.norm2[0:128], r.v_krope[...])
+    r.krd[:, 0:64] = key_pre
+    r.krd[:, 64:128] = key_pre
+    key_pre = r.krd[...]
+    key_rot = (key_pre * r.cosine[...] + swap_halves(key_pre) * r.sine[...]).astype(BF)
+    r.kr[y, z] = pick(key_rot)
+    for copy in gather(0)[1::2]:
+        copy.start()
+    send_norm = paired(0, r.norm2.at[pl.ds(0, 128)], r.norm2.at[pl.ds(128, 128)])
+    send_norm.start()
+    normed = r.norm2[0:128]
     for name in ("w_upval", "w_out", "w_gate", "w_up", "w_down"):
         loads[name].start()
 
@@ -518,7 +524,7 @@
     for part in range(4):
         cols = slice(part * 256, part * 256 + 256)
         r.gh[:, cols] = dot_nt(r.gb2[...], r.v_down[cols, :])
-    for ref in (r.outacc, r.gnm, r.acc, r.dqa, r.dqr, r.dlat, r.dkr):
+    for ref in (r.acc, r.dqa, r.dqr, r.dlat, r.dkr):
         ref[...] = jnp.zeros_like(ref)
 
     for part in (1, 0):
@@ -527,47 +533,56 @@
         for copy in spread(part, 1):
             copy.start()
 
-    def transpose_latents():
-        def body(step, carried):
-            j, c = lax.div(step, 4), lax.rem(step, 4)
-            r.latt[j, c] = r.lat[j, c].reshape(256, 256).T.reshape(4, 64, 256)
-            return carried
-
-        lax.fori_loop(0, 16, body, 0)
-
-    query_blk = (blk, 31 - blk)
-
-    counts = (y + 1, 4 - y)
-
-    def masks(half, step):
-        first = query_blk[half] * 64
-        near = r.rel[0] <= first - 512 * step - 64 * x_hi
-        far = r.rel[1] <= first - 1984 + 512 * (3 - step) + 64 * x_hi
-        return near, far
-
-    def pair_keys(g, step):
-        keys = [r.lat[far * 2 + g, chunk].reshape(256, 256) for far, chunk in ((0, step), (1, 3 - step))]
-        return jnp.concatenate(keys, axis=0)
-
-    def pair_scores(at, keys, step):
-        rot = jnp.concatenate([r.krm[0, step], r.krm[1, 3 - step]], axis=0)
-        return dot_nt(keys, r.qs[at]) + dot_nt(rot, r.qrx[at])
-
-    def pair_turned(g, step):
-        turned = [r.latt[far * 2 + g, chunk].reshape(256, 256) for far, chunk in ((0, step), (1, 3 - step))]
-        return jnp.concatenate(turned, axis=1)
-
-    for copy in spread(1, 1) + spread(0, 1):
-        copy.wait()
     top = lax.broadcasted_iota(jnp.int32, (128, 256), 0) < 64
-    for c in range(4):
+
+    def turn(j, c):
+        r.latt[j, c] = r.lat[j, c].reshape(256, 256).T.reshape(4, 64, 256)
+
+    def turn_rot(c):
         rot = r.kr[c].reshape(256, 128).astype(F32)
         r.krm[0, c] = jnp.where(low64(256), rot, 0.0).astype(BF)
         r.krm[1, c] = jnp.where(low64(256), 0.0, rot).astype(BF)
         turned = rot.T
         r.krt[0, c] = jnp.where(top, turned, 0.0).astype(BF)
         r.krt[1, c] = jnp.where(top, 0.0, turned).astype(BF)
-    transpose_latents()
+
+    for step in (0, 1, 3):
+        plane = lax.rem(y + step, 4)
+        turn(0, plane)
+        turn(1, plane)
+        turn_rot(plane)
+
+    query_blk = (blk, 31 - blk)
+
+    counts = (y + 1, 4 - y)
+
+    def masks(half, step):
+        first = query_blk[half] * 64
+        near = r.rel[0] <= first - 512 * step - 64 * x_hi
+        far = r.rel[1] <= first - 1984 + 512 * (3 - step) + 64 * x_hi
+        return near, far
+
+    def pair_keys(g, step):
+        keys = [r.lat[far * 2 + g, chunk].reshape(256, 256) for far, chunk in ((0, step), (1, 3 - step))]
+        return jnp.concatenate(keys, axis=0)
+
+    def pair_scores(at, keys, step):
+        rot = jnp.concatenate([r.krm[0, step], r.krm[1, 3 - step]], axis=0)
+        return dot_nt(keys, r.qs[at]) + dot_nt(rot, r.qrx[at])
+
+    def pair_turned(g, step):
+        turned = [r.latt[far * 2 + g, chunk].reshape(256, 256) for far, chunk in ((0, step), (1, 3 - step))]
+        return jnp.concatenate(turned, axis=1)
+
+    for copy in spread(1, 1) + spread(0, 1):
+        copy.wait()
+    across = lax.rem(y + 2, 4)
+    turn(0, across)
+    turn(1, across)
+    turn_rot(across)
+    for c in range(4):
+        turn(2, c)
+        turn(3, c)
 
     def forward(half):
         def chunk_step(step, state):
@@ -621,6 +636,7 @@
     send_nm.start()
     loads["w_gate"].wait()
     loads["w_up"].wait()
+    r.nmt[:, 0:128] = r.nm2[0:128].T
     send_nm.wait()
 
     def tile(step, carried):
@@ -637,21 +653,14 @@
         r.acts[0, :, at] = hidden
         r.acts[1, :, at] = grad_gate
         r.acts[2, :, at] = grad_up
-        r.outacc[...] += dot(hidden, r.v_down[at, :])
-        r.gnm[...] += dot_nt(grad_gate, r.v_gate[:, at]) + dot_nt(grad_up, r.v_up[:, at])
         return carried
 
     lax.fori_loop(0, 2, tile, 0)
-    send_gnm = paired(4, r.gnm.at[pl.ds(128, 128)], r.gnmx)
-    send_out = paired(10, r.outacc.at[pl.ds(128, 128)], r.outx)
-    send_gnm.start()
-    send_out.start()
-
     wide = Reduction(r, "wide", place, r.g_wide, True)
     outer = Reduction(r, "out", place, r.g_out, False)
     early = Reduction(r, "early", place, r.g_early, False, True)
     late = Reduction(r, "late", place, r.g_late, False, True)
-    r.nmt[...] = r.nm2[...].T
+    r.nmt[:, 128:256] = r.nm2[128:256].T
     r.hidt[...] = r.acts[0].T
     for o in range(3):
         left = r.nmt[o * 256 : o * 256 + 256]
@@ -661,6 +670,13 @@
             r.wide_total[o, i, 1] = dot(left, r.acts[2, :, cols]).astype(BF)
             r.wide_total[o, i, 2] = dot(r.hidt[cols, :], r.gb2[:, o * 256 : o * 256 + 256]).astype(BF)
         wide.start(0, (o,))
+
+    r.gnm[...] = dot_nt(r.acts[1], r.v_gate[...]) + dot_nt(r.acts[2], r.v_up[...])
+    send_gnm = paired(4, r.gnm.at[pl.ds(128, 128)], r.gnmx)
+    send_gnm.start()
+    r.outacc[...] = dot(r.acts[0], r.v_down[...])
+    send_out = paired(10, r.outacc.at[pl.ds(128, 128)], r.outx)
+    send_out.start()
 
     def norm_back(grads, values, gain):
         unit_rows, inverse = unit_of(values)

time: 182 us -> 178 us (0.978)
  Pallas kernels: 182 us -> 177 us
    pallas_call x1, Pallas kernels: 167 us -> 163 us  [layer(): pl.pallas_call(layer_kernel, out_shape=[jax.ShapeDtypeStruct(shape, kind)...]
where the time goes in v7:
time: 178 us
  Pallas kernels  177 us (99%)
    pallas_call x1, Pallas kernels, layer(): pl.pallas_call(layer_kernel, out_shape=[jax.ShapeDtypeStruct(shape, kind)...  163 us
    pallas_call x1, Pallas kernels, cast_sums(): pl.pallas_call(cast_kernel, grid=(CAST_STEPS,), out_shape=[jax.ShapeDtype...  14.5 us

profile of v7, /device:TPU:1, one launch (start us, length us, event | category | flops | bytes accessed | tf_op | source)
XLA Modules:
  0.0 177.9 jit_solution(14827010598604897652)
XLA Ops:
  0.7 162.5 %shard_map.272 = (bf16[2,64,768]{2,1,0:T(8,128)(2,1)}, f32[2,64,768]{2,1,0:T(8,128)}, bf16[3,768,2048]{2,1,0:T(8,128)(2,1)}, bf16[1,768,1024]{2,1,0:T(8,128)(2,1...) custom-call(bf16[2,64,768]{2,1,0:T(8,128)(2,1)} %args_0_.4, bf16[2,64,768]{2,1,0:T(8,128)(2,1)} %args_1_.4, ...), custom_call_target="tpu_custom_call" | custom-call | tf_op jit(solution)/shard_map/pallas_call | solution.py:944
  163.2 14.5 %shard_map.273 = (f32[768,2048]{1,0:T(8,128)}, f32[768,2048]{1,0:T(8,128)}, f32[2048,768]{1,0:T(8,128)}, f32[768,768]{1,0:T(8,128)}, f32[768,768]{1,0:T(8,128)},...) custom-call(bf16[3,768,2048]{2,1,0:T(8,128)(2,1)} %get-tuple-element, ...), custom_call_target="tpu_custom_call" | custom-call | tf_op jit(solution)/shard_map/pallas_call | solution.py:1010

commit v8 on v7

--- a/solution.py
+++ b/solution.py
@@ -360,6 +360,9 @@
     def pick(value):
         return jnp.where(low64(64), value[0:64], value[64:128])
 
+    barrier = pltpu.get_barrier_semaphore()
+    for peer in peers:
+        pl.semaphore_signal(barrier, inc=1, device_id=peer, device_id_type=MESH)
     loads = {}
     for at, name in enumerate(WEIGHTS):
         source = getattr(r, name)
@@ -378,9 +381,6 @@
     loads["w_krope"].start()
     for table in tables:
         table.start()
-    barrier = pltpu.get_barrier_semaphore()
-    for peer in peers:
-        pl.semaphore_signal(barrier, inc=1, device_id=peer, device_id_type=MESH)
     pl.semaphore_wait(barrier, len(peers))
 
     def swap(at, src, dst):
@@ -392,7 +392,6 @@
     swap_x = swap(0, r.tokens.at[1 - x_hi], r.xbuf.at[pl.ds(64, 64)])
     swap_c = swap(1, r.cotangent.at[1 - x_hi], r.cbuf.at[pl.ds(64, 64)])
     swap_x.start()
-    swap_c.start()
     for name in ("w_query", "w_qrope", "w_upkey"):
         loads[name].start()
     r.xbuf[0:64] = r.tokens[x_hi]
@@ -448,6 +447,7 @@
     r.kr[y, z] = pick(key_rot)
     for copy in gather(0)[1::2]:
         copy.start()
+    swap_c.start()
     send_norm = paired(0, r.norm2.at[pl.ds(0, 128)], r.norm2.at[pl.ds(128, 128)])
     send_norm.start()
     normed = r.norm2[0:128]
@@ -462,8 +462,6 @@
         lanes = slice(p * 128, p * 128 + 128)
         piece = query_pre[:, lanes]
         r.qr[:, lanes] = (piece * r.cosine[...] + swap_halves(piece) * r.sine[...]).astype(BF)
-    loads["w_upkey"].wait()
-
     def to_latent(source, weights, target):
         for half in range(2):
             for g in range(2):
@@ -473,24 +471,6 @@
                     rows = dot_nt(block, weights[g, :, j * 128 : j * 128 + 128])
                     target[half * 2 + g, j * 128 : j * 128 + 128] = rows.astype(BF)
 
-    to_latent(r.q, r.v_upkey, r.qs)
-    for half in range(2):
-        for p in range(6):
-            pair = r.qr[half * 64 : half * 64 + 64, p * 128 : p * 128 + 128].astype(F32)
-            turned = pltpu.roll(pair, 64, 1)
-            for odd in range(2):
-                front, back = (turned, pair) if odd else (pair, turned)
-                at = (p % 3) * 128 + odd * 64
-                r.qrx[half * 2 + p // 3, at : at + 64] = jnp.where(low64(64), front, back).astype(BF)
-
-    swap_c.wait()
-    group = jnp.where(x_hi == 0, r.group_of_seq[0], r.group_of_seq[1])
-    weight = r.group_weight[0]
-    for g in range(1, GROUPS):
-        weight = jnp.where(group == g, r.group_weight[g], weight)
-    r.gb2[0:128] = (r.cbuf[...].astype(F32) * weight).astype(BF)
-    send_gb = paired(3, r.gb2.at[pl.ds(0, 128)], r.gb2.at[pl.ds(128, 128)])
-    send_gb.start()
     def spread(part, stage):
         axis = (1, 2)[part]
         me = place[axis]
@@ -519,13 +499,33 @@
             copy.wait()
         for copy in spread(part, 0):
             copy.start()
+    loads["w_upkey"].wait()
+    to_latent(r.q, r.v_upkey, r.qs)
+    for half in range(2):
+        for p in range(6):
+            pair = r.qr[half * 64 : half * 64 + 64, p * 128 : p * 128 + 128].astype(F32)
+            turned = pltpu.roll(pair, 64, 1)
+            for odd in range(2):
+                front, back = (turned, pair) if odd else (pair, turned)
+                at = (p % 3) * 128 + odd * 64
+                r.qrx[half * 2 + p // 3, at : at + 64] = jnp.where(low64(64), front, back).astype(BF)
+
+    swap_c.wait()
+    group = jnp.where(x_hi == 0, r.group_of_seq[0], r.group_of_seq[1])
+    weight = r.group_weight[0]
+    for g in range(1, GROUPS):
+        weight = jnp.where(group == g, r.group_weight[g], weight)
+    r.gb2[0:128] = (r.cbuf[...].astype(F32) * weight).astype(BF)
+    send_gb = paired(3, r.gb2.at[pl.ds(0, 128)], r.gb2.at[pl.ds(128, 128)])
+    send_gb.start()
+
+    for ref in (r.acc, r.dqa, r.dqr, r.dlat, r.dkr):
+        ref[...] = jnp.zeros_like(ref)
     loads["w_down"].wait()
     send_gb.wait()
     for part in range(4):
         cols = slice(part * 256, part * 256 + 256)
         r.gh[:, cols] = dot_nt(r.gb2[...], r.v_down[cols, :])
-    for ref in (r.acc, r.dqa, r.dqr, r.dlat, r.dkr):
-        ref[...] = jnp.zeros_like(ref)
 
     for part in (1, 0):
         for copy in spread(part, 0):
@@ -639,8 +639,8 @@
     r.nmt[:, 0:128] = r.nm2[0:128].T
     send_nm.wait()
 
-    def tile(step, carried):
-        at = rows_at(step * 512, 512, 512)
+    for part in range(2):
+        at = slice(part * 512, part * 512 + 512)
         act = r.nm2[...]
         gate = dot(act, r.v_gate[:, at])
         up = dot(act, r.v_up[:, at])
@@ -653,9 +653,7 @@
         r.acts[0, :, at] = hidden
         r.acts[1, :, at] = grad_gate
         r.acts[2, :, at] = grad_up
-        return carried
-
-    lax.fori_loop(0, 2, tile, 0)
+
     wide = Reduction(r, "wide", place, r.g_wide, True)
     outer = Reduction(r, "out", place, r.g_out, False)
     early = Reduction(r, "early", place, r.g_early, False, True)

time: 178 us -> 177 us (level)
  no operation moved by 1% of the time
where the time goes in v8:
time: 177 us; the launch traced here: 176 us
  Pallas kernels  176 us (99%)
    pallas_call x1, Pallas kernels, layer(): pl.pallas_call(layer_kernel, out_shape=[jax.ShapeDtypeStruct(shape, kind)...  161 us
    pallas_call x1, Pallas kernels, cast_sums(): pl.pallas_call(cast_kernel, grid=(CAST_STEPS,), out_shape=[jax.ShapeDtype...  14.5 us

profile of v8, /device:TPU:1, one launch (start us, length us, event | category | flops | bytes accessed | tf_op | source)
XLA Modules:
  0.0 176.4 jit_solution(6667322087112654129)
XLA Ops:
  0.7 161.1 %shard_map.272 = (bf16[2,64,768]{2,1,0:T(8,128)(2,1)}, f32[2,64,768]{2,1,0:T(8,128)}, bf16[3,768,2048]{2,1,0:T(8,128)(2,1)}, bf16[1,768,1024]{2,1,0:T(8,128)(2,1...) custom-call(bf16[2,64,768]{2,1,0:T(8,128)(2,1)} %args_0_.4, bf16[2,64,768]{2,1,0:T(8,128)(2,1)} %args_1_.4, ...), custom_call_target="tpu_custom_call" | custom-call | tf_op jit(solution)/shard_map/pallas_call | solution.py:942
  161.7 14.5 %shard_map.273 = (f32[768,2048]{1,0:T(8,128)}, f32[768,2048]{1,0:T(8,128)}, f32[2048,768]{1,0:T(8,128)}, f32[768,768]{1,0:T(8,128)}, f32[768,768]{1,0:T(8,128)},...) custom-call(bf16[3,768,2048]{2,1,0:T(8,128)(2,1)} %get-tuple-element, ...), custom_call_target="tpu_custom_call" | custom-call | tf_op jit(solution)/shard_map/pallas_call | solution.py:1008

commit v9 on v8

--- a/solution.py
+++ b/solution.py
@@ -158,7 +158,7 @@
 
     def step(self, *stages):
         for stage in stages:
-            for o in range(3):
+            for o in (1, 2, 0):
                 self.finish(stage, (o,))
                 self.start(stage + 1, (o,))
 
@@ -888,6 +888,21 @@
     turned = pltpu.roll(rot, 64, 1)
     rot = jnp.concatenate([jnp.where(low64(64), rot, turned), jnp.where(low64(64), turned, rot)], axis=0)
     grad_kpre = (rot * r.cosine[...] - swap_halves(rot) * r.sine[...]).astype(BF)
+    for o in range(3):
+        r.late_total[o, 3, 0] = jnp.zeros((256, 128), BF)
+    grad_krope = dot_tn(grad_kpre, r.norm2[0:128]).astype(BF)
+    send_gl.wait()
+    for o in range(3):
+        rows = slice(o * 256, o * 256 + 256)
+        block = dot(r.normt[rows], r.gl2[core]).astype(BF)
+        for i in range(2):
+            r.late_total[o, i, 0] = block[:, i * 128 : i * 128 + 128]
+        for part in range(2):
+            at = o * 256 + part * 128
+            r.late_total[o, 2, 0, part * 64 : part * 64 + 64] = grad_krope[0:64, at : at + 128]
+        r.late_total[o, 2, 0, 128:256] = jnp.zeros((128, 128), BF)
+        if o > 0:
+            late.start(0, (o,))
     grad_normed = r.gnm[0:128] + dot(grad_kpre[:, 0:64], r.v_krope[...])
     for g in range(2):
         grad_normed = grad_normed + dot_nt(grad_latents[g], r.v_latent[:, g * 256 : g * 256 + 256])
@@ -899,21 +914,8 @@
     gains = r.gains[...]
     for p in range(6):
         gains = gains + jnp.where(gain_row == p, gain_attn[:, p * 128 : p * 128 + 128], 0.0)
-    for o in range(3):
-        r.late_total[o, 3, 0] = jnp.zeros((256, 128), BF)
     r.late_total[0, 3, 0, 0:16] = gains.astype(BF)
-    grad_krope = dot_tn(grad_kpre, r.norm2[0:128]).astype(BF)
-    send_gl.wait()
-    for o in range(3):
-        rows = slice(o * 256, o * 256 + 256)
-        block = dot(r.normt[rows], r.gl2[core]).astype(BF)
-        for i in range(2):
-            r.late_total[o, i, 0] = block[:, i * 128 : i * 128 + 128]
-        for part in range(2):
-            at = o * 256 + part * 128
-            r.late_total[o, 2, 0, part * 64 : part * 64 + 64] = grad_krope[0:64, at : at + 128]
-        r.late_total[o, 2, 0, 128:256] = jnp.zeros((128, 128), BF)
-        late.start(0, (o,))
+    late.start(0, (0,))
     wide.step(5)
     early.step(2)
     late.step(0, 1)

time: 177 us -> 180 us (1.017)
  Pallas kernels: 176 us -> 179 us
    pallas_call x1, Pallas kernels: 161 us -> 164 us  [layer(): pl.pallas_call(layer_kernel, out_shape=[jax.ShapeDtypeStruct(shape, kind)...]
where the time goes in v9:
time: 180 us; the launch traced here: 179 us
  Pallas kernels  179 us (99%)
    pallas_call x1, Pallas kernels, layer(): pl.pallas_call(layer_kernel, out_shape=[jax.ShapeDtypeStruct(shape, kind)...  164 us
    pallas_call x1, Pallas kernels, cast_sums(): pl.pallas_call(cast_kernel, grid=(CAST_STEPS,), out_shape=[jax.ShapeDtype...  14.5 us

profile of v9, /device:TPU:1, one launch (start us, length us, event | category | flops | bytes accessed | tf_op | source)
XLA Modules:
  0.0 179.5 jit_solution(4170607713166396423)
XLA Ops:
  0.7 164.1 %shard_map.272 = (bf16[2,64,768]{2,1,0:T(8,128)(2,1)}, f32[2,64,768]{2,1,0:T(8,128)}, bf16[3,768,2048]{2,1,0:T(8,128)(2,1)}, bf16[1,768,1024]{2,1,0:T(8,128)(2,1...) custom-call(bf16[2,64,768]{2,1,0:T(8,128)(2,1)} %args_0_.4, bf16[2,64,768]{2,1,0:T(8,128)(2,1)} %args_1_.4, ...), custom_call_target="tpu_custom_call" | custom-call | tf_op jit(solution)/shard_map/pallas_call | solution.py:944
  164.8 14.5 %shard_map.273 = (f32[768,2048]{1,0:T(8,128)}, f32[768,2048]{1,0:T(8,128)}, f32[2048,768]{1,0:T(8,128)}, f32[768,768]{1,0:T(8,128)}, f32[768,768]{1,0:T(8,128)},...) custom-call(bf16[3,768,2048]{2,1,0:T(8,128)(2,1)} %get-tuple-element, ...), custom_call_target="tpu_custom_call" | custom-call | tf_op jit(solution)/shard_map/pallas_call | solution.py:1010
